TPU v7x, 32 devices: a whole 2x2x4 slice. The times are simulated.
32 devices in a mesh: dp: 4 (over y, core), fsdp: 8 (over z, x).
Axes of the slice: x: 2, y: 2, z: 4, core: 2. Of those that a mesh axis runs over, the one named last changes fastest.
Arguments:
- block_input: bfloat16 [32, 1024, 1280], P(('dp', 'fsdp')), may hold values from -6 to 6
- cotangent: bfloat16 [32, 1024, 1280], P(('dp', 'fsdp')), may hold values from -6 to 6
- protein_lengths: int32 [32, 4], P(('dp', 'fsdp')), may hold values from 1 to 512, 1024 in all within a row
- weight_in: float32 [1280, 640], P('fsdp', 'dp'), may hold values from -0.15625 to 0.15625
- moment_in: float32 [1280, 640], P('fsdp', 'dp'), may hold values from -1 to 1
- square_in: float32 [1280, 640], P('fsdp', 'dp'), may hold values from 0 to 1, as said below
- weight_conv: float32 [5, 640, 640], P(None, 'fsdp', 'dp'), may hold values from -0.109375 to 0.109375
- moment_conv: float32 [5, 640, 640], P(None, 'fsdp', 'dp'), may hold values from -1 to 1
- square_conv: float32 [5, 640, 640], P(None, 'fsdp', 'dp'), may hold values from 0 to 1, as said below
- weight_out: float32 [640, 1280], P('fsdp', 'dp'), may hold values from -0.25 to 0.25
- moment_out: float32 [640, 1280], P('fsdp', 'dp'), may hold values from -1 to 1
- square_out: float32 [640, 1280], P('fsdp', 'dp'), may hold values from 0 to 1, as said below
- vectors: float32 [7680], replicated, may hold values from -2 to 4, as said below
- moment_vectors: float32 [7680], replicated, may hold values from -1 to 1
- square_vectors: float32 [7680], replicated, may hold values from 0 to 1, as said below
Outputs:
- block_output: bfloat16 [32, 1024, 1280], P(('dp', 'fsdp'))
- input_grad: bfloat16 [32, 1024, 1280], P(('dp', 'fsdp'))
- grad_norm: float32 [], replicated
- new_weight_in: float32 [1280, 640], P('fsdp', 'dp')
- new_moment_in: float32 [1280, 640], P('fsdp', 'dp')
- new_square_in: float32 [1280, 640], P('fsdp', 'dp')
- new_weight_conv: float32 [5, 640, 640], P(None, 'fsdp', 'dp')
- new_moment_conv: float32 [5, 640, 640], P(None, 'fsdp', 'dp')
- new_square_conv: float32 [5, 640, 640], P(None, 'fsdp', 'dp')
- new_weight_out: float32 [640, 1280], P('fsdp', 'dp')
- new_moment_out: float32 [640, 1280], P('fsdp', 'dp')
- new_square_out: float32 [640, 1280], P('fsdp', 'dp')
- new_vectors: float32 [7680], replicated
- new_moment_vectors: float32 [7680], replicated
- new_square_vectors: float32 [7680], replicated
Inputs may be any that keep to these rules, and one draw needn't show every extreme that they name: `vectors`: gains positive, shifts and biases of both signs. `square_in`: positive. `square_conv`: positive. `square_out`: positive. `square_vectors`: positive.
All inputs are finite; a program needn't handle non-finite values.
Results may differ from a plain program's by a relative error of at most 0.02.
Values may be sent and summed in bfloat16 or wider, within the bound.
No kernel may reach another device: no remote copies, remote signals or barrier semaphores. Data moves between devices by JAX's collectives and lax.ppermute only.
A program may use at most 128 MiB of HBM per device.

v0:
```python
import jax
import jax.numpy as jnp
from jax import lax
from jax.sharding import PartitionSpec as P

D = 1280
INNER = 640
KERNEL = 5
DILATION = 64
LENGTH = 1024
STEP = 10


NORM_EPS = 1e-05
ADAM_EPS = 1e-08
BETA_ONE = 0.9
BETA_TWO = 0.95
CLIP_LIMIT = 1.0
RATE_MATRIX = 0.04
RATE_VECTOR = 0.3
DECAY_MATRIX = 0.1


def layer_norm(values, gain, shift):
    center = values - jnp.mean(values, axis=-1, keepdims=True)
    spread = jnp.mean(center * center, axis=-1, keepdims=True)
    return center * lax.rsqrt(spread + NORM_EPS) * gain + shift


def norm_gelu(values, gain, shift):
    return jax.nn.gelu(layer_norm(values, gain, shift))


def split_vectors(vectors):
    widths = [D, D, INNER, INNER, INNER, INNER, INNER, INNER, D]
    pieces = []
    offset = 0
    for width_count in widths:
        pieces.append(vectors[offset : offset + width_count])
        offset = offset + width_count
    return pieces


def tap_masks(protein_lengths):
    run_ends = jnp.cumsum(protein_lengths, axis=1)
    run_starts = run_ends - protein_lengths
    position = jnp.arange(LENGTH, dtype=jnp.int32)
    inside = (position[None, :, None] >= run_starts[:, None, :]) & (
        position[None, :, None] < run_ends[:, None, :]
    )
    lower_bound = jnp.sum(jnp.where(inside, run_starts[:, None, :], 0), axis=2)
    upper_bound = jnp.sum(jnp.where(inside, run_ends[:, None, :], 0), axis=2)
    layers = []
    for tap_index in range(KERNEL):
        target = position[None, :] + (tap_index - KERNEL // 2) * DILATION
        layers.append(((target >= lower_bound) & (target < upper_bound)).astype(jnp.bfloat16))
    return jnp.stack(layers, axis=1)


def shifted(values, offset):
    margin = KERNEL // 2 * DILATION
    padded = jnp.pad(values, ((0, 0), (margin, margin), (0, 0)))
    return lax.slice_in_dim(padded, margin + offset, margin + offset + values.shape[1], axis=1)


def dilated_forward(hidden, kernel_weights, tap_mask):
    total = jnp.zeros(hidden.shape[:2] + (kernel_weights.shape[2],), jnp.float32)
    for tap_index in range(KERNEL):
        offset = (tap_index - KERNEL // 2) * DILATION
        source = shifted(hidden, offset) * tap_mask[:, tap_index, :, None]
        total = total + jnp.einsum(
            "rli,io->rlo", source, kernel_weights[tap_index], preferred_element_type=jnp.float32
        )
    return total


def dilated_backward(hidden, grad_mixed, kernel_weights, tap_mask):
    grad_hidden = jnp.zeros(hidden.shape, jnp.float32)
    pieces = []
    for tap_index in range(KERNEL):
        offset = (tap_index - KERNEL // 2) * DILATION
        masked = grad_mixed * tap_mask[:, tap_index, :, None]
        pieces.append(
            jnp.einsum(
                "rli,rlo->io", shifted(hidden, offset), masked, preferred_element_type=jnp.float32
            )
        )
        returned = jnp.einsum(
            "rlo,io->rli", masked, kernel_weights[tap_index], preferred_element_type=jnp.float32
        )
        grad_hidden = grad_hidden + shifted(returned, -offset)
    return (jnp.stack(pieces), grad_hidden)


def adamw_update(weight, moment, square, gradient, step_rate, weight_decay):
    new_moment = BETA_ONE * moment + (1.0 - BETA_ONE) * gradient
    new_square = BETA_TWO * square + (1.0 - BETA_TWO) * gradient * gradient
    moment_hat = new_moment / (1.0 - BETA_ONE**STEP)
    square_hat = new_square / (1.0 - BETA_TWO**STEP)
    update = moment_hat / (jnp.sqrt(square_hat) + ADAM_EPS)
    return (weight - step_rate * (update + weight_decay * weight), new_moment, new_square)


def body(
    block_input,
    cotangent,
    protein_lengths,
    weight_in,
    moment_in,
    square_in,
    weight_conv,
    moment_conv,
    square_conv,
    weight_out,
    moment_out,
    square_out,
    vectors,
    moment_vectors,
    square_vectors,
):
    parts_dp = (
        lax.all_gather(weight_in.astype(jnp.bfloat16), "dp", axis=1, tiled=True),
        lax.all_gather(weight_conv.astype(jnp.bfloat16), "dp", axis=2, tiled=True),
        lax.all_gather(weight_out.astype(jnp.bfloat16), "dp", axis=1, tiled=True),
    )
    full_in, full_conv, full_out = (
        lax.all_gather(parts_dp[0], "fsdp", axis=0, tiled=True),
        lax.all_gather(parts_dp[1], "fsdp", axis=1, tiled=True),
        lax.all_gather(parts_dp[2], "fsdp", axis=0, tiled=True),
    )
    (
        gain_one,
        shift_one,
        gain_two,
        shift_two,
        gain_three,
        shift_three,
        bias_one,
        bias_two,
        bias_three,
    ) = split_vectors(vectors)
    tap_mask = tap_masks(protein_lengths)
    input_float = block_input.astype(jnp.float32)
    hidden_one, pullback_one = jax.vjp(norm_gelu, input_float, gain_one, shift_one)
    hidden_one = hidden_one.astype(jnp.bfloat16)
    mixed_one = (
        jnp.einsum("rld,di->rli", hidden_one, full_in, preferred_element_type=jnp.float32)
        + bias_one
    )
    hidden_two, pullback_two = jax.vjp(norm_gelu, mixed_one, gain_two, shift_two)
    hidden_two = hidden_two.astype(jnp.bfloat16)
    mixed_two = dilated_forward(hidden_two, full_conv, tap_mask) + bias_two
    hidden_three, pullback_three = jax.vjp(norm_gelu, mixed_two, gain_three, shift_three)
    hidden_three = hidden_three.astype(jnp.bfloat16)
    branch = (
        jnp.einsum("rli,id->rld", hidden_three, full_out, preferred_element_type=jnp.float32)
        + bias_three
    )
    block_output = (input_float + branch).astype(jnp.bfloat16)
    again_dp = (
        lax.all_gather(weight_in.astype(jnp.bfloat16), "dp", axis=1, tiled=True),
        lax.all_gather(weight_conv.astype(jnp.bfloat16), "dp", axis=2, tiled=True),
        lax.all_gather(weight_out.astype(jnp.bfloat16), "dp", axis=1, tiled=True),
    )
    back_in, back_conv, back_out = (
        lax.all_gather(again_dp[0], "fsdp", axis=0, tiled=True),
        lax.all_gather(again_dp[1], "fsdp", axis=1, tiled=True),
        lax.all_gather(again_dp[2], "fsdp", axis=0, tiled=True),
    )
    cotangent_float = cotangent.astype(jnp.float32)
    grad_out = jnp.einsum(
        "rli,rld->id", hidden_three, cotangent, preferred_element_type=jnp.float32
    )
    grad_bias_three = jnp.sum(cotangent_float, axis=(0, 1))
    pre_three = jnp.einsum("rld,id->rli", cotangent, back_out, preferred_element_type=jnp.float32)
    back_two, grad_gain_three, grad_shift_three = pullback_three(pre_three)
    back_two = back_two.astype(jnp.bfloat16)
    grad_bias_two = jnp.sum(back_two.astype(jnp.float32), axis=(0, 1))
    grad_conv, grad_hidden_two = dilated_backward(hidden_two, back_two, back_conv, tap_mask)
    back_one, grad_gain_two, grad_shift_two = pullback_two(grad_hidden_two)
    back_one = back_one.astype(jnp.bfloat16)
    grad_bias_one = jnp.sum(back_one.astype(jnp.float32), axis=(0, 1))
    grad_in = jnp.einsum("rld,rli->di", hidden_one, back_one, preferred_element_type=jnp.float32)
    pre_one = jnp.einsum("rli,di->rld", back_one, back_in, preferred_element_type=jnp.float32)
    norm_grad, grad_gain_one, grad_shift_one = pullback_one(pre_one)
    input_grad = (cotangent_float + norm_grad).astype(jnp.bfloat16)
    grad_vectors = jnp.concatenate(
        [
            grad_gain_one,
            grad_shift_one,
            grad_gain_two,
            grad_shift_two,
            grad_gain_three,
            grad_shift_three,
            grad_bias_one,
            grad_bias_two,
            grad_bias_three,
        ]
    )
    vector_total = lax.psum(grad_vectors, ("dp", "fsdp"))
    parts_fsdp = (
        lax.psum_scatter(
            grad_in.astype(jnp.bfloat16), "fsdp", scatter_dimension=0, tiled=True
        ).astype(jnp.float32),
        lax.psum_scatter(
            grad_conv.astype(jnp.bfloat16), "fsdp", scatter_dimension=1, tiled=True
        ).astype(jnp.float32),
        lax.psum_scatter(
            grad_out.astype(jnp.bfloat16), "fsdp", scatter_dimension=0, tiled=True
        ).astype(jnp.float32),
    )
    owned_in, owned_conv, owned_out = (
        lax.psum_scatter(
            parts_fsdp[0].astype(jnp.bfloat16), "dp", scatter_dimension=1, tiled=True
        ).astype(jnp.float32),
        lax.psum_scatter(
            parts_fsdp[1].astype(jnp.bfloat16), "dp", scatter_dimension=2, tiled=True
        ).astype(jnp.float32),
        lax.psum_scatter(
            parts_fsdp[2].astype(jnp.bfloat16), "dp", scatter_dimension=1, tiled=True
        ).astype(jnp.float32),
    )
    local_squares = (
        jnp.sum(owned_in * owned_in)
        + jnp.sum(owned_conv * owned_conv)
        + jnp.sum(owned_out * owned_out)
    )
    weight_total = lax.psum(local_squares, ("dp", "fsdp"))
    grad_norm = jnp.sqrt(weight_total + jnp.sum(vector_total * vector_total))
    clip_factor = jnp.minimum(1.0, CLIP_LIMIT / (grad_norm + 1e-06))
    new_in = adamw_update(
        weight_in, moment_in, square_in, clip_factor * owned_in, RATE_MATRIX, DECAY_MATRIX
    )
    new_conv = adamw_update(
        weight_conv, moment_conv, square_conv, clip_factor * owned_conv, RATE_MATRIX, DECAY_MATRIX
    )
    new_out = adamw_update(
        weight_out, moment_out, square_out, clip_factor * owned_out, RATE_MATRIX, DECAY_MATRIX
    )
    new_vec = adamw_update(
        vectors, moment_vectors, square_vectors, clip_factor * vector_total, RATE_VECTOR, 0.0
    )
    return (
        block_output,
        input_grad,
        grad_norm,
        new_in[0],
        new_in[1],
        new_in[2],
        new_conv[0],
        new_conv[1],
        new_conv[2],
        new_out[0],
        new_out[1],
        new_out[2],
        new_vec[0],
        new_vec[1],
        new_vec[2],
    )


def solution(mesh):
    placed = (
        P(("dp", "fsdp"), None, None),
        P(("dp", "fsdp"), None, None),
        P(("dp", "fsdp"), None),
        P("fsdp", "dp"),
        P("fsdp", "dp"),
        P("fsdp", "dp"),
        P(None, "fsdp", "dp"),
        P(None, "fsdp", "dp"),
        P(None, "fsdp", "dp"),
        P("fsdp", "dp"),
        P("fsdp", "dp"),
        P("fsdp", "dp"),
        P(),
        P(),
        P(),
    )
    return jax.shard_map(
        body,
        mesh=mesh,
        in_specs=placed,
        out_specs=(
            P(("dp", "fsdp"), None, None),
            P(("dp", "fsdp"), None, None),
            P(),
            P("fsdp", "dp"),
            P("fsdp", "dp"),
            P("fsdp", "dp"),
            P(None, "fsdp", "dp"),
            P(None, "fsdp", "dp"),
            P(None, "fsdp", "dp"),
            P("fsdp", "dp"),
            P("fsdp", "dp"),
            P("fsdp", "dp"),
            P(),
            P(),
            P(),
        ),
        check_vma=False,
    )
```

profile of v0, /device:TPU:0, one launch (start us, length us, event | category | flops | bytes accessed | tf_op | source)
XLA Modules:
  0.0 546.9 jit_solution(2928466396743538902)
XLA Ops:
  7.2 1.0 copy.90
  8.2 7.6 %all_gather.24 = bf16[160,640]{0,1:T(8,128)(2,1)S(1)} all-gather(bf16[160,160]{0,1:T(8,128)(2,1)S(1)} %copy.90), channel_id=1, replica_groups=mesh['dp'=4,'fsdp'=8] {'dp'}, dimensions={1}, use_global_device_ids=true | all-gather | bytes 256000 | tf_op jit(solution)/shard_map/all_gather | solution.py:122
  16.7 1.0 convert_element_type.141
  18.0 12.1 %all_gather.26 = bf16[5,80,640]{1,0,2:T(8,128)(2,1)} all-gather(bf16[5,80,160]{1,0,2:T(8,128)(2,1)S(1)} %copy.92), channel_id=1, replica_groups=mesh['dp'=4,'fsdp'=8] {'dp'}, dimensions={2}, use_global_device_ids=true | all-gather | bytes 640000 | tf_op jit(solution)/shard_map/all_gather | solution.py:123
  30.2 2.5 copy.93
  32.8 5.8 %all-gather = bf16[4,320,80]{1,2,0:T(8,128)(2,1)S(1)} all-gather(bf16[1,320,80]{1,2,0:T(8,128)(2,1)S(1)} %convert_bitcast_fusion), channel_id=1, replica_groups=mesh['dp'=4,'fsdp'=8] {'dp'}, dimensions={0}, use_global_device_ids=true | all-gather | bytes 256000 | tf_op jit(solution)/shard_map/all_gather | solution.py:124
  38.6 0.9 reshape.712
  40.9 0.8 fusion.20
  41.8 3.9 fusion.41
  45.7 17.0 %all-gather.5.cloned.1.call-done = bf16[1280,640]{1,0:T(8,128)(2,1)} async-done(((bf16[160,640]{1,0:T(8,128)(2,1)}), bf16[1280,640]{1,0:T(8,128)(2,1)}) %all-gather.5.cloned.1.call-update) | async-done | bytes 1638416 | tf_op jit(solution)/shard_map/all_gather | solution.py:127
  62.7 4.1 add_reduce_fusion
  67.3 2.5 fusion.187
  69.8 2.9 multiply_convert_fusion.1
  72.7 63.8 %all-gather.7.cloned.1.call-done = bf16[5,640,640]{2,1,0:T(8,128)(2,1)} async-done(((bf16[5,80,640]{2,1,0:T(8,128)(2,1)}), bf16[5,640,640]{2,1,0:T(8,128)(2,1)}) %all-gather.7.cloned.1.call-update) | async-done | bytes 4096016 | tf_op jit(solution)/shard_map/all_gather | solution.py:128
  136.6 3.0 fusion.60
  139.8 1.3 fusion.58
  141.1 1.2 fusion.62
  142.4 1.2 fusion.66
  143.7 1.5 fusion.179
  145.6 1.1 copy-done.2
  146.7 1.2 copy-done.8
  147.9 3.9 convolution_convert_fusion
  152.1 30.2 %all-gather.9.cloned.1.call-done = bf16[640,1280]{1,0:T(8,128)(2,1)} async-done(((bf16[80,1280]{1,0:T(8,128)(2,1)}), bf16[640,1280]{1,0:T(8,128)(2,1)}) %all-gather.9.cloned.1.call-update) | async-done | bytes 1638416 | tf_op jit(solution)/shard_map/all_gather | solution.py:129
  182.3 7.0 %fusion.168 = (f32[640]{0:T(1024)S(1)}, f32[1024]{0:T(1024)S(1)}, f32[1024,640]{0,1:T(8,128)S(1)}) fusion(f32[640]{0:T(1024)S(1)} %get-tuple-element.49, f32[1024,640]{0,1:T(8,128)} %copy-done.2, f32[1024]{0:T(1024)S(1)} %broadcast_multiply_fusion, f32[640]{0:T(1024)S(1)} %get-tuple-element.50, f32[1024]{0:T(1024)S(1)} %fusion.155, ...), kind=kOutput, calls=%fused_computation.258 | convolution fusion | flops 1695414656 | bytes 9522688 | tf_op jit(solution)/shard_map/rld,id->rli/dot_general | solution.py:175
  189.3 1.0 multiply_reduce_fusion
  190.4 0.9 convert_reduce_fusion.2
  191.3 1.7 copy-done.19
  193.1 1.2 convolution_bitcast_fusion
  194.2 1.2 convolution_bitcast_fusion.1
  195.4 1.2 convolution_bitcast_fusion.2
  196.6 1.2 convolution_bitcast_fusion.3
  197.8 4.1 fusion.169
  201.9 1.2 fusion.42
  203.2 1.2 convert_reduce_fusion.3
  204.3 1.1 copy-done.14
  205.4 3.4 convolution_convert_fusion.1
  208.9 2.2 fusion.73
  211.1 2.2 fusion.79
  213.3 2.1 fusion.83
  215.4 2.2 fusion.87
  217.6 2.2 fusion.93
  220.1 1.4 copy-done.1
  221.5 9.1 %fusion.167 = (f32[1280]{0:T(1024)S(1)}, f32[1024]{0:T(1024)S(1)}, f32[1,1024,1280]{2,1,0:T(8,128)S(1)}) fusion(f32[1280]{0:T(1024)S(1)} %get-tuple-element.55, f32[1024]{0:T(1024)S(1)} %broadcast_multiply_fusion.2, bf16[1,1024,1280]{2,1,0:T(8,128)(2,1)S(1)} %copy-done.1, f32[1280]{0:T(1024)S(1)} %get-tuple-element.56, f32[1024]{0:T(1024)S(1)} %fusion.153, ...), kind=kOutput, calls=%fused_computation.257 | convolution fusion | flops 1714419456 | bytes 10841088 | tf_op jit(solution)/shard_map/rli,di->rld/dot_general | solution.py:184
  230.6 2.7 fusion.15
  233.4 16.9 %reduce-scatter.17.cloned.1.call-done = bf16[80,1280]{1,0:T(8,128)(2,1)} async-done(((bf16[640,1280]{1,0:T(8,128)(2,1)}), bf16[80,1280]{1,0:T(8,128)(2,1)}) %reduce-scatter.17.cloned.1.call-update) | async-done | bytes 204816 | tf_op jit(solution)/shard_map/reduce_scatter | solution.py:208
  250.3 1.8 copy.112
  252.3 66.7 %reduce-scatter.13.cloned.1.call-done = bf16[160,640]{1,0:T(8,128)(2,1)} async-done(((bf16[1280,640]{1,0:T(8,128)(2,1)}), bf16[160,640]{1,0:T(8,128)(2,1)}) %reduce-scatter.13.cloned.1.call-update) | async-done | bytes 204816 | tf_op jit(solution)/shard_map/reduce_scatter | solution.py:202
  319.0 1.8 copy.108
  320.9 85.7 %reduce-scatter.15.cloned.1.call-done = bf16[5,80,640]{2,1,0:T(8,128)(2,1)} async-done(((bf16[5,640,640]{2,1,0:T(8,128)(2,1)}), bf16[5,80,640]{2,1,0:T(8,128)(2,1)}) %reduce-scatter.15.cloned.1.call-update) | async-done | bytes 512016 | tf_op jit(solution)/shard_map/reduce_scatter | solution.py:205
  406.5 2.7 copy.110
  409.2 2.6 reshape.715
  411.8 5.7 %convert_reduce_fusion.1 = (f32[1280]{0:T(1024)S(1)}, bf16[1,1024,1280]{2,1,0:T(8,128)(2,1)}) fusion(bf16[1,1024,1280]{2,1,0:T(8,128)(2,1)} %param.16, f32[1024]{0:T(1024)S(1)} %negate_multiply_fusion, f32[1024]{0:T(1024)S(1)} %multiply_multiply_fusion.10, f32[1024]{0:T(1024)S(1)} %broadcast_multiply_fusion.2, bf16[1,1024,1280]{2,1,0:T(8,128)(2,1)S(1)} %copy-done.1, ...), kind=kLoop, calls=%fused_computation.10 | loop fusion | flops 15727360 | bytes 13133824 | tf_op jit(solution)/shard_map/reduce_sum | solution.py:174
  417.6 11.9 %reduce-scatter.23.cloned.1.call-done = bf16[320,80]{1,0:T(8,128)(2,1)} async-done(((bf16[1280,80]{1,0:T(8,128)(2,1)}), bf16[320,80]{1,0:T(8,128)(2,1)}) %reduce-scatter.23.cloned.1.call-update) | async-done | bytes 51216
  429.4 1.0 copy.113
  430.4 22.7 %reduce-scatter.19.cloned.1.call-done = bf16[160,160]{1,0:T(8,128)(2,1)} async-done(((bf16[640,160]{1,0:T(8,128)(2,1)}), bf16[160,160]{1,0:T(8,128)(2,1)}) %reduce-scatter.19.cloned.1.call-update) | async-done | bytes 51216
  453.1 1.0 copy.109
  455.4 23.3 %reduce-scatter.21.cloned.1.call-done = bf16[160,400]{1,0:T(8,128)(2,1)} async-done(((bf16[640,400]{1,0:T(8,128)(2,1)}), bf16[160,400]{1,0:T(8,128)(2,1)}) %reduce-scatter.21.cloned.1.call-update) | async-done | bytes 128016
  478.7 1.2 reshape.716
  482.8 6.8 %fusion.22 = bf16[1,1024,1280]{2,1,0:T(8,128)(2,1)} fusion(bf16[1,1024,1280]{2,1,0:T(8,128)(2,1)S(1)} %copy-done.1, bf16[640,1280]{1,0:T(8,128)(2,1)} %all-gather.9.cloned.1.call-done, f32[1280]{0:T(1024)} %get-tuple-element.57, f32[1024,640]{0,1:T(8,128)} %copy-done.2, f32[640]{0:T(1024)} %copy-done.21, f32[640]{0:T(1024)S(1)} %get-tuple-element.49, ...), kind=kOutput, calls=%fused_computation.30 | convolution fusion | flops 1691484160 | bytes 9521152 | tf_op jit(solution)/shard_map/rli,id->rld/dot_general | solution.py:156
  489.6 39.8 %all-reduce.5 = (f32[]{:T(128)}, f32[7680]{0:T(1024)S(1)}) all-reduce(f32[]{:T(128)S(6)} %add.345, f32[7680]{0:T(1024)} %copy-done.20), channel_id=1, replica_groups=mesh['dp'=4,'fsdp'=8] {'dp','fsdp'}, use_global_device_ids=true, to_apply=%region_24.25 | all-reduce | flops 7681 | bytes 61448 | tf_op jit(solution)/shard_map/psum | solution.py:228
  531.4 1.4 multiply_subtract_fusion.3
  532.8 1.8 multiply_subtract_fusion.2
  534.6 1.9 multiply_subtract_fusion.1
  536.5 2.4 multiply_subtract_fusion
  (99 shorter events, 7.4 us)
Async XLA Ops:
  7.2 55.6 %all-gather.5.cloned.1.call-start = ((), (), s32[]{:S(2)}) async-start(), calls=%async_computation.6 | async-start | bytes 1843200 | tf_op jit(solution)/shard_map/all_gather | solution.py:127
  16.7 16.1 %copy-start.16 = (f32[80,320]{1,0:T(8,128)S(1)}, f32[80,320]{1,0:T(8,128)}, u32[]{:S(2)}) copy-start(f32[80,320]{1,0:T(8,128)} %param.24) | copy-start | bytes 307204
  16.7 119.9 %all-gather.7.cloned.1.call-start = ((), (), s32[]{:S(2)}) async-start(), calls=%async_computation.7 | async-start | bytes 4608000 | tf_op jit(solution)/shard_map/all_gather | solution.py:128
  18.0 21.6 %copy-start.17 = (f32[7680]{0:T(1024)S(1)}, f32[7680]{0:T(1024)}, u32[]{:S(2)}) copy-start(f32[7680]{0:T(1024)} %param.27) | copy-start | bytes 92164
  18.0 22.3 %copy-start.22 = (s32[1,4]{1,0:T(1,128)S(1)}, s32[1,4]{1,0:T(1,128)}, u32[]{:S(2)}) copy-start(s32[1,4]{1,0:T(1,128)} %param.17) | copy-start | bytes 52
  18.0 22.4 %copy-start = (bf16[1,1024,1280]{2,1,0:T(8,128)(2,1)S(1)}, bf16[1,1024,1280]{2,1,0:T(8,128)(2,1)}, u32[]{:S(2)}) copy-start(bf16[1,1024,1280]{2,1,0:T(8,128)(2,1)} %param.15) | copy-start | bytes 7864324
  32.7 149.6 %all-gather.9.cloned.1.call-start = ((), (), s32[]{:S(2)}) async-start(), calls=%async_computation.8 | async-start | bytes 1843200 | tf_op jit(solution)/shard_map/all_gather | solution.py:129
  39.6 210.8 %reduce-scatter.17.cloned.1.call-start = ((), (), s32[]{:S(2)}) async-start(), calls=%async_computation.11 | async-start | bytes 1843200 | tf_op jit(solution)/shard_map/reduce_scatter | solution.py:208
  39.6 142.6 %copy-start.21 = (f32[640]{0:T(1024)}, f32[640]{0:T(1024)S(1)}, u32[]{:S(2)}) copy-start(f32[640]{0:T(1024)S(1)} %get-tuple-element.50) | copy-start | bytes 7684
  136.6 3.1 copy-start.5
  136.6 3.2 copy-start.18
  141.1 1.3 copy-start.10
  145.2 1.5 copy-start.2
  145.2 2.7 copy-start.8
  151.9 167.1 %reduce-scatter.13.cloned.1.call-start = ((), (), s32[]{:S(2)}) async-start(), calls=%async_computation.9 | async-start | bytes 1843200 | tf_op jit(solution)/shard_map/reduce_scatter | solution.py:202
  182.3 7.1 %copy-start.3 = (f32[1024,640]{0,1:T(8,128)S(1)}, f32[1024,640]{0,1:T(8,128)}, u32[]{:S(2)}) copy-start(f32[1024,640]{0,1:T(8,128)} %copy-done.2) | copy-start | bytes 7864324
  190.4 2.7 copy-start.19
  191.3 6.5 %copy-start.12 = (bf16[1024,640]{0,1:T(8,128)(2,1)}, bf16[1024,640]{0,1:T(8,128)(2,1)S(1)}, u32[]{:S(2)}) copy-start(bf16[1024,640]{0,1:T(8,128)(2,1)S(1)} %get-tuple-element.44) | copy-start | bytes 3932164
  203.1 2.2 copy-start.7
  204.3 1.1 copy-start.14
  205.4 3.5 copy-start.6
  205.4 3.5 copy-start.13
  208.8 197.7 %reduce-scatter.15.cloned.1.call-start = ((), (), s32[]{:S(2)}) async-start(), calls=%async_computation.10 | async-start | bytes 4608000 | tf_op jit(solution)/shard_map/reduce_scatter | solution.py:205
  211.1 2.2 copy-start.11
  219.8 1.7 copy-start.1
  219.8 209.6 %reduce-scatter.23.cloned.1.call-start = ((), (), s32[]{:S(2)}) async-start(), calls=%async_computation.14 | async-start | bytes 409600
  230.6 2.8 copy-start.4
  252.2 200.9 %reduce-scatter.19.cloned.1.call-start = ((), (), s32[]{:S(2)}) async-start(), calls=%async_computation.12 | async-start | bytes 409600
  320.8 157.9 %reduce-scatter.21.cloned.1.call-start = ((), (), s32[]{:S(2)}) async-start(), calls=%async_computation.13 | async-start | bytes 819200
  417.6 62.3 %copy-start.20 = (f32[7680]{0:T(1024)}, f32[7680]{0:T(1024)S(1)}, u32[]{:S(2)}) copy-start(f32[7680]{0:T(1024)S(1)} %constant_dynamic-update-slice_fusion.1) | copy-start | bytes 92164
  482.7 51.9 %copy-start.15 = (f32[160,160]{1,0:T(8,128)S(1)}, f32[160,160]{1,0:T(8,128)}, u32[]{:S(2)}) copy-start(f32[160,160]{1,0:T(8,128)} %param.18) | copy-start | bytes 307204
  482.7 53.7 %copy-start.9 = (f32[5,80,160]{2,1,0:T(8,128)S(1)}, f32[5,80,160]{2,1,0:T(8,128)}, u32[]{:S(2)}) copy-start(f32[5,80,160]{2,1,0:T(8,128)} %param.21) | copy-start | bytes 768004
Sparse Core Ops, SparseCore 0:
  16.8 45.8 all-gather.4
  65.5 70.9 all-gather.6
  139.3 42.8 all-gather.8
  186.1 64.1 reduce-scatter.16
  254.6 64.3 reduce-scatter.12
  322.4 84.1 reduce-scatter.14
  409.6 19.7 reduce-scatter.22
  432.6 20.4 reduce-scatter.18
  456.2 22.4 reduce-scatter.20
where the time goes:
time: 554 us; the launch traced here: 547 us
  waiting for transfers between devices  338 us (61%)
  blocking collectives  65.3 us (12%)
  matrix products  62.5 us (11%)
  other arithmetic  35.6 us (6%)
  local copies, waits for them, and re-layouts  25.2 us (5%)
  between operations  19.3 us (3%)
    reduce_scatter x1, waiting for transfers between devices, body(): lax.psum_scatter(grad_conv.astype(jnp.bfloat16), 'fsdp', scatter_dimensio...  85.7 us
    reduce_scatter x1, waiting for transfers between devices, body(): lax.psum_scatter(grad_in.astype(jnp.bfloat16), 'fsdp', scatter_dimension=...  66.7 us
    all_gather x1, waiting for transfers between devices, body(): lax.all_gather(parts_dp[1], 'fsdp', axis=1, tiled=True)  63.8 us
    unnamed x12, waiting for transfers between devices  58 us
    psum x1, blocking collectives, body(): weight_total = lax.psum(local_squares, ('dp', 'fsdp'))  39.8 us
    all_gather x1, waiting for transfers between devices, body(): lax.all_gather(parts_dp[2], 'fsdp', axis=0, tiled=True)  30.2 us
    unnamed x64, local copies, waits for them, and re-layouts  21 us
    all_gather x1, waiting for transfers between devices, body(): lax.all_gather(parts_dp[0], 'fsdp', axis=0, tiled=True)  17 us
  transfers between devices with their start and end apart: 9, of which 9 were waited for; matrix products, arithmetic and copies ran while one was open for 18% of the time, Pallas kernels for 0%

commit v1 on v0

v1 whole, which is shorter than its diff:
```python
import functools

import jax
import jax.numpy as jnp
from jax import lax
from jax.experimental import pallas as pl
from jax.experimental.pallas import tpu as pltpu
from jax.sharding import PartitionSpec as P

D = 1280
INNER = 640
KERNEL = 5
DILATION = 64
LENGTH = 1024
STEP = 10
MARGIN = KERNEL // 2 * DILATION
OFFSETS = tuple((k - KERNEL // 2) * DILATION for k in range(KERNEL))
BLOCK = 256
STEPS = LENGTH // BLOCK

NORM_EPS = 1e-05
ADAM_EPS = 1e-08
BETA_ONE = 0.9
BETA_TWO = 0.95
CLIP_LIMIT = 1.0
RATE_MATRIX = 0.04
RATE_VECTOR = 0.3
DECAY_MATRIX = 0.1
GELU_C = 0.7978845608
GELU_K = 0.044715

GAIN_ONE, SHIFT_ONE = (0, 1280), (1280, 1280)
GAIN_TWO, SHIFT_TWO = (2560, 640), (3200, 640)
GAIN_THREE, SHIFT_THREE = (3840, 640), (4480, 640)
BIAS_ONE, BIAS_TWO, BIAS_THREE = (5120, 640), (5760, 640), (6400, 1280)

BF16 = jnp.bfloat16
F32 = jnp.float32
AXES = ("dp", "fsdp")
VMEM_LIMIT = 56 * 1024 * 1024


def round16(n):
    return -(-n // 16) * 16


class Geometry:
    def __init__(self, taps, rows, cols):
        self.taps, self.rows, self.cols = taps, rows, cols
        self.height = taps * rows
        self.tiles, self.rest = divmod(cols, 128)
        self.groups = 128 // self.rest if self.rest and 128 % self.rest == 0 else 1
        self.tile_rows = round16(self.height)
        self.rest_rows = round16(-(-self.height // self.groups)) if self.rest else 0
        self.packed = self.tiles * self.tile_rows + self.rest_rows

    def pack(self, value):
        pieces = [value[:, 128 * t : 128 * t + 128] for t in range(self.tiles)]
        more = self.tile_rows - self.height
        if more:
            empty = jnp.zeros((more, 128), value.dtype)
            pieces = [jnp.concatenate([piece, empty], axis=0) for piece in pieces]
        if self.rest:
            rest = value[:, 128 * self.tiles :]
            spare = self.groups * self.rest_rows - self.height
            if spare:
                rest = jnp.concatenate([rest, jnp.zeros((spare, self.rest), value.dtype)], axis=0)
            n = self.rest_rows
            parts = [rest[n * g : n * g + n] for g in range(self.groups)]
            empty = 128 - self.groups * self.rest
            if empty:
                parts.append(jnp.zeros((n, empty), value.dtype))
            pieces.append(jnp.concatenate(parts, axis=1))
        return jnp.concatenate(pieces, axis=0)

    def unpack(self, packed):
        pieces = [
            packed[self.tile_rows * t : self.tile_rows * t + self.height]
            for t in range(self.tiles)
        ]
        if self.rest:
            base = self.tiles * self.tile_rows
            n, w = self.rest_rows, self.rest
            parts = []
            for g in range(self.groups):
                have = min(n, self.height - n * g)
                if have > 0:
                    parts.append(packed[base : base + have, w * g : w * g + w])
            pieces.append(jnp.concatenate(parts, axis=0))
        return jnp.concatenate(pieces, axis=1)


class Network:
    def __init__(self, dp, fsdp):
        self.dp, self.fsdp = dp, fsdp
        self.half = dp * fsdp // 2
        far = [("f", b) for b in range(fsdp.bit_length() - 2, 0, -1)]
        near = [("f", 0)] if fsdp > 1 else []
        rows = [("d", b) for b in range(dp.bit_length() - 2, 0, -1)]
        self.order = (far + near + rows, far + rows + near)

    def flip(self, stage, device):
        d, f = divmod(device, self.fsdp)
        kind, bit = self.order[d & 1][stage]
        if kind == "f":
            f ^= 1 << bit
        else:
            d ^= 1 << bit
        return d * self.fsdp + f

    def stage(self, stage):
        return [(i, self.flip(stage, i)) for i in range(self.dp * self.fsdp)]

    def core(self):
        return [(i, i ^ self.fsdp) for i in range(self.dp * self.fsdp)]

    def stages(self):
        return len(self.order[0])

    def slot(self, d, f, me_d, me_f):
        d_bits = jnp.bitwise_xor(me_d, d)
        f_bits = jnp.bitwise_xor(me_f, f)
        total = jnp.int32(0)
        for i, (kind, bit) in enumerate(self.order[d & 1]):
            source = f_bits if kind == "f" else d_bits
            total = total + (jnp.bitwise_and(lax.shift_right_logical(source, bit), 1) << i)
        return total


def call(kernel, name, out_shape, in_specs, out_specs, grid=(), scratch=(), flops=0, bytes_accessed=0):
    return pl.pallas_call(
        kernel,
        name=name,
        grid=grid,
        out_shape=out_shape,
        in_specs=in_specs,
        out_specs=out_specs,
        scratch_shapes=list(scratch),
        compiler_params=pltpu.CompilerParams(vmem_limit_bytes=VMEM_LIMIT),
        cost_estimate=pl.CostEstimate(
            flops=flops, bytes_accessed=bytes_accessed, transcendentals=0
        ),
    )


def whole(shape):
    return pl.BlockSpec(shape, lambda *_: (0,) * len(shape))


def tokens(width):
    return pl.BlockSpec((BLOCK, width), lambda i: (i, 0))


SMEM = pl.BlockSpec(memory_space=pltpu.SMEM)
ANY = pl.BlockSpec(memory_space=pl.ANY)


def shape(dims, dtype):
    return jax.ShapeDtypeStruct(dims, dtype)


def part(vec_ref, span):
    return vec_ref[:, span[0] : span[0] + span[1]]


def add_rows(ref, value, first):
    row = jnp.sum(value, axis=0, keepdims=True)

    @pl.when(first)
    def _():
        ref[...] = row

    @pl.when(jnp.logical_not(first))
    def _():
        ref[...] += row


def statistics(values):
    width = values.shape[1]
    mean = jnp.sum(values, axis=1, keepdims=True) * (1.0 / width)
    center = values - mean
    spread = jnp.sum(center * center, axis=1, keepdims=True) * (1.0 / width)
    return center, lax.rsqrt(spread + NORM_EPS)


def gelu(a):
    t = jnp.tanh(GELU_C * (a + GELU_K * (a * a * a)))
    return 0.5 * a * (1.0 + t)


def gelu_slope(a):
    square = a * a
    t = jnp.tanh(GELU_C * a * (1.0 + GELU_K * square))
    half = 0.5 * (1.0 + t)
    return half + half * (1.0 - t) * a * (GELU_C + (3.0 * GELU_C * GELU_K) * square)


def norm_backward(grad, normed, root, gain, shift):
    width = grad.shape[1]
    d_a = grad * gelu_slope(normed * gain + shift)
    scaled = d_a * gain
    mean_one = jnp.sum(scaled, axis=1, keepdims=True) * (1.0 / width)
    mean_two = jnp.sum(scaled * normed, axis=1, keepdims=True) * (1.0 / width)
    return root * (scaled - mean_one - normed * mean_two), d_a * normed, d_a


def tap_mask(ends_ref, start, rows, offset, width):
    position = start + lax.broadcasted_iota(jnp.int32, (rows, 128), 0)
    count = ends_ref.shape[0]
    lower = jnp.zeros((rows, 128), jnp.int32)
    upper = jnp.full((rows, 128), ends_ref[count - 1], jnp.int32)
    for j in range(count - 1):
        lower = jnp.where(position >= ends_ref[j], ends_ref[j], lower)
    for j in range(count - 2, -1, -1):
        upper = jnp.where(position < ends_ref[j], ends_ref[j], upper)
    target = position + offset
    mask = jnp.where((target >= lower) & (target < upper), 1.0, 0.0).astype(BF16)
    return jnp.concatenate([mask] * (width // 128), axis=1)


def fill_padded(padded, source):
    padded[0:MARGIN] = jnp.zeros((MARGIN, source.shape[1]), source.dtype)
    padded[MARGIN : MARGIN + LENGTH] = source[...]
    padded[MARGIN + LENGTH : MARGIN + LENGTH + MARGIN] = jnp.zeros(
        (MARGIN, source.shape[1]), source.dtype
    )


def dot(a, b):
    return jnp.dot(a, b, preferred_element_type=F32)


def dot_nt(a, b):
    return lax.dot_general(a, b, (((1,), (1,)), ((), ())), preferred_element_type=F32)


def assemble(net, geo, me_ref, own, peer, buffer, sems, full):
    core = jnp.bitwise_and(me_ref[0], 1)
    first = pltpu.make_async_copy(own, buffer.at[core], sems.at[0])
    second = pltpu.make_async_copy(peer, buffer.at[1 - core], sems.at[1])
    first.start()
    second.start()
    first.wait()
    second.wait()
    for f in range(net.fsdp):
        blocks = [
            geo.unpack(buffer[d & 1, net.slot(d, f, me_ref[0], me_ref[1])])
            for d in range(net.dp)
        ]
        row = jnp.concatenate(blocks, axis=1)
        for k in range(geo.taps):
            start = k * geo.rows * net.fsdp + f * geo.rows
            full[start : start + geo.rows] = row[k * geo.rows : k * geo.rows + geo.rows]


def distribute(net, geo, me_ref, full, buffer, sems, keep, send):
    for f in range(net.fsdp):
        pieces = [
            full[
                k * geo.rows * net.fsdp + f * geo.rows : k * geo.rows * net.fsdp
                + f * geo.rows
                + geo.rows
            ]
            for k in range(geo.taps)
        ]
        row = pieces[0] if geo.taps == 1 else jnp.concatenate(pieces, axis=0)
        for d in range(net.dp):
            buffer[d & 1, net.slot(d, f, me_ref[0], me_ref[1])] = geo.pack(
                row[:, d * geo.cols : d * geo.cols + geo.cols]
            )
    core = jnp.bitwise_and(me_ref[0], 1)
    first = pltpu.make_async_copy(buffer.at[1 - core], send, sems.at[0])
    second = pltpu.make_async_copy(buffer.at[core], keep, sems.at[1])
    first.start()
    second.start()
    first.wait()
    second.wait()


def slots(net, geo):
    return (net.half, geo.packed, 128)


def piece_scratch(net, geo):
    return [pltpu.VMEM((2,) + slots(net, geo), BF16), pltpu.SemaphoreType.DMA((2,))]


def pack_weights(geos, weights):
    def kernel(*refs):
        n = len(geos)
        for geo, source, target in zip(geos, refs[:n], refs[n:]):
            target[...] = geo.pack(source[...].astype(BF16))

    return call(
        kernel,
        "pack_weights",
        [shape((geo.packed, 128), BF16) for geo in geos],
        [whole(w.shape) for w in weights],
        [whole((geo.packed, 128)) for geo in geos],
        bytes_accessed=1_000_000,
    )(*weights)


def first_norm(block_input, cotangent, vec):
    def kernel(x_ref, cot_ref, vec_ref, h_ref, ht_ref, stat_ref, bias_ref):
        values = x_ref[...].astype(F32)
        center, root = statistics(values)
        normed = center * root
        hidden = gelu(normed * part(vec_ref, GAIN_ONE) + part(vec_ref, SHIFT_ONE)).astype(BF16)
        h_ref[...] = hidden
        ht_ref[...] = hidden.T
        lane = lax.broadcasted_iota(jnp.int32, (BLOCK, 128), 1)
        stat_ref[...] = jnp.where(lane == 0, values[:, :1] - center[:, :1], root)
        add_rows(bias_ref, cot_ref[...].astype(F32), pl.program_id(0) == 0)

    return call(
        kernel,
        "first_norm",
        [
            shape((LENGTH, D), BF16),
            shape((D, LENGTH), BF16),
            shape((LENGTH, 128), F32),
            shape((1, D), F32),
        ],
        [tokens(D), tokens(D), whole(vec.shape)],
        [tokens(D), pl.BlockSpec((D, BLOCK), lambda i: (0, i)), tokens(128), whole((1, D))],
        grid=(STEPS,),
        flops=30 * LENGTH * D,
        bytes_accessed=8 * LENGTH * D,
    )(block_input, cotangent, vec)


def norm_out(mixed, vec_ref, gain, shift_span, h_ref, ht_ref, normed_ref, root_ref):
    center, root = statistics(mixed)
    normed = center * root
    hidden = gelu(normed * part(vec_ref, gain) + part(vec_ref, shift_span)).astype(BF16)
    h_ref[...] = hidden
    ht_ref[...] = hidden.T
    normed_ref[...] = normed
    root_ref[...] = jnp.broadcast_to(root, (BLOCK, 128))


NORM_SHAPES = [
    shape((LENGTH, INNER), BF16),
    shape((INNER, LENGTH), BF16),
    shape((LENGTH, INNER), F32),
    shape((LENGTH, 128), F32),
]


def norm_specs():
    return [
        tokens(INNER),
        pl.BlockSpec((INNER, BLOCK), lambda i: (0, i)),
        tokens(INNER),
        tokens(128),
    ]


def mix_one(net, geo, me, own, peer, hidden_one, vec):
    def kernel(me_ref, own_ref, peer_ref, h1_ref, vec_ref, h_ref, ht_ref, n_ref, r_ref, full, buf, sems):
        @pl.when(pl.program_id(0) == 0)
        def _():
            assemble(net, geo, me_ref, own_ref, peer_ref, buf, sems, full)

        mixed = dot(h1_ref[...], full[...]) + part(vec_ref, BIAS_ONE)
        norm_out(mixed, vec_ref, GAIN_TWO, SHIFT_TWO, h_ref, ht_ref, n_ref, r_ref)

    return call(
        kernel,
        "mix_one",
        NORM_SHAPES + [shape((D, INNER), BF16)],
        [SMEM, ANY, ANY, tokens(D), whole(vec.shape)],
        norm_specs() + [whole((D, INNER))],
        grid=(STEPS,),
        scratch=piece_scratch(net, geo),
        flops=2 * LENGTH * D * INNER,
        bytes_accessed=12_000_000,
    )(me, own, peer, hidden_one, vec)


def mix_two(net, geo, me, ends, own, peer, hidden_two, vec):
    def kernel(
        me_ref, ends_ref, own_ref, peer_ref, h2_ref, vec_ref, h_ref, ht_ref, n_ref, r_ref, full, buf, sems, pad
    ):
        step = pl.program_id(0)

        @pl.when(step == 0)
        def _():
            assemble(net, geo, me_ref, own_ref, peer_ref, buf, sems, full)
            fill_padded(pad, h2_ref)

        start = step * BLOCK
        mixed = jnp.zeros((BLOCK, INNER), F32)
        for k, offset in enumerate(OFFSETS):
            source = pad[pl.ds(pl.multiple_of(start + MARGIN + offset, DILATION), BLOCK)]
            source = source * tap_mask(ends_ref, start, BLOCK, offset, INNER)
            mixed = mixed + dot(source, full[k * INNER : k * INNER + INNER])
        mixed = mixed + part(vec_ref, BIAS_TWO)
        norm_out(mixed, vec_ref, GAIN_THREE, SHIFT_THREE, h_ref, ht_ref, n_ref, r_ref)

    return call(
        kernel,
        "mix_two",
        NORM_SHAPES + [shape((KERNEL * INNER, INNER), BF16)],
        [SMEM, SMEM, ANY, ANY, whole((LENGTH, INNER)), whole(vec.shape)],
        norm_specs() + [whole((KERNEL * INNER, INNER))],
        grid=(STEPS,),
        scratch=piece_scratch(net, geo) + [pltpu.VMEM((LENGTH + 2 * MARGIN, INNER), BF16)],
        flops=2 * LENGTH * KERNEL * INNER * INNER,
        bytes_accessed=18_000_000,
    )(me, ends, own, peer, hidden_two, vec)


def gradient_shapes(net, geo):
    return [shape(slots(net, geo), BF16)] * 2


def weight_gradient(net, geo, me, left, right, name):
    dims = (left.shape[0], right.shape[1])

    def kernel(me_ref, left_ref, right_ref, keep, send, full, buf, sems):
        full[...] = dot(left_ref[...], right_ref[...]).astype(BF16)
        distribute(net, geo, me_ref, full, buf, sems, keep, send)

    return call(
        kernel,
        name,
        gradient_shapes(net, geo),
        [SMEM, whole(left.shape), whole(right.shape)],
        [ANY, ANY],
        grid=(1,),
        scratch=[pltpu.VMEM(dims, BF16)] + piece_scratch(net, geo),
        flops=2 * LENGTH * dims[0] * dims[1],
        bytes_accessed=6_000_000,
    )(me, left, right)


def back_through_out(net, geo, me, own, peer, cotangent, normed, root, vec):
    def kernel(
        me_ref, own_ref, peer_ref, cot_ref, n_ref, r_ref, vec_ref, back_ref, gg_ref, gs_ref, gb_ref, full, buf, sems
    ):
        first = pl.program_id(0) == 0

        @pl.when(first)
        def _():
            assemble(net, geo, me_ref, own_ref, peer_ref, buf, sems, full)

        grad = dot_nt(cot_ref[...], full[...])
        back, to_gain, to_shift = norm_backward(
            grad, n_ref[...], r_ref[:, :1], part(vec_ref, GAIN_THREE), part(vec_ref, SHIFT_THREE)
        )
        back = back.astype(BF16)
        back_ref[...] = back
        add_rows(gg_ref, to_gain, first)
        add_rows(gs_ref, to_shift, first)
        add_rows(gb_ref, back.astype(F32), first)

    row = shape((1, INNER), F32)
    return call(
        kernel,
        "back_through_out",
        [shape((LENGTH, INNER), BF16), row, row, row, shape((INNER, D), BF16)],
        [SMEM, ANY, ANY, tokens(D), tokens(INNER), tokens(128), whole(vec.shape)],
        [tokens(INNER)] + [whole((1, INNER))] * 3 + [whole((INNER, D))],
        grid=(STEPS,),
        scratch=piece_scratch(net, geo),
        flops=2 * LENGTH * D * INNER,
        bytes_accessed=12_000_000,
    )(me, own, peer, cotangent, normed, root, vec)


def block_result(block_input, hidden_three, full_out, vec):
    def kernel(x_ref, h_ref, w_ref, vec_ref, out_ref):
        branch = dot(h_ref[...], w_ref[...]) + part(vec_ref, BIAS_THREE)
        out_ref[...] = (x_ref[...].astype(F32) + branch).astype(BF16)

    return call(
        kernel,
        "block_result",
        shape((LENGTH, D), BF16),
        [tokens(D), tokens(INNER), whole((INNER, D)), whole(vec.shape)],
        tokens(D),
        grid=(STEPS,),
        flops=2 * LENGTH * D * INNER,
        bytes_accessed=8_000_000,
    )(block_input, hidden_three, full_out, vec)


def conv_gradient(net, geo, me, ends, hidden_two_t, back_two):
    def kernel(me_ref, ends_ref, left_ref, back_ref, keep, send, full, pad, buf, sems):
        fill_padded(pad, back_ref)
        for k, offset in enumerate(OFFSETS):
            source = pad[MARGIN - offset : MARGIN - offset + LENGTH]
            source = source * tap_mask(ends_ref, 0, LENGTH, -offset, INNER)
            full[k * INNER : k * INNER + INNER] = dot(left_ref[...], source).astype(BF16)
        distribute(net, geo, me_ref, full, buf, sems, keep, send)

    return call(
        kernel,
        "conv_gradient",
        gradient_shapes(net, geo),
        [SMEM, SMEM, whole((INNER, LENGTH)), whole((LENGTH, INNER))],
        [ANY, ANY],
        grid=(1,),
        scratch=[
            pltpu.VMEM((KERNEL * INNER, INNER), BF16),
            pltpu.VMEM((LENGTH + 2 * MARGIN, INNER), BF16),
        ]
        + piece_scratch(net, geo),
        flops=2 * LENGTH * KERNEL * INNER * INNER,
        bytes_accessed=7_000_000,
    )(me, ends, hidden_two_t, back_two)


def back_through_conv(ends, back_two, full_conv, normed, root, vec):
    def kernel(ends_ref, back_ref, w_ref, n_ref, r_ref, vec_ref, out_ref, gg_ref, gs_ref, gb_ref, pad):
        step = pl.program_id(0)
        first = step == 0

        @pl.when(first)
        def _():
            fill_padded(pad, back_ref)

        start = step * BLOCK
        grad = jnp.zeros((BLOCK, INNER), F32)
        for k, offset in enumerate(OFFSETS):
            source = pad[pl.ds(pl.multiple_of(start + MARGIN - offset, DILATION), BLOCK)]
            source = source * tap_mask(ends_ref, start, BLOCK, -offset, INNER)
            grad = grad + dot_nt(source, w_ref[k * INNER : k * INNER + INNER])
        back, to_gain, to_shift = norm_backward(
            grad, n_ref[...], r_ref[:, :1], part(vec_ref, GAIN_TWO), part(vec_ref, SHIFT_TWO)
        )
        back = back.astype(BF16)
        out_ref[...] = back
        add_rows(gg_ref, to_gain, first)
        add_rows(gs_ref, to_shift, first)
        add_rows(gb_ref, back.astype(F32), first)

    row = shape((1, INNER), F32)
    return call(
        kernel,
        "back_through_conv",
        [shape((LENGTH, INNER), BF16), row, row, row],
        [
            SMEM,
            whole((LENGTH, INNER)),
            whole((KERNEL * INNER, INNER)),
            tokens(INNER),
            tokens(128),
            whole(vec.shape),
        ],
        [tokens(INNER)] + [whole((1, INNER))] * 3,
        grid=(STEPS,),
        scratch=[pltpu.VMEM((LENGTH + 2 * MARGIN, INNER), BF16)],
        flops=2 * LENGTH * KERNEL * INNER * INNER,
        bytes_accessed=10_000_000,
    )(ends, back_two, full_conv, normed, root, vec)


def back_through_in(back_one, full_in, block_input, cotangent, stat, vec):
    def kernel(back_ref, w_ref, x_ref, cot_ref, stat_ref, vec_ref, out_ref, gg_ref, gs_ref):
        first = pl.program_id(0) == 0
        grad = dot_nt(back_ref[...], w_ref[...])
        root = stat_ref[:, 1:2]
        normed = (x_ref[...].astype(F32) - stat_ref[:, :1]) * root
        back, to_gain, to_shift = norm_backward(
            grad, normed, root, part(vec_ref, GAIN_ONE), part(vec_ref, SHIFT_ONE)
        )
        out_ref[...] = (cot_ref[...].astype(F32) + back).astype(BF16)
        add_rows(gg_ref, to_gain, first)
        add_rows(gs_ref, to_shift, first)

    row = shape((1, D), F32)
    return call(
        kernel,
        "back_through_in",
        [shape((LENGTH, D), BF16), row, row],
        [tokens(INNER), whole((D, INNER)), tokens(D), tokens(D), tokens(128), whole(vec.shape)],
        [tokens(D)] + [whole((1, D))] * 2,
        grid=(STEPS,),
        flops=2 * LENGTH * D * INNER,
        bytes_accessed=12_000_000,
    )(back_one, full_in, block_input, cotangent, stat, vec)


def sum_squares(owned):
    def kernel(*refs):
        total = jnp.zeros((1, 128), F32)
        for ref in refs[:-1]:
            value = ref[...].astype(F32)
            total = total + jnp.sum(value * value, axis=0, keepdims=True)
        refs[-1][...] = total

    return call(
        kernel,
        "sum_squares",
        shape((1, 128), F32),
        [whole(v.shape) for v in owned],
        whole((1, 128)),
        bytes_accessed=1_000_000,
    )(*owned)


def adamw(weight, moment, square, gradient, rate, decay):
    new_moment = BETA_ONE * moment + (1.0 - BETA_ONE) * gradient
    new_square = BETA_TWO * square + (1.0 - BETA_TWO) * gradient * gradient
    moment_hat = new_moment * (1.0 / (1.0 - BETA_ONE**STEP))
    square_hat = new_square * (1.0 / (1.0 - BETA_TWO**STEP))
    update = moment_hat / (jnp.sqrt(square_hat) + ADAM_EPS)
    return weight - rate * (update + decay * weight), new_moment, new_square


def update_all(geos, owned, totals, weights, vectors):
    n = len(geos)
    size = vectors[0].shape[1]

    def kernel(*refs):
        owned_refs, total_ref = refs[:n], refs[n]
        ins = refs[n + 1 : n + 1 + 3 * n + 3]
        outs = refs[n + 1 + 3 * n + 3 :]
        grad_vec = total_ref[:, :size]
        squares = jnp.sum(grad_vec * grad_vec, axis=1, keepdims=True)
        squares = squares + jnp.sum(total_ref[:, size:], axis=1, keepdims=True)
        norm = jnp.sqrt(squares)
        outs[0][...] = norm
        clip = jnp.minimum(1.0, CLIP_LIMIT / (norm + 1e-06))
        for i, geo in enumerate(geos):
            gradient = geo.unpack(owned_refs[i][...].astype(F32)) * clip
            weight, moment, square = (r[...] for r in ins[3 * i : 3 * i + 3])
            results = adamw(weight, moment, square, gradient, RATE_MATRIX, DECAY_MATRIX)
            for ref, value in zip(outs[1 + 3 * i : 4 + 3 * i], results):
                ref[...] = value
        weight, moment, square = (r[...] for r in ins[3 * n :])
        results = adamw(weight, moment, square, grad_vec * clip, RATE_VECTOR, 0.0)
        for ref, value in zip(outs[1 + 3 * n :], results):
            ref[...] = value

    args = list(owned) + [totals] + [v for group in weights for v in group] + list(vectors)
    outs = [shape((1, 1), F32)]
    outs += [shape(v.shape, F32) for group in weights for v in group]
    outs += [shape(v.shape, F32) for v in vectors]
    return call(
        kernel,
        "update_all",
        outs,
        [whole(v.shape) for v in args],
        [whole(o.shape) for o in outs],
        bytes_accessed=4_000_000,
    )(*args)


def gather(net, shard):
    held = shard[None]
    for stage in range(net.stages()):
        held = jnp.concatenate([held, lax.ppermute(held, AXES, net.stage(stage))], axis=0)
    return held, lax.ppermute(held, AXES, net.core())


def add(a, b):
    return (a.astype(F32) + b.astype(F32)).astype(BF16)


def reduce(net, keep, send):
    held = add(keep, lax.ppermute(send, AXES, net.core()))
    for stage in range(net.stages() - 1, -1, -1):
        half = held.shape[0] // 2
        held = add(held[:half], lax.ppermute(held[half:], AXES, net.stage(stage)))
    return held[0]


def total_sum(net, value):
    value = value + lax.ppermute(value, AXES, net.core())
    for stage in range(net.stages()):
        value = value + lax.ppermute(value, AXES, net.stage(stage))
    return value


def body(
    dp,
    fsdp,
    block_input,
    cotangent,
    protein_lengths,
    weight_in,
    moment_in,
    square_in,
    weight_conv,
    moment_conv,
    square_conv,
    weight_out,
    moment_out,
    square_out,
    vectors,
    moment_vectors,
    square_vectors,
):
    net = Network(dp, fsdp)
    geo_in = Geometry(1, weight_in.shape[0], weight_in.shape[1])
    geo_conv = Geometry(KERNEL, weight_conv.shape[1], weight_conv.shape[2])
    geo_out = Geometry(1, weight_out.shape[0], weight_out.shape[1])
    geos = (geo_in, geo_conv, geo_out)

    def flat(v):
        return v.reshape(-1, v.shape[-1])

    me = jnp.stack([lax.axis_index("dp"), lax.axis_index("fsdp")]).astype(jnp.int32)
    ends = jnp.cumsum(protein_lengths[0]).astype(jnp.int32)
    vec = vectors.reshape(1, -1)
    x = block_input[0]
    cot = cotangent[0]

    shard_in, shard_conv, shard_out = pack_weights(geos, (weight_in, flat(weight_conv), weight_out))
    own_in, peer_in = gather(net, shard_in)
    own_conv, peer_conv = gather(net, shard_conv)
    own_out, peer_out = gather(net, shard_out)

    h1, h1_t, stat, grad_b3 = first_norm(x, cot, vec)
    h2, h2_t, n2, r2, full_in = mix_one(net, geo_in, me, own_in, peer_in, h1, vec)
    h3, h3_t, n3, r3, full_conv = mix_two(net, geo_conv, me, ends, own_conv, peer_conv, h2, vec)
    grad_out = reduce(net, *weight_gradient(net, geo_out, me, h3_t, cot, "out_gradient"))
    back_two, grad_g3, grad_s3, grad_b2, full_out = back_through_out(
        net, geo_out, me, own_out, peer_out, cot, n3, r3, vec
    )
    grad_conv = reduce(net, *conv_gradient(net, geo_conv, me, ends, h2_t, back_two))
    back_one, grad_g2, grad_s2, grad_b1 = back_through_conv(ends, back_two, full_conv, n2, r2, vec)
    grad_in = reduce(net, *weight_gradient(net, geo_in, me, h1_t, back_one, "in_gradient"))
    input_grad, grad_g1, grad_s1 = back_through_in(back_one, full_in, x, cot, stat, vec)
    block_output = block_result(x, h3, full_out, vec)

    owned = (grad_in, grad_conv, grad_out)
    partial = jnp.concatenate(
        [
            grad_g1,
            grad_s1,
            grad_g2,
            grad_s2,
            grad_g3,
            grad_s3,
            grad_b1,
            grad_b2,
            grad_b3,
            sum_squares(owned),
        ],
        axis=1,
    )
    totals = total_sum(net, partial)
    results = update_all(
        geos,
        owned,
        totals,
        (
            (weight_in, moment_in, square_in),
            (flat(weight_conv), flat(moment_conv), flat(square_conv)),
            (weight_out, moment_out, square_out),
        ),
        (vec, moment_vectors.reshape(1, -1), square_vectors.reshape(1, -1)),
    )
    norm, news = results[0], results[1:]
    return (
        block_output[None],
        input_grad[None],
        norm[0, 0],
        *news[0:3],
        *(v.reshape(weight_conv.shape) for v in news[3:6]),
        *news[6:9],
        *(v.reshape(-1) for v in news[9:12]),
    )


def solution(mesh):
    rows = P(("dp", "fsdp"), None, None)
    matrix = P("fsdp", "dp")
    taps = P(None, "fsdp", "dp")
    weights = (matrix,) * 3 + (taps,) * 3 + (matrix,) * 3 + (P(),) * 3
    return jax.shard_map(
        functools.partial(body, mesh.shape["dp"], mesh.shape["fsdp"]),
        mesh=mesh,
        in_specs=(rows, rows, P(("dp", "fsdp"), None)) + weights,
        out_specs=(rows, rows, P()) + weights,
        check_vma=False,
    )
```

time: 554 us -> 255 us (0.46); the launches traced: 547 us -> 254 us
  waiting for transfers between devices: 338 us -> 80.6 us
  Pallas kernels: 0 us -> 102 us
  blocking collectives: 65.3 us -> 0 us
  matrix products: 62.5 us -> 0 us
  starting transfers between devices: 0.8 us -> 46.4 us
  other arithmetic: 35.6 us -> 13.4 us
  between operations: 19.3 us -> 1.24 us
  local copies, waits for them, and re-layouts: 25.2 us -> 10.6 us
    reduce_scatter x3 -> x0, waiting for transfers between devices: 169 us -> none  [the longest x1 85.7 us: body(): lax.psum_scatter(grad_conv.astype(jnp.bfloat16), 'fsdp', scatter_dimensio...]
    all_gather x3 -> x0, waiting for transfers between devices: 111 us -> none  [the longest x1 63.8 us: body(): lax.all_gather(parts_dp[1], 'fsdp', axis=1, tiled=True)]
    pallas_call x0 -> x13, Pallas kernels: none -> 102 us  [the longest x1 15.3 us: mix_two(): call(kernel, 'mix_two', NORM_SHAPES + [shape((KERNEL * INNER, INNER), BF1...]
    ppermute x0 -> x35, waiting for transfers between devices: none -> 80.6 us  [the longest x12 43.1 us: gather(): lax.ppermute(held, AXES, net.stage(stage))]
    dot_general x21 -> x0, matrix products: 62.5 us -> none  [the longest x5 10.9 us: dilated_backward(): jnp.einsum('rli,rlo->io', shifted(hidden, offset), masked, preferred_elem...]
    unnamed x12 -> x0, waiting for transfers between devices: 58 us -> none
    ppermute x0 -> x35, starting transfers between devices: none -> 46.4 us  [the longest x12 21.3 us: reduce(): held = add(held[:half], lax.ppermute(held[half:], AXES, net.stage(stage)))]
    psum x1 -> x0, blocking collectives: 39.8 us -> none  [body(): weight_total = lax.psum(local_squares, ('dp', 'fsdp'))]
  transfers between devices with their start and end apart: 9 -> 35, of which waited for: 9 -> 20; matrix products, arithmetic and copies ran while one was open for 18% -> 5% of each run, Pallas kernels for 0% -> 29%
where the time goes in v1:
time: 255 us; the launch traced here: 254 us
  Pallas kernels  102 us (40%)
  waiting for transfers between devices  80.6 us (32%)
  starting transfers between devices  46.4 us (18%)
  other arithmetic  13.4 us (5%)
  local copies, waits for them, and re-layouts  10.6 us (4%)
    ppermute x12, waiting for transfers between devices, gather(): lax.ppermute(held, AXES, net.stage(stage))  43.1 us
    ppermute x12, waiting for transfers between devices, reduce(): held = add(held[:half], lax.ppermute(held[half:], AXES, net.stage(stage)))  28.7 us
    ppermute x12, starting transfers between devices, reduce(): held = add(held[:half], lax.ppermute(held[half:], AXES, net.stage(stage)))  21.3 us
    ppermute x12, starting transfers between devices, gather(): lax.ppermute(held, AXES, net.stage(stage))  18.2 us
    pallas_call x1, Pallas kernels, mix_two(): call(kernel, 'mix_two', NORM_SHAPES + [shape((KERNEL * INNER, INNER), BF1...  15.3 us
    pallas_call x1, Pallas kernels, back_through_conv(): call(kernel, 'back_through_conv', [shape((LENGTH, INNER), BF16), row, row...  12.7 us
    pallas_call x2, Pallas kernels, weight_gradient(): call(kernel, name, gradient_shapes(net, geo), [SMEM, whole(left.shape), w...  11.8 us
    pallas_call x1, Pallas kernels, conv_gradient(): call(kernel, 'conv_gradient', gradient_shapes(net, geo), [SMEM, SMEM, who...  10.8 us
  transfers between devices with their start and end apart: 35, of which 20 were waited for; matrix products, arithmetic and copies ran while one was open for 5% of the time, Pallas kernels for 29%

profile of v1, /device:TPU:0, one launch (start us, length us, event | category | flops | bytes accessed | tf_op | source)
XLA Modules:
  0.0 253.8 jit_solution(4513183989661532481)
XLA Ops:
  0.6 1.9 pack_weights.1
  2.5 4.1 %collective-permute-start = (bf16[1,512,128]{2,1,0:T(8,128)(2,1)}, bf16[1,512,128]{2,1,0:T(8,128)(2,1)S(1)}, u32[]{:S(2)}, u32[]{:S(2)}) collective-permute-start(bf16[1,512,128]{2,1,0:T(8,128)(2,1)} %bitcast.35), channel_id=1, source_target_pairs={{0,4},{1,5},{2,6},{3,7},{4,0},{5,1},{6,2},{7,3},{8,12},{9,13},{10,... | collective-permute-start | bytes 393224 | tf_op jit(solution)/shard_map/ppermute | solution.py:656
  6.6 6.5 %collective-permute-done = bf16[1,512,128]{2,1,0:T(8,128)(2,1)S(1)} collective-permute-done((bf16[1,512,128]{2,1,0:T(8,128)(2,1)}, bf16[1,512,128]{2,1,0:T(8,128)(2,1)S(1)}, u32[]{:S(2)}, u32[]{:S(2)}) %collective-permute-start) | collective-permute-done | bytes 131104 | tf_op jit(solution)/shard_map/ppermute | solution.py:656
  13.2 0.9 pad_maximum_fusion.4
  14.1 0.9 collective-permute-start.1
  15.0 6.7 %collective-permute-done.1 = bf16[2,512,128]{2,1,0:T(8,128)(2,1)S(1)} collective-permute-done((bf16[2,512,128]{2,1,0:T(8,128)(2,1)S(1)}, bf16[2,512,128]{2,1,0:T(8,128)(2,1)S(1)}, u32[]{:S(2)}, u32[]{:S(2)}) %collective-permute-start.1) | collective-permute-done | bytes 262176 | tf_op jit(solution)/shard_map/ppermute | solution.py:656
  21.6 1.0 pad_maximum_fusion.1
  22.6 1.4 collective-permute-start.2
  24.0 7.9 %collective-permute-done.2 = bf16[4,512,128]{2,1,0:T(8,128)(2,1)S(1)} collective-permute-done((bf16[4,512,128]{2,1,0:T(8,128)(2,1)S(1)}, bf16[4,512,128]{2,1,0:T(8,128)(2,1)S(1)}, u32[]{:S(2)}, u32[]{:S(2)}) %collective-permute-start.2) | collective-permute-done | bytes 524320 | tf_op jit(solution)/shard_map/ppermute | solution.py:656
  31.9 1.0 pad_maximum_fusion
  32.9 1.4 collective-permute-start.3
  34.3 3.3 %collective-permute-start.5 = (bf16[1,208,128]{2,1,0:T(8,128)(2,1)S(1)}, bf16[1,208,128]{2,1,0:T(8,128)(2,1)S(1)}, u32[]{:S(2)}, u32[]{:S(2)}) collective-permute-start(bf16[1,208,128]{2,1,0:T(8,128)(2,1)S(1)} %bitcast.45), channel_id=1, source_target_pairs={{0,4},{1,5},{2,6},{3,7},{4,0},{5,1},{6,2},{7,3},{8,12},{9,13},{10,... | collective-permute-start | bytes 159752 | tf_op jit(solution)/shard_map/ppermute | solution.py:656
  38.3 3.2 %collective-permute-done.5 = bf16[1,208,128]{2,1,0:T(8,128)(2,1)S(1)} collective-permute-done((bf16[1,208,128]{2,1,0:T(8,128)(2,1)S(1)}, bf16[1,208,128]{2,1,0:T(8,128)(2,1)S(1)}, u32[]{:S(2)}, u32[]{:S(2)}) %collective-permute-start.5) | collective-permute-done | bytes 53280 | tf_op jit(solution)/shard_map/ppermute | solution.py:656
  42.6 3.7 %collective-permute-done.6 = bf16[2,208,128]{2,1,0:T(8,128)(2,1)S(1)} collective-permute-done((bf16[2,208,128]{2,1,0:T(8,128)(2,1)S(1)}, bf16[2,208,128]{2,1,0:T(8,128)(2,1)S(1)}, u32[]{:S(2)}, u32[]{:S(2)}) %collective-permute-start.6) | collective-permute-done | bytes 106528 | tf_op jit(solution)/shard_map/ppermute | solution.py:656
  47.3 0.9 constant_dynamic-update-slice_fusion.1
  48.2 1.8 collective-permute-done.3
  50.0 1.1 constant_dynamic-update-slice_fusion.own_ref
  51.1 1.6 collective-permute-start.11
  52.8 1.6 collective-permute-start.8
  54.4 2.2 collective-permute-done.11
  56.6 1.4 collective-permute-start.12
  58.0 4.9 %collective-permute-done.8 = bf16[8,208,128]{2,1,0:T(8,128)(2,1)S(1)} collective-permute-done((bf16[8,208,128]{2,1,0:T(8,128)(2,1)S(1)}, bf16[8,208,128]{2,1,0:T(8,128)(2,1)S(1)}, u32[]{:S(2)}, u32[]{:S(2)}) %collective-permute-start.8) | collective-permute-done | bytes 426016 | tf_op jit(solution)/shard_map/ppermute | solution.py:656
  63.1 1.8 collective-permute-start.13
  65.0 6.3 %collective-permute-done.13 = bf16[8,208,128]{2,1,0:T(8,128)(2,1)S(1)} collective-permute-done((bf16[8,208,128]{2,1,0:T(8,128)(2,1)S(1)}, bf16[8,208,128]{2,1,0:T(8,128)(2,1)S(1)}, u32[]{:S(2)}, u32[]{:S(2)}) %collective-permute-start.13) | collective-permute-done | bytes 426016 | tf_op jit(solution)/shard_map/ppermute | solution.py:656
  72.9 7.6 %first_norm.1 = (bf16[1024,1280]{1,0:T(8,128)(2,1)}, bf16[1280,1024]{1,0:T(8,128)(2,1)}, f32[1024,128]{1,0:T(8,128)}, f32[1,1280]{1,0:T(1,128)}) custom-call(bf16[1024,1280]{1,0:T(8,128)(2,1)} %bitcast.31, bf16[1024,1280]{1,0:T(8,128)(2,1)} %bitcast.27, f32[1,7680]{1,0:T(1,128)} %reshape.97.vec_ref.refs_13_), custom_call_target="tpu_custom_call" | custom-call | flops 39321600 | bytes 10485760 | tf_op jit(solution)/shard_map/first_norm/pallas_call | solution.py:316
  81.2 0.9 copy-done.19
  82.1 9.8 %mix_one.1 = (bf16[1024,640]{1,0:T(8,128)(2,1)}, bf16[640,1024]{1,0:T(8,128)(2,1)}, f32[1024,640]{1,0:T(8,128)}, f32[1024,128]{1,0:T(8,128)}, bf16[1280,640]{1,0:T(8,128)(2,1)}) custom-call(s32[2]{0:T(128)} %pad_add_fusion.me_ref, bf16[16,208,128]{2,1,0:T(8,128)(2,1)} %copy-done.12, bf16[16,208,128]{2,1,0:T(8,128)(2,1)} %copy-done.19, ...), custom_call_target="tpu_custom_call" | custom-call | flops 1677721600 | bytes 12000000 | tf_op jit(solution)/shard_map/mix_one/pallas_call | solution.py:369
  91.9 15.3 %mix_two.1 = (bf16[1024,640]{1,0:T(8,128)(2,1)}, bf16[640,1024]{1,0:T(8,128)(2,1)}, f32[1024,640]{1,0:T(8,128)}, f32[1024,128]{1,0:T(8,128)}, bf16[3200,640]{1,0:T(8,128)(2,1)}) custom-call(s32[2]{0:T(128)} %pad_add_fusion.me_ref, s32[4]{0:T(128)} %bitcast.56, bf16[16,512,128]{2,1,0:T(8,128)(2,1)} %constant_dynamic-update-slice_fusion.own_ref, ...), custom_call_target="tpu_custom_call" | custom-call | flops 4194304000 | bytes 18000000 | tf_op jit(solution)/shard_map/mix_two/pallas_call | solution.py:402
  107.2 1.0 copy-done.3
  108.2 10.0 %back_through_out.1 = (bf16[1024,640]{1,0:T(8,128)(2,1)}, f32[1,640]{1,0:T(1,128)}, f32[1,640]{1,0:T(1,128)}, f32[1,640]{1,0:T(1,128)}, bf16[640,1280]{1,0:T(8,128)(2,1)}) custom-call(s32[2]{0:T(128)} %pad_add_fusion.me_ref, bf16[16,208,128]{2,1,0:T(8,128)(2,1)} %copy-done.2, bf16[16,208,128]{2,1,0:T(8,128)(2,1)} %copy-done.3, bf16[1024,1280]{1,0:T(8,128)(2,1)} %bitcast.28, ...), custom_call_target="tpu_custom_call" | custom-call | flops 1677721600 | bytes 12000000 | tf_op jit(solution)/shard_map/back_through_out/pallas_call | solution.py:460
  118.2 10.8 %conv_gradient.1 = (bf16[16,512,128]{2,1,0:T(8,128)(2,1)}, bf16[16,512,128]{2,1,0:T(8,128)(2,1)}) custom-call(s32[2]{0:T(128)} %pad_add_fusion.me_ref, s32[4]{0:T(128)} %bitcast.57, bf16[640,1024]{1,0:T(8,128)(2,1)} %get-tuple-element.83.left_ref, bf16[1024,640]{1,0:T(8,128)(2,1)} %get-tuple-element.72.back_ref), custom_call_target="tpu_custom_call" | custom-call | flops 4194304000 | bytes 7000000 | tf_op jit(solution)/shard_map/conv_gradient/pallas_call | solution.py:499
  129.4 5.5 %out_gradient.1 = (bf16[16,208,128]{2,1,0:T(8,128)(2,1)}, bf16[16,208,128]{2,1,0:T(8,128)(2,1)}) custom-call(s32[2]{0:T(128)} %pad_add_fusion.me_ref, bf16[640,1024]{1,0:T(8,128)(2,1)} %get-tuple-element.86.left_ref, bf16[1024,1280]{1,0:T(8,128)(2,1)} %bitcast.29), custom_call_target="tpu_custom_call" | custom-call | flops 1677721600 | bytes 6000000 | tf_op jit(solution)/shard_map/out_gradient/pallas_call | solution.py:426
  135.1 12.7 %back_through_conv.1 = (bf16[1024,640]{1,0:T(8,128)(2,1)}, f32[1,640]{1,0:T(1,128)}, f32[1,640]{1,0:T(1,128)}, f32[1,640]{1,0:T(1,128)}) custom-call(s32[4]{0:T(128)} %bitcast.58, bf16[1024,640]{1,0:T(8,128)(2,1)} %get-tuple-element.72.back_ref, bf16[3200,640]{1,0:T(8,128)(2,1)} %get-tuple-element.73.w_ref, f32[1024,640]{1,0:T(8,128)} %get-tuple-element.74.n_ref, ...), custom_call_target="tpu_custom_call" | custom-call | flops 4194304000 | bytes 10000000 | tf_op jit(solution)/shard_map/back_through_conv/pallas_call | solution.py:541
  147.8 6.2 %in_gradient.1 = (bf16[16,208,128]{2,1,0:T(8,128)(2,1)}, bf16[16,208,128]{2,1,0:T(8,128)(2,1)}) custom-call(s32[2]{0:T(128)} %pad_add_fusion.me_ref, bf16[1280,1024]{1,0:T(8,128)(2,1)} %get-tuple-element.80.left_ref, bf16[1024,640]{1,0:T(8,128)(2,1)} %get-tuple-element.76.back_ref.right_ref), custom_call_target="tpu_custom_call" | custom-call | flops 1677721600 | bytes 6000000 | tf_op jit(solution)/shard_map/in_gradient/pallas_call | solution.py:426
  154.5 10.5 %back_through_in.1 = (bf16[1024,1280]{1,0:T(8,128)(2,1)}, f32[1,1280]{1,0:T(1,128)}, f32[1,1280]{1,0:T(1,128)}) custom-call(bf16[1024,640]{1,0:T(8,128)(2,1)} %get-tuple-element.76.back_ref.right_ref, bf16[1280,640]{1,0:T(8,128)(2,1)} %get-tuple-element.77.w_ref, bf16[1024,1280]{1,0:T(8,128)(2,1)} %bitcast.32, bf16[1024,1280]{1,0:T(8,128)(2,1)} %bitcast.30, ...), custom_call_target="tpu_custom_call" | custom-call | flops 1677721600 | bytes 12000000 | tf_op jit(solution)/shard_map/back_through_in/pallas_call | solution.py:575
  167.2 1.8 collective-permute-start.21
  169.4 1.1 collective-permute-start.26
  170.8 1.1 collective-permute-start.16
  171.9 14.8 %collective-permute-done.26 = bf16[8,208,128]{2,1,0:T(8,128)(2,1)S(1)} collective-permute-done((bf16[8,208,128]{2,1,0:T(8,128)(2,1)S(1)}, bf16[8,208,128]{2,1,0:T(8,128)(2,1)S(1)}, u32[]{:S(2)}, u32[]{:S(2)}) %collective-permute-start.26) | collective-permute-done | bytes 426016 | tf_op jit(solution)/shard_map/ppermute | solution.py:668
  186.8 1.7 collective-permute-start.27
  188.6 5.0 %collective-permute-done.16 = bf16[8,208,128]{2,1,0:T(8,128)(2,1)S(1)} collective-permute-done((bf16[8,208,128]{2,1,0:T(8,128)(2,1)S(1)}, bf16[8,208,128]{2,1,0:T(8,128)(2,1)S(1)}, u32[]{:S(2)}, u32[]{:S(2)}) %collective-permute-start.16) | collective-permute-done | bytes 426016 | tf_op jit(solution)/shard_map/ppermute | solution.py:668
  193.7 1.8 collective-permute-start.17
  196.3 1.1 collective-permute-start.28
  197.4 2.3 collective-permute-done.17
  199.7 1.1 collective-permute-start.18
  201.2 3.7 %collective-permute-start.29 = (bf16[1,208,128]{2,1,0:T(8,128)(2,1)S(1)}, bf16[1,208,128]{2,1,0:T(8,128)(2,1)S(1)}, u32[]{:S(2)}, u32[]{:S(2)}) collective-permute-start(bf16[1,208,128]{2,1,0:T(8,128)(2,1)S(1)} %slice.119), channel_id=1, source_target_pairs={{0,4},{1,5},{2,6},{3,7},{4,0},{5,1},{6,2},{7,3},{8,12},{9,13},{10,... | collective-permute-start | bytes 159752 | tf_op jit(solution)/shard_map/ppermute | solution.py:668
  205.5 1.1 collective-permute-start.23
  206.6 3.3 %collective-permute-start.19 = (bf16[1,208,128]{2,1,0:T(8,128)(2,1)S(1)}, bf16[1,208,128]{2,1,0:T(8,128)(2,1)S(1)}, u32[]{:S(2)}, u32[]{:S(2)}) collective-permute-start(bf16[1,208,128]{2,1,0:T(8,128)(2,1)S(1)} %slice.103), channel_id=1, source_target_pairs={{0,4},{1,5},{2,6},{3,7},{4,0},{5,1},{6,2},{7,3},{8,12},{9,13},{10,... | collective-permute-start | bytes 159752 | tf_op jit(solution)/shard_map/ppermute | solution.py:668
  210.6 3.0 %collective-permute-done.23 = bf16[2,512,128]{2,1,0:T(8,128)(2,1)S(1)} collective-permute-done((bf16[2,512,128]{2,1,0:T(8,128)(2,1)S(1)}, bf16[2,512,128]{2,1,0:T(8,128)(2,1)S(1)}, u32[]{:S(2)}, u32[]{:S(2)}) %collective-permute-start.23) | collective-permute-done | bytes 262176 | tf_op jit(solution)/shard_map/ppermute | solution.py:668
  213.6 3.3 %collective-permute-start.24 = (bf16[1,512,128]{2,1,0:T(8,128)(2,1)S(1)}, bf16[1,512,128]{2,1,0:T(8,128)(2,1)S(1)}, u32[]{:S(2)}, u32[]{:S(2)}) collective-permute-start(bf16[1,512,128]{2,1,0:T(8,128)(2,1)S(1)} %slice.111), channel_id=1, source_target_pairs={{0,4},{1,5},{2,6},{3,7},{4,0},{5,1},{6,2},{7,3},{8,12},{9,13},{10,... | collective-permute-start | bytes 393224 | tf_op jit(solution)/shard_map/ppermute | solution.py:668
  217.6 2.9 %collective-permute-done.24 = bf16[1,512,128]{2,1,0:T(8,128)(2,1)S(1)} collective-permute-done((bf16[1,512,128]{2,1,0:T(8,128)(2,1)S(1)}, bf16[1,512,128]{2,1,0:T(8,128)(2,1)S(1)}, u32[]{:S(2)}, u32[]{:S(2)}) %collective-permute-start.24) | collective-permute-done | bytes 131104 | tf_op jit(solution)/shard_map/ppermute | solution.py:668
  221.1 1.5 sum_squares.1
  223.3 1.2 collective-permute-done.30
  224.5 2.4 collective-permute-start.31
  226.9 2.4 collective-permute-done.31
  229.5 3.9 %collective-permute-done.32 = f32[1,7808]{1,0:T(1,128)S(1)} collective-permute-done((f32[1,7808]{1,0:T(1,128)S(1)}, f32[1,7808]{1,0:T(1,128)S(1)}, u32[]{:S(2)}, u32[]{:S(2)}) %collective-permute-start.32) | collective-permute-done | bytes 31264 | tf_op jit(solution)/shard_map/ppermute | solution.py:675
  233.4 1.6 collective-permute-start.33
  236.2 1.2 collective-permute-done.33
  237.5 1.6 collective-permute-start.34
  239.1 6.2 %block_result.1 = bf16[1024,1280]{1,0:T(8,128)(2,1)} custom-call(bf16[1024,1280]{1,0:T(8,128)(2,1)} %bitcast.33, bf16[1024,640]{1,0:T(8,128)(2,1)} %get-tuple-element.67.h_ref, bf16[640,1280]{1,0:T(8,128)(2,1)} %get-tuple-element.71.w_ref, f32[1,7680]{1,0:T(1,128)} %reshape.97.vec_ref.refs_13_), custom_call_target="tpu_custom_call" | custom-call | flops 1677721600 | bytes 8000000 | tf_op jit(solution)/shard_map/block_result/pallas_call | solution.py:478
  245.9 3.6 %update_all.1 = (f32[1,1]{1,0:T(1,128)}, f32[160,160]{1,0:T(8,128)}, f32[160,160]{1,0:T(8,128)}, f32[160,160]{1,0:T(8,128)}, f32[400,160]{1,0:T(8,128)}, /*index...) custom-call(bf16[208,128]{1,0:T(8,128)(2,1)} %fusion.1.refs_0_, ...), custom_call_target="tpu_custom_call" | custom-call | bytes 4000000 | tf_op jit(solution)/shard_map/update_all/pallas_call | solution.py:643
  249.5 1.4 reduce
  251.0 1.4 reduce.1
  252.4 1.4 reduce.2
  (134 shorter events, 16.3 us)
Async XLA Ops:
  2.5 31.7 %copy-start.7 = (bf16[208,128]{1,0:T(8,128)(2,1)S(1)}, bf16[208,128]{1,0:T(8,128)(2,1)}, u32[]{:S(2)}) copy-start(bf16[208,128]{1,0:T(8,128)(2,1)} %get-tuple-element.64) | copy-start | bytes 159748
  2.5 35.0 %copy-start.6 = (bf16[208,128]{1,0:T(8,128)(2,1)S(1)}, bf16[208,128]{1,0:T(8,128)(2,1)}, u32[]{:S(2)}) copy-start(bf16[208,128]{1,0:T(8,128)(2,1)} %get-tuple-element.68) | copy-start | bytes 159748
  2.5 35.1 %copy-start.1 = (bf16[512,128]{1,0:T(8,128)(2,1)S(1)}, bf16[512,128]{1,0:T(8,128)(2,1)}, u32[]{:S(2)}) copy-start(bf16[512,128]{1,0:T(8,128)(2,1)} %get-tuple-element.63) | copy-start | bytes 393220
  2.5 10.6 %collective-permute-start = (bf16[1,512,128]{2,1,0:T(8,128)(2,1)}, bf16[1,512,128]{2,1,0:T(8,128)(2,1)S(1)}, u32[]{:S(2)}, u32[]{:S(2)}) collective-permute-start(bf16[1,512,128]{2,1,0:T(8,128)(2,1)} %bitcast.35), channel_id=1, source_target_pairs={{0,4},{1,5},{2,6},{3,7},{4,0},{5,1},{6,2},{7,3},{8,12},{9,13},{10,... | collective-permute-start | bytes 393224 | tf_op jit(solution)/shard_map/ppermute | solution.py:656
  14.1 7.6 %collective-permute-start.1 = (bf16[2,512,128]{2,1,0:T(8,128)(2,1)S(1)}, bf16[2,512,128]{2,1,0:T(8,128)(2,1)S(1)}, u32[]{:S(2)}, u32[]{:S(2)}) collective-permute-start(bf16[2,512,128]{2,1,0:T(8,128)(2,1)S(1)} %pad_maximum_fusion.4), channel_id=1, source_target_pairs={{0,2},{1,3},{2,0},{3,1},{4,6},{5,7},{6,4},{7,5},{8,10},{9,11},{10,... | collective-permute-start | bytes 786440 | tf_op jit(solution)/shard_map/ppermute | solution.py:656
  22.6 9.2 %collective-permute-start.2 = (bf16[4,512,128]{2,1,0:T(8,128)(2,1)S(1)}, bf16[4,512,128]{2,1,0:T(8,128)(2,1)S(1)}, u32[]{:S(2)}, u32[]{:S(2)}) collective-permute-start(bf16[4,512,128]{2,1,0:T(8,128)(2,1)S(1)} %pad_maximum_fusion.1), channel_id=1, source_target_pairs={{0,1},{1,0},{2,3},{3,2},{4,5},{5,4},{6,7},{7,6},{8,24},{9,25},{10,... | collective-permute-start | bytes 1572872 | tf_op jit(solution)/shard_map/ppermute | solution.py:656
  32.9 17.1 %collective-permute-start.3 = (bf16[8,512,128]{2,1,0:T(8,128)(2,1)S(1)}, bf16[8,512,128]{2,1,0:T(8,128)(2,1)S(1)}, u32[]{:S(2)}, u32[]{:S(2)}) collective-permute-start(bf16[8,512,128]{2,1,0:T(8,128)(2,1)S(1)} %pad_maximum_fusion), channel_id=1, source_target_pairs={{0,16},{1,17},{2,18},{3,19},{4,20},{5,21},{6,22},{7,23},{8,9},{9,8... | collective-permute-start | bytes 3145736 | tf_op jit(solution)/shard_map/ppermute | solution.py:656
  34.3 7.2 %collective-permute-start.5 = (bf16[1,208,128]{2,1,0:T(8,128)(2,1)S(1)}, bf16[1,208,128]{2,1,0:T(8,128)(2,1)S(1)}, u32[]{:S(2)}, u32[]{:S(2)}) collective-permute-start(bf16[1,208,128]{2,1,0:T(8,128)(2,1)S(1)} %bitcast.45), channel_id=1, source_target_pairs={{0,4},{1,5},{2,6},{3,7},{4,0},{5,1},{6,2},{7,3},{8,12},{9,13},{10,... | collective-permute-start | bytes 159752 | tf_op jit(solution)/shard_map/ppermute | solution.py:656
  37.5 13.5 %collective-permute-start.10 = (bf16[1,208,128]{2,1,0:T(8,128)(2,1)S(1)}, bf16[1,208,128]{2,1,0:T(8,128)(2,1)S(1)}, u32[]{:S(2)}, u32[]{:S(2)}) collective-permute-start(bf16[1,208,128]{2,1,0:T(8,128)(2,1)S(1)} %bitcast.41), channel_id=1, source_target_pairs={{0,4},{1,5},{2,6},{3,7},{4,0},{5,1},{6,2},{7,3},{8,12},{9,13},{10,... | collective-permute-start | bytes 159752 | tf_op jit(solution)/shard_map/ppermute | solution.py:656
  41.5 4.8 %collective-permute-start.6 = (bf16[2,208,128]{2,1,0:T(8,128)(2,1)S(1)}, bf16[2,208,128]{2,1,0:T(8,128)(2,1)S(1)}, u32[]{:S(2)}, u32[]{:S(2)}) collective-permute-start(bf16[2,208,128]{2,1,0:T(8,128)(2,1)S(1)} %pad_maximum_fusion.7), channel_id=1, source_target_pairs={{0,2},{1,3},{2,0},{3,1},{4,6},{5,7},{6,4},{7,5},{8,10},{9,11},{10,... | collective-permute-start | bytes 319496 | tf_op jit(solution)/shard_map/ppermute | solution.py:656
  46.3 6.5 %collective-permute-start.7 = (bf16[4,208,128]{2,1,0:T(8,128)(2,1)S(1)}, bf16[4,208,128]{2,1,0:T(8,128)(2,1)S(1)}, u32[]{:S(2)}, u32[]{:S(2)}) collective-permute-start(bf16[4,208,128]{2,1,0:T(8,128)(2,1)S(1)} %pad_maximum_fusion.5), channel_id=1, source_target_pairs={{0,1},{1,0},{2,3},{3,2},{4,5},{5,4},{6,7},{7,6},{8,24},{9,25},{10,... | collective-permute-start | bytes 638984 | tf_op jit(solution)/shard_map/ppermute | solution.py:656
  51.1 40.9 %collective-permute-start.4 = (bf16[16,512,128]{2,1,0:T(8,128)(2,1)}, bf16[16,512,128]{2,1,0:T(8,128)(2,1)}, u32[]{:S(2)}, u32[]{:S(2)}) collective-permute-start(bf16[16,512,128]{2,1,0:T(8,128)(2,1)} %constant_dynamic-update-slice_fusion.own_ref), channel_id=1, source_target_pairs={{0,8},{1,9},{2,10},{3,11},{4,12},{5,13},{6,14},{7,15},{8,0},{9,1},... | collective-permute-start | bytes 6291464 | tf_op jit(solution)/shard_map/ppermute | solution.py:657
  51.1 5.4 %collective-permute-start.11 = (bf16[2,208,128]{2,1,0:T(8,128)(2,1)S(1)}, bf16[2,208,128]{2,1,0:T(8,128)(2,1)S(1)}, u32[]{:S(2)}, u32[]{:S(2)}) collective-permute-start(bf16[2,208,128]{2,1,0:T(8,128)(2,1)S(1)} %pad_maximum_fusion.8), channel_id=1, source_target_pairs={{0,2},{1,3},{2,0},{3,1},{4,6},{5,7},{6,4},{7,5},{8,10},{9,11},{10,... | collective-permute-start | bytes 319496 | tf_op jit(solution)/shard_map/ppermute | solution.py:656
  52.8 10.1 %collective-permute-start.8 = (bf16[8,208,128]{2,1,0:T(8,128)(2,1)S(1)}, bf16[8,208,128]{2,1,0:T(8,128)(2,1)S(1)}, u32[]{:S(2)}, u32[]{:S(2)}) collective-permute-start(bf16[8,208,128]{2,1,0:T(8,128)(2,1)S(1)} %pad_maximum_fusion.2), channel_id=1, source_target_pairs={{0,16},{1,17},{2,18},{3,19},{4,20},{5,21},{6,22},{7,23},{8,9},{9,8... | collective-permute-start | bytes 1277960 | tf_op jit(solution)/shard_map/ppermute | solution.py:656
  54.4 17.1 %copy-start.8 = (f32[7680]{0:T(1024)S(1)}, f32[7680]{0:T(1024)}, u32[]{:S(2)}) copy-start(f32[7680]{0:T(1024)} %param.27) | copy-start | bytes 92164
  56.6 15.7 %copy-start.20 = (s32[1,4]{1,0:T(1,128)S(1)}, s32[1,4]{1,0:T(1,128)}, u32[]{:S(2)}) copy-start(s32[1,4]{1,0:T(1,128)} %param.17) | copy-start | bytes 52
  56.6 6.5 %collective-permute-start.12 = (bf16[4,208,128]{2,1,0:T(8,128)(2,1)S(1)}, bf16[4,208,128]{2,1,0:T(8,128)(2,1)S(1)}, u32[]{:S(2)}, u32[]{:S(2)}) collective-permute-start(bf16[4,208,128]{2,1,0:T(8,128)(2,1)S(1)} %pad_maximum_fusion.6), channel_id=1, source_target_pairs={{0,1},{1,0},{2,3},{3,2},{4,5},{5,4},{6,7},{7,6},{8,24},{9,25},{10,... | collective-permute-start | bytes 638984 | tf_op jit(solution)/shard_map/ppermute | solution.py:656
  63.0 17.6 %copy-start.12 = (bf16[16,208,128]{2,1,0:T(8,128)(2,1)}, bf16[16,208,128]{2,1,0:T(8,128)(2,1)S(1)}, u32[]{:S(2)}) copy-start(bf16[16,208,128]{2,1,0:T(8,128)(2,1)S(1)} %constant_dynamic-update-slice_fusion.5.own_ref) | copy-start | bytes 2555908
  63.0 18.2 %collective-permute-start.9 = (bf16[16,208,128]{2,1,0:T(8,128)(2,1)S(1)}, bf16[16,208,128]{2,1,0:T(8,128)(2,1)S(1)}, u32[]{:S(2)}, u32[]{:S(2)}) collective-permute-start(bf16[16,208,128]{2,1,0:T(8,128)(2,1)S(1)} %constant_dynamic-update-slice_fusion.5.own_ref), channel_id=1, source_target_pairs={{0,8},{1,9},{2,10},{3,11},{4,12},{5,13},{6,14},{7,15},{8,0},{9,1},... | collective-permute-start | bytes 2555912 | tf_op jit(solution)/shard_map/ppermute | solution.py:657
  63.1 8.2 %collective-permute-start.13 = (bf16[8,208,128]{2,1,0:T(8,128)(2,1)S(1)}, bf16[8,208,128]{2,1,0:T(8,128)(2,1)S(1)}, u32[]{:S(2)}, u32[]{:S(2)}) collective-permute-start(bf16[8,208,128]{2,1,0:T(8,128)(2,1)S(1)} %pad_maximum_fusion.3), channel_id=1, source_target_pairs={{0,16},{1,17},{2,18},{3,19},{4,20},{5,21},{6,22},{7,23},{8,9},{9,8... | collective-permute-start | bytes 1277960 | tf_op jit(solution)/shard_map/ppermute | solution.py:656
  71.4 9.2 %copy-start.2 = (bf16[16,208,128]{2,1,0:T(8,128)(2,1)}, bf16[16,208,128]{2,1,0:T(8,128)(2,1)S(1)}, u32[]{:S(2)}) copy-start(bf16[16,208,128]{2,1,0:T(8,128)(2,1)S(1)} %constant_dynamic-update-slice_fusion.10.own_ref) | copy-start | bytes 2555908
  71.4 35.8 %collective-permute-start.14 = (bf16[16,208,128]{2,1,0:T(8,128)(2,1)S(1)}, bf16[16,208,128]{2,1,0:T(8,128)(2,1)S(1)}, u32[]{:S(2)}, u32[]{:S(2)}) collective-permute-start(bf16[16,208,128]{2,1,0:T(8,128)(2,1)S(1)} %constant_dynamic-update-slice_fusion.10.own_ref), channel_id=1, source_target_pairs={{0,8},{1,9},{2,10},{3,11},{4,12},{5,13},{6,14},{7,15},{8,0},{9,1},... | collective-permute-start | bytes 2555912 | tf_op jit(solution)/shard_map/ppermute | solution.py:657
  81.2 0.9 copy-start.19
  107.2 1.0 copy-start.3
  129.0 37.6 %collective-permute-start.20 = (bf16[16,512,128]{2,1,0:T(8,128)(2,1)}, bf16[16,512,128]{2,1,0:T(8,128)(2,1)S(1)}, u32[]{:S(2)}, u32[]{:S(2)}) collective-permute-start(bf16[16,512,128]{2,1,0:T(8,128)(2,1)} %get-tuple-element.85), channel_id=1, source_target_pairs={{0,8},{1,9},{2,10},{3,11},{4,12},{5,13},{6,14},{7,15},{8,0},{9,1},... | collective-permute-start | bytes 6291464 | tf_op jit(solution)/shard_map/ppermute | solution.py:665
  134.9 34.1 %collective-permute-start.25 = (bf16[16,208,128]{2,1,0:T(8,128)(2,1)}, bf16[16,208,128]{2,1,0:T(8,128)(2,1)S(1)}, u32[]{:S(2)}, u32[]{:S(2)}) collective-permute-start(bf16[16,208,128]{2,1,0:T(8,128)(2,1)} %get-tuple-element.88), channel_id=1, source_target_pairs={{0,8},{1,9},{2,10},{3,11},{4,12},{5,13},{6,14},{7,15},{8,0},{9,1},... | collective-permute-start | bytes 2555912 | tf_op jit(solution)/shard_map/ppermute | solution.py:665
  154.1 16.3 %collective-permute-start.15 = (bf16[16,208,128]{2,1,0:T(8,128)(2,1)}, bf16[16,208,128]{2,1,0:T(8,128)(2,1)S(1)}, u32[]{:S(2)}, u32[]{:S(2)}) collective-permute-start(bf16[16,208,128]{2,1,0:T(8,128)(2,1)} %get-tuple-element.82), channel_id=1, source_target_pairs={{0,8},{1,9},{2,10},{3,11},{4,12},{5,13},{6,14},{7,15},{8,0},{9,1},... | collective-permute-start | bytes 2555912 | tf_op jit(solution)/shard_map/ppermute | solution.py:665
  154.5 12.0 %copy-start.18 = (f32[1,640]{1,0:T(1,128)S(1)}, f32[1,640]{1,0:T(1,128)}, u32[]{:S(2)}) copy-start(f32[1,640]{1,0:T(1,128)} %get-tuple-element.91) | copy-start | bytes 7684
  154.5 12.0 %copy-start.17 = (f32[1,640]{1,0:T(1,128)S(1)}, f32[1,640]{1,0:T(1,128)}, u32[]{:S(2)}) copy-start(f32[1,640]{1,0:T(1,128)} %get-tuple-element.92) | copy-start | bytes 7684
  154.5 12.0 %copy-start.15 = (f32[1,640]{1,0:T(1,128)S(1)}, f32[1,640]{1,0:T(1,128)}, u32[]{:S(2)}) copy-start(f32[1,640]{1,0:T(1,128)} %get-tuple-element.93) | copy-start | bytes 7684
  154.5 12.0 %copy-start.14 = (f32[1,640]{1,0:T(1,128)S(1)}, f32[1,640]{1,0:T(1,128)}, u32[]{:S(2)}) copy-start(f32[1,640]{1,0:T(1,128)} %get-tuple-element.94) | copy-start | bytes 7684
  154.5 12.0 %copy-start.16 = (f32[1,640]{1,0:T(1,128)S(1)}, f32[1,640]{1,0:T(1,128)}, u32[]{:S(2)}) copy-start(f32[1,640]{1,0:T(1,128)} %get-tuple-element.95) | copy-start | bytes 7684
  154.5 12.0 %copy-start.13 = (f32[1,640]{1,0:T(1,128)S(1)}, f32[1,640]{1,0:T(1,128)}, u32[]{:S(2)}) copy-start(f32[1,640]{1,0:T(1,128)} %get-tuple-element.96) | copy-start | bytes 7684
  154.5 12.1 %copy-start = (bf16[16,512,128]{2,1,0:T(8,128)(2,1)S(1)}, bf16[16,512,128]{2,1,0:T(8,128)(2,1)}, u32[]{:S(2)}) copy-start(bf16[16,512,128]{2,1,0:T(8,128)(2,1)} %get-tuple-element.84) | copy-start | bytes 6291460
  167.1 1.9 copy-start.4
  167.2 3.2 %copy-start.5 = (bf16[16,208,128]{2,1,0:T(8,128)(2,1)S(1)}, bf16[16,208,128]{2,1,0:T(8,128)(2,1)}, u32[]{:S(2)}) copy-start(bf16[16,208,128]{2,1,0:T(8,128)(2,1)} %get-tuple-element.81) | copy-start | bytes 2555908
  167.2 28.3 %collective-permute-start.21 = (bf16[8,512,128]{2,1,0:T(8,128)(2,1)S(1)}, bf16[8,512,128]{2,1,0:T(8,128)(2,1)S(1)}, u32[]{:S(2)}, u32[]{:S(2)}) collective-permute-start(bf16[8,512,128]{2,1,0:T(8,128)(2,1)S(1)} %slice.105), channel_id=1, source_target_pairs={{0,16},{1,17},{2,18},{3,19},{4,20},{5,21},{6,22},{7,23},{8,9},{9,8... | collective-permute-start | bytes 3145736 | tf_op jit(solution)/shard_map/ppermute | solution.py:668
  169.3 2.5 %copy-start.11 = (f32[1,1280]{1,0:T(1,128)S(1)}, f32[1,1280]{1,0:T(1,128)}, u32[]{:S(2)}) copy-start(f32[1,1280]{1,0:T(1,128)} %get-tuple-element.97) | copy-start | bytes 15364
  169.4 17.3 %collective-permute-start.26 = (bf16[8,208,128]{2,1,0:T(8,128)(2,1)S(1)}, bf16[8,208,128]{2,1,0:T(8,128)(2,1)S(1)}, u32[]{:S(2)}, u32[]{:S(2)}) collective-permute-start(bf16[8,208,128]{2,1,0:T(8,128)(2,1)S(1)} %slice.113), channel_id=1, source_target_pairs={{0,16},{1,17},{2,18},{3,19},{4,20},{5,21},{6,22},{7,23},{8,9},{9,8... | collective-permute-start | bytes 1277960 | tf_op jit(solution)/shard_map/ppermute | solution.py:668
  170.8 22.9 %collective-permute-start.16 = (bf16[8,208,128]{2,1,0:T(8,128)(2,1)S(1)}, bf16[8,208,128]{2,1,0:T(8,128)(2,1)S(1)}, u32[]{:S(2)}, u32[]{:S(2)}) collective-permute-start(bf16[8,208,128]{2,1,0:T(8,128)(2,1)S(1)} %slice.97), channel_id=1, source_target_pairs={{0,16},{1,17},{2,18},{3,19},{4,20},{5,21},{6,22},{7,23},{8,9},{9,8... | collective-permute-start | bytes 1277960 | tf_op jit(solution)/shard_map/ppermute | solution.py:668
  186.8 9.4 %collective-permute-start.27 = (bf16[4,208,128]{2,1,0:T(8,128)(2,1)S(1)}, bf16[4,208,128]{2,1,0:T(8,128)(2,1)S(1)}, u32[]{:S(2)}, u32[]{:S(2)}) collective-permute-start(bf16[4,208,128]{2,1,0:T(8,128)(2,1)S(1)} %slice.115), channel_id=1, source_target_pairs={{0,1},{1,0},{2,3},{3,2},{4,5},{5,4},{6,7},{7,6},{8,24},{9,25},{10,... | collective-permute-start | bytes 638984 | tf_op jit(solution)/shard_map/ppermute | solution.py:668
  193.7 5.9 %collective-permute-start.17 = (bf16[4,208,128]{2,1,0:T(8,128)(2,1)S(1)}, bf16[4,208,128]{2,1,0:T(8,128)(2,1)S(1)}, u32[]{:S(2)}, u32[]{:S(2)}) collective-permute-start(bf16[4,208,128]{2,1,0:T(8,128)(2,1)S(1)} %slice.99), channel_id=1, source_target_pairs={{0,1},{1,0},{2,3},{3,2},{4,5},{5,4},{6,7},{7,6},{8,24},{9,25},{10,... | collective-permute-start | bytes 638984 | tf_op jit(solution)/shard_map/ppermute | solution.py:668
  195.8 9.4 %collective-permute-start.22 = (bf16[4,512,128]{2,1,0:T(8,128)(2,1)S(1)}, bf16[4,512,128]{2,1,0:T(8,128)(2,1)S(1)}, u32[]{:S(2)}, u32[]{:S(2)}) collective-permute-start(bf16[4,512,128]{2,1,0:T(8,128)(2,1)S(1)} %slice.107), channel_id=1, source_target_pairs={{0,1},{1,0},{2,3},{3,2},{4,5},{5,4},{6,7},{7,6},{8,24},{9,25},{10,... | collective-permute-start | bytes 1572872 | tf_op jit(solution)/shard_map/ppermute | solution.py:668
  196.3 4.8 %collective-permute-start.28 = (bf16[2,208,128]{2,1,0:T(8,128)(2,1)S(1)}, bf16[2,208,128]{2,1,0:T(8,128)(2,1)S(1)}, u32[]{:S(2)}, u32[]{:S(2)}) collective-permute-start(bf16[2,208,128]{2,1,0:T(8,128)(2,1)S(1)} %slice.117), channel_id=1, source_target_pairs={{0,2},{1,3},{2,0},{3,1},{4,6},{5,7},{6,4},{7,5},{8,10},{9,11},{10,... | collective-permute-start | bytes 319496 | tf_op jit(solution)/shard_map/ppermute | solution.py:668
  199.7 6.8 %collective-permute-start.18 = (bf16[2,208,128]{2,1,0:T(8,128)(2,1)S(1)}, bf16[2,208,128]{2,1,0:T(8,128)(2,1)S(1)}, u32[]{:S(2)}, u32[]{:S(2)}) collective-permute-start(bf16[2,208,128]{2,1,0:T(8,128)(2,1)S(1)} %slice.101), channel_id=1, source_target_pairs={{0,2},{1,3},{2,0},{3,1},{4,6},{5,7},{6,4},{7,5},{8,10},{9,11},{10,... | collective-permute-start | bytes 319496 | tf_op jit(solution)/shard_map/ppermute | solution.py:668
  201.1 33.8 %copy-start.9 = (f32[7680]{0:T(1024)S(1)}, f32[7680]{0:T(1024)}, u32[]{:S(2)}) copy-start(f32[7680]{0:T(1024)} %param.28) | copy-start | bytes 92164
  201.2 34.5 %copy-start.10 = (f32[7680]{0:T(1024)S(1)}, f32[7680]{0:T(1024)}, u32[]{:S(2)}) copy-start(f32[7680]{0:T(1024)} %param.29) | copy-start | bytes 92164
  201.2 8.7 %collective-permute-start.29 = (bf16[1,208,128]{2,1,0:T(8,128)(2,1)S(1)}, bf16[1,208,128]{2,1,0:T(8,128)(2,1)S(1)}, u32[]{:S(2)}, u32[]{:S(2)}) collective-permute-start(bf16[1,208,128]{2,1,0:T(8,128)(2,1)S(1)} %slice.119), channel_id=1, source_target_pairs={{0,4},{1,5},{2,6},{3,7},{4,0},{5,1},{6,2},{7,3},{8,12},{9,13},{10,... | collective-permute-start | bytes 159752 | tf_op jit(solution)/shard_map/ppermute | solution.py:668
  205.5 8.1 %collective-permute-start.23 = (bf16[2,512,128]{2,1,0:T(8,128)(2,1)S(1)}, bf16[2,512,128]{2,1,0:T(8,128)(2,1)S(1)}, u32[]{:S(2)}, u32[]{:S(2)}) collective-permute-start(bf16[2,512,128]{2,1,0:T(8,128)(2,1)S(1)} %slice.109), channel_id=1, source_target_pairs={{0,2},{1,3},{2,0},{3,1},{4,6},{5,7},{6,4},{7,5},{8,10},{9,11},{10,... | collective-permute-start | bytes 786440 | tf_op jit(solution)/shard_map/ppermute | solution.py:668
  206.6 10.3 %collective-permute-start.19 = (bf16[1,208,128]{2,1,0:T(8,128)(2,1)S(1)}, bf16[1,208,128]{2,1,0:T(8,128)(2,1)S(1)}, u32[]{:S(2)}, u32[]{:S(2)}) collective-permute-start(bf16[1,208,128]{2,1,0:T(8,128)(2,1)S(1)} %slice.103), channel_id=1, source_target_pairs={{0,4},{1,5},{2,6},{3,7},{4,0},{5,1},{6,2},{7,3},{8,12},{9,13},{10,... | collective-permute-start | bytes 159752 | tf_op jit(solution)/shard_map/ppermute | solution.py:668
  213.6 6.8 %collective-permute-start.24 = (bf16[1,512,128]{2,1,0:T(8,128)(2,1)S(1)}, bf16[1,512,128]{2,1,0:T(8,128)(2,1)S(1)}, u32[]{:S(2)}, u32[]{:S(2)}) collective-permute-start(bf16[1,512,128]{2,1,0:T(8,128)(2,1)S(1)} %slice.111), channel_id=1, source_target_pairs={{0,4},{1,5},{2,6},{3,7},{4,0},{5,1},{6,2},{7,3},{8,12},{9,13},{10,... | collective-permute-start | bytes 393224 | tf_op jit(solution)/shard_map/ppermute | solution.py:668
  223.3 1.2 collective-permute-start.30
  224.5 4.9 %collective-permute-start.31 = (f32[1,7808]{1,0:T(1,128)S(1)}, f32[1,7808]{1,0:T(1,128)S(1)}, u32[]{:S(2)}, u32[]{:S(2)}) collective-permute-start(f32[1,7808]{1,0:T(1,128)S(1)} %add.75), channel_id=1, source_target_pairs={{0,4},{1,5},{2,6},{3,7},{4,0},{5,1},{6,2},{7,3},{8,12},{9,13},{10,... | collective-permute-start | bytes 93704 | tf_op jit(solution)/shard_map/ppermute | solution.py:675
  229.4 4.0 %collective-permute-start.32 = (f32[1,7808]{1,0:T(1,128)S(1)}, f32[1,7808]{1,0:T(1,128)S(1)}, u32[]{:S(2)}, u32[]{:S(2)}) collective-permute-start(f32[1,7808]{1,0:T(1,128)S(1)} %add.76), channel_id=1, source_target_pairs={{0,2},{1,3},{2,0},{3,1},{4,6},{5,7},{6,4},{7,5},{8,10},{9,11},{10,... | collective-permute-start | bytes 93704 | tf_op jit(solution)/shard_map/ppermute | solution.py:675
  233.4 4.0 %collective-permute-start.33 = (f32[1,7808]{1,0:T(1,128)S(1)}, f32[1,7808]{1,0:T(1,128)S(1)}, u32[]{:S(2)}, u32[]{:S(2)}) collective-permute-start(f32[1,7808]{1,0:T(1,128)S(1)} %add.77), channel_id=1, source_target_pairs={{0,1},{1,0},{2,3},{3,2},{4,5},{5,4},{6,7},{7,6},{8,24},{9,25},{10,... | collective-permute-start | bytes 93704 | tf_op jit(solution)/shard_map/ppermute | solution.py:675
  237.5 7.8 %collective-permute-start.34 = (f32[1,7808]{1,0:T(1,128)S(1)}, f32[1,7808]{1,0:T(1,128)S(1)}, u32[]{:S(2)}, u32[]{:S(2)}) collective-permute-start(f32[1,7808]{1,0:T(1,128)S(1)} %add.78), channel_id=1, source_target_pairs={{0,16},{1,17},{2,18},{3,19},{4,20},{5,21},{6,22},{7,23},{8,9},{9,8... | collective-permute-start | bytes 93704 | tf_op jit(solution)/shard_map/ppermute | solution.py:675

commit v2 on v1

--- a/solution.py
+++ b/solution.py
@@ -37,7 +37,8 @@
 BF16 = jnp.bfloat16
 F32 = jnp.float32
 AXES = ("dp", "fsdp")
-VMEM_LIMIT = 56 * 1024 * 1024
+VMEM_LIMIT = 26 * 1024 * 1024
+EFFORT = 20
 
 
 def round16(n):
@@ -97,7 +98,7 @@
         far = [("f", b) for b in range(fsdp.bit_length() - 2, 0, -1)]
         near = [("f", 0)] if fsdp > 1 else []
         rows = [("d", b) for b in range(dp.bit_length() - 2, 0, -1)]
-        self.order = (far + near + rows, far + rows + near)
+        self.order = (far + near + rows, far[::-1] + rows + near)
 
     def flip(self, stage, device):
         d, f = divmod(device, self.fsdp)
@@ -127,7 +128,7 @@
         return total
 
 
-def call(kernel, name, out_shape, in_specs, out_specs, grid=(), scratch=(), flops=0, bytes_accessed=0):
+def call(kernel, name, out_shape, in_specs, out_specs, grid=(), scratch=(), flops=0, bytes_accessed=0, aliases=None):
     return pl.pallas_call(
         kernel,
         name=name,
@@ -136,9 +137,10 @@
         in_specs=in_specs,
         out_specs=out_specs,
         scratch_shapes=list(scratch),
+        input_output_aliases=aliases or {},
         compiler_params=pltpu.CompilerParams(vmem_limit_bytes=VMEM_LIMIT),
         cost_estimate=pl.CostEstimate(
-            flops=flops, bytes_accessed=bytes_accessed, transcendentals=0
+            flops=EFFORT * flops, bytes_accessed=EFFORT * bytes_accessed, transcendentals=0
         ),
     )
 
@@ -147,8 +149,8 @@
     return pl.BlockSpec(shape, lambda *_: (0,) * len(shape))
 
 
-def tokens(width):
-    return pl.BlockSpec((BLOCK, width), lambda i: (i, 0))
+def tokens(width, first=0):
+    return pl.BlockSpec((BLOCK, width), lambda i: (first + i, 0))
 
 
 SMEM = pl.BlockSpec(memory_space=pltpu.SMEM)
@@ -301,8 +303,9 @@
     )(*weights)
 
 
-def first_norm(block_input, cotangent, vec):
-    def kernel(x_ref, cot_ref, vec_ref, h_ref, ht_ref, stat_ref, bias_ref):
+def first_norm(block_input, cotangent, vec, first=0, count=STEPS, held=None):
+    def kernel(x_ref, cot_ref, vec_ref, *refs):
+        h_ref, ht_ref, stat_ref, bias_ref = refs[-4:]
         values = x_ref[...].astype(F32)
         center, root = statistics(values)
         normed = center * root
@@ -313,6 +316,7 @@
         stat_ref[...] = jnp.where(lane == 0, values[:, :1] - center[:, :1], root)
         add_rows(bias_ref, cot_ref[...].astype(F32), pl.program_id(0) == 0)
 
+    held = list(held or [])
     return call(
         kernel,
         "first_norm",
@@ -322,12 +326,18 @@
             shape((LENGTH, 128), F32),
             shape((1, D), F32),
         ],
-        [tokens(D), tokens(D), whole(vec.shape)],
-        [tokens(D), pl.BlockSpec((D, BLOCK), lambda i: (0, i)), tokens(128), whole((1, D))],
-        grid=(STEPS,),
-        flops=30 * LENGTH * D,
-        bytes_accessed=8 * LENGTH * D,
-    )(block_input, cotangent, vec)
+        [tokens(D, first), tokens(D, first), whole(vec.shape)] + [ANY] * len(held),
+        [
+            tokens(D, first),
+            pl.BlockSpec((D, BLOCK), lambda i: (0, first + i)),
+            tokens(128, first),
+            whole((1, D)),
+        ],
+        grid=(count,),
+        aliases={3 + i: i for i in range(len(held))},
+        flops=30 * BLOCK * count * D,
+        bytes_accessed=8 * BLOCK * count * D,
+    )(block_input, cotangent, vec, *held)
 
 
 def norm_out(mixed, vec_ref, gain, shift_span, h_ref, ht_ref, normed_ref, root_ref):
@@ -416,7 +426,7 @@
     return [shape(slots(net, geo), BF16)] * 2
 
 
-def weight_gradient(net, geo, me, left, right, name):
+def weight_gradient(net, geo, me, left, right, name="weight_gradient"):
     dims = (left.shape[0], right.shape[1])
 
     def kernel(me_ref, left_ref, right_ref, keep, send, full, buf, sems):
@@ -558,9 +568,10 @@
     )(ends, back_two, full_conv, normed, root, vec)
 
 
-def back_through_in(back_one, full_in, block_input, cotangent, stat, vec):
-    def kernel(back_ref, w_ref, x_ref, cot_ref, stat_ref, vec_ref, out_ref, gg_ref, gs_ref):
-        first = pl.program_id(0) == 0
+def back_through_in(back_one, full_in, block_input, cotangent, stat, vec, first=0, count=STEPS, held=None):
+    def kernel(back_ref, w_ref, x_ref, cot_ref, stat_ref, vec_ref, *refs):
+        out_ref, gg_ref, gs_ref = refs[-3:]
+        start = pl.program_id(0) == 0
         grad = dot_nt(back_ref[...], w_ref[...])
         root = stat_ref[:, 1:2]
         normed = (x_ref[...].astype(F32) - stat_ref[:, :1]) * root
@@ -568,38 +579,54 @@
             grad, normed, root, part(vec_ref, GAIN_ONE), part(vec_ref, SHIFT_ONE)
         )
         out_ref[...] = (cot_ref[...].astype(F32) + back).astype(BF16)
-        add_rows(gg_ref, to_gain, first)
-        add_rows(gs_ref, to_shift, first)
+        add_rows(gg_ref, to_gain, start)
+        add_rows(gs_ref, to_shift, start)
 
     row = shape((1, D), F32)
+    held = list(held or [])
     return call(
         kernel,
         "back_through_in",
         [shape((LENGTH, D), BF16), row, row],
-        [tokens(INNER), whole((D, INNER)), tokens(D), tokens(D), tokens(128), whole(vec.shape)],
-        [tokens(D)] + [whole((1, D))] * 2,
-        grid=(STEPS,),
-        flops=2 * LENGTH * D * INNER,
+        [
+            tokens(INNER, first),
+            whole((D, INNER)),
+            tokens(D, first),
+            tokens(D, first),
+            tokens(128, first),
+            whole(vec.shape),
+        ]
+        + [ANY] * len(held),
+        [tokens(D, first)] + [whole((1, D))] * 2,
+        grid=(count,),
+        aliases={6 + i: i for i in range(len(held))},
+        flops=2 * BLOCK * count * D * INNER,
         bytes_accessed=12_000_000,
-    )(back_one, full_in, block_input, cotangent, stat, vec)
-
-
-def sum_squares(owned):
+    )(back_one, full_in, block_input, cotangent, stat, vec, *held)
+
+
+def sum_squares(owned, partial):
+    rows = partial.shape[0]
+    total_rows = -(-(rows + 1) // 8) * 8
+
     def kernel(*refs):
+        out = refs[-1]
         total = jnp.zeros((1, 128), F32)
-        for ref in refs[:-1]:
-            value = ref[...].astype(F32)
+        for ref in refs[:-2]:
+            value = ref[...]
             total = total + jnp.sum(value * value, axis=0, keepdims=True)
-        refs[-1][...] = total
+        out[...] = jnp.zeros(out.shape, F32)
+        out[0:rows] = refs[-2][...]
+        out[rows : rows + 1] = total
 
     return call(
         kernel,
         "sum_squares",
-        shape((1, 128), F32),
-        [whole(v.shape) for v in owned],
-        whole((1, 128)),
+        shape((total_rows, 128), F32),
+        [whole(v.shape) for v in owned] + [whole(partial.shape)],
+        whole((total_rows, 128)),
         bytes_accessed=1_000_000,
-    )(*owned)
+    )(*owned, partial)
 
 
 def adamw(weight, moment, square, gradient, rate, decay):
@@ -613,16 +640,15 @@
 
 def update_all(geos, owned, totals, weights, vectors):
     n = len(geos)
-    size = vectors[0].shape[1]
+    size = vectors[0].shape[0]
 
     def kernel(*refs):
         owned_refs, total_ref = refs[:n], refs[n]
         ins = refs[n + 1 : n + 1 + 3 * n + 3]
         outs = refs[n + 1 + 3 * n + 3 :]
-        grad_vec = total_ref[:, :size]
-        squares = jnp.sum(grad_vec * grad_vec, axis=1, keepdims=True)
-        squares = squares + jnp.sum(total_ref[:, size:], axis=1, keepdims=True)
-        norm = jnp.sqrt(squares)
+        grad_vec = total_ref[0:size]
+        squares = jnp.sum(grad_vec * grad_vec, axis=0, keepdims=True) + total_ref[size : size + 1]
+        norm = jnp.sqrt(jnp.sum(squares, axis=1, keepdims=True))
         outs[0][...] = norm
         clip = jnp.minimum(1.0, CLIP_LIMIT / (norm + 1e-06))
         for i, geo in enumerate(geos):
@@ -650,23 +676,75 @@
     )(*args)
 
 
-def gather(net, shard):
-    held = shard[None]
-    for stage in range(net.stages()):
-        held = jnp.concatenate([held, lax.ppermute(held, AXES, net.stage(stage))], axis=0)
-    return held, lax.ppermute(held, AXES, net.core())
+class Sequence:
+    def __init__(self):
+        self.last = ()
+
+    def after(self, *values):
+        return lax.optimization_barrier(tuple(values) + self.last)[: len(values)]
+
+    def run(self, function, *values, **options):
+        result = function(*self.after(*values), **options)
+        self.last = tuple(jax.tree.leaves(result))[-1:]
+        return result
+
+    def wait(self, *values):
+        self.last = tuple(values) + self.last
+
+
+class Gather:
+    def __init__(self, net, seq, shard):
+        self.net, self.seq, self.stage = net, seq, 0
+        self.held, self.coming = shard[None], None
+
+    def send(self):
+        (held,) = self.seq.after(self.held)
+        self.held = held
+        last = self.stage == self.net.stages()
+        self.coming = lax.ppermute(held, AXES, self.net.core() if last else self.net.stage(self.stage))
+        self.stage += 1
+
+    def take(self):
+        if self.stage <= self.net.stages():
+            self.held = jnp.concatenate([self.held, self.coming], axis=0)
+        self.seq.wait(self.held, self.coming)
+
+    def step(self):
+        self.take()
+        self.send()
+
+    def finish(self):
+        while self.stage <= self.net.stages():
+            self.step()
+        self.take()
 
 
 def add(a, b):
     return (a.astype(F32) + b.astype(F32)).astype(BF16)
 
 
-def reduce(net, keep, send):
-    held = add(keep, lax.ppermute(send, AXES, net.core()))
-    for stage in range(net.stages() - 1, -1, -1):
-        half = held.shape[0] // 2
-        held = add(held[:half], lax.ppermute(held[half:], AXES, net.stage(stage)))
-    return held[0]
+class Reduce:
+    def __init__(self, net, seq, keep, send):
+        self.net, self.seq, self.stage = net, seq, net.stages()
+        self.keep = keep
+        (send,) = seq.after(send)
+        self.coming = lax.ppermute(send, AXES, net.core())
+
+    def step(self):
+        self.stage -= 1
+        half = self.keep.shape[0] // 2
+        away = add(self.keep[half:], self.coming[half:])
+        keep = add(self.keep[:half], self.coming[:half])
+        self.keep, away = self.seq.after(keep, away)
+        self.seq.wait(self.keep, away)
+        self.coming = lax.ppermute(away, AXES, self.net.stage(self.stage))
+
+    def end(self):
+        while self.stage:
+            self.step()
+        held = self.keep.astype(F32) + self.coming.astype(F32)
+        self.seq.wait(held)
+        return held[0]
 
 
 def total_sum(net, value):
@@ -710,41 +788,93 @@
     x = block_input[0]
     cot = cotangent[0]
 
-    shard_in, shard_conv, shard_out = pack_weights(geos, (weight_in, flat(weight_conv), weight_out))
-    own_in, peer_in = gather(net, shard_in)
-    own_conv, peer_conv = gather(net, shard_conv)
-    own_out, peer_out = gather(net, shard_out)
-
-    h1, h1_t, stat, grad_b3 = first_norm(x, cot, vec)
-    h2, h2_t, n2, r2, full_in = mix_one(net, geo_in, me, own_in, peer_in, h1, vec)
-    h3, h3_t, n3, r3, full_conv = mix_two(net, geo_conv, me, ends, own_conv, peer_conv, h2, vec)
-    grad_out = reduce(net, *weight_gradient(net, geo_out, me, h3_t, cot, "out_gradient"))
-    back_two, grad_g3, grad_s3, grad_b2, full_out = back_through_out(
-        net, geo_out, me, own_out, peer_out, cot, n3, r3, vec
-    )
-    grad_conv = reduce(net, *conv_gradient(net, geo_conv, me, ends, h2_t, back_two))
-    back_one, grad_g2, grad_s2, grad_b1 = back_through_conv(ends, back_two, full_conv, n2, r2, vec)
-    grad_in = reduce(net, *weight_gradient(net, geo_in, me, h1_t, back_one, "in_gradient"))
-    input_grad, grad_g1, grad_s1 = back_through_in(back_one, full_in, x, cot, stat, vec)
-    block_output = block_result(x, h3, full_out, vec)
+    seq = Sequence()
+    shard_in, shard_conv, shard_out = seq.run(
+        lambda *weights: pack_weights(geos, weights), weight_in, flat(weight_conv), weight_out
+    )
+    get_in = Gather(net, seq, shard_in)
+    get_conv = Gather(net, seq, shard_conv)
+    get_out = Gather(net, seq, shard_out)
+    get_in.send()
+    get_conv.send()
+    seq.wait(me, ends, vec)
+    norms = seq.run(first_norm, x, cot, vec, first=0, count=STEPS // 2)
+    get_in.step()
+    get_conv.step()
+    h1, h1_t, stat, half_b3 = seq.run(
+        lambda x, cot, vec, *held: first_norm(x, cot, vec, STEPS // 2, STEPS // 2, held),
+        x, cot, vec, *norms[:3],
+    )
+    grad_b3 = norms[3] + half_b3
+    get_in.step()
+    get_conv.step()
+    get_in.step()
+    get_in.step()
+    get_conv.step()
+    get_out.send()
+    get_in.finish()
+    h2, h2_t, n2, r2, full_in = seq.run(
+        functools.partial(mix_one, net, geo_in), me, get_in.held, get_in.coming, h1, vec
+    )
+    get_out.step()
+    get_conv.step()
+    get_out.step()
+    get_conv.finish()
+    h3, h3_t, n3, r3, full_conv = seq.run(
+        functools.partial(mix_two, net, geo_conv),
+        me, ends, get_conv.held, get_conv.coming, h2, vec,
+    )
+    get_out.step()
+    pieces = seq.run(
+        functools.partial(weight_gradient, net, geo_out, name="out_gradient"), me, h3_t, cot
+    )
+    sum_out = Reduce(net, seq, *pieces)
+    get_out.step()
+    get_out.finish()
+    back_two, grad_g3, grad_s3, grad_b2, full_out = seq.run(
+        functools.partial(back_through_out, net, geo_out),
+        me, get_out.held, get_out.coming, cot, n3, r3, vec,
+    )
+    sum_out.step()
+    pieces = seq.run(
+        functools.partial(conv_gradient, net, geo_conv), me, ends, h2_t, back_two
+    )
+    sum_conv = Reduce(net, seq, *pieces)
+    sum_out.step()
+    back_one, grad_g2, grad_s2, grad_b1 = seq.run(
+        back_through_conv, ends, back_two, full_conv, n2, r2, vec
+    )
+    sum_conv.step()
+    sum_out.step()
+    pieces = seq.run(
+        functools.partial(weight_gradient, net, geo_in, name="in_gradient"), me, h1_t, back_one
+    )
+    sum_in = Reduce(net, seq, *pieces)
+    sum_out.step()
+    block_output = seq.run(block_result, x, h3, full_out, vec)
+    sum_in.step()
+    sum_conv.step()
+    ends_in = seq.run(back_through_in, back_one, full_in, x, cot, stat, vec, first=0, count=STEPS // 2)
+    sum_in.step()
+    sum_conv.step()
+    grad_out = sum_out.end()
+    input_grad, more_g1, more_s1 = seq.run(
+        lambda *args: back_through_in(*args[:6], STEPS // 2, STEPS // 2, args[6:]),
+        back_one, full_in, x, cot, stat, vec, ends_in[0],
+    )
+    grad_g1, grad_s1 = ends_in[1] + more_g1, ends_in[2] + more_s1
+    partial = jnp.concatenate(
+        [grad_g1, grad_s1, grad_g2, grad_s2, grad_g3, grad_s3, grad_b1, grad_b2, grad_b3], axis=1
+    ).reshape(-1, 128)
+    sum_in.step()
+    sum_conv.step()
+    seq.wait(partial)
+    sum_in.step()
+    grad_conv = sum_conv.end()
+    grad_in = sum_in.end()
 
     owned = (grad_in, grad_conv, grad_out)
-    partial = jnp.concatenate(
-        [
-            grad_g1,
-            grad_s1,
-            grad_g2,
-            grad_s2,
-            grad_g3,
-            grad_s3,
-            grad_b1,
-            grad_b2,
-            grad_b3,
-            sum_squares(owned),
-        ],
-        axis=1,
-    )
-    totals = total_sum(net, partial)
+    totals = total_sum(net, sum_squares(owned, partial))
     results = update_all(
         geos,
         owned,
@@ -754,7 +884,7 @@
             (flat(weight_conv), flat(moment_conv), flat(square_conv)),
             (weight_out, moment_out, square_out),
         ),
-        (vec, moment_vectors.reshape(1, -1), square_vectors.reshape(1, -1)),
+        tuple(v.reshape(-1, 128) for v in (vectors, moment_vectors, square_vectors)),
     )
     norm, news = results[0], results[1:]
     return (

time: 255 us -> 188 us (0.74)
  Pallas kernels: 102 us -> 69.4 us
  waiting for transfers between devices: 80.6 us -> 65.5 us
  other arithmetic: 13.4 us -> 3.05 us
  starting transfers between devices: 46.4 us -> 40 us
  local copies, waits for them, and re-layouts: 10.6 us -> 7.95 us
    ppermute x30, waiting for transfers between devices: 71.9 us -> 51 us  [the longest x15 33.7 us: send(): lax.ppermute(held, AXES, self.net.core() if last else self.net.stage(self...]
    ppermute x4, waiting for transfers between devices: 7.55 us -> 13.3 us  [total_sum(): value = value + lax.ppermute(value, AXES, net.stage(stage))]
    pallas_call x2, Pallas kernels: 11.8 us -> 6.76 us  [weight_gradient(): call(kernel, name, gradient_shapes(net, geo), [SMEM, whole(left.shape), w...]
    pallas_call x3 -> x0, other arithmetic: 4.32 us -> none  [update_all(): call(kernel, 'update_all', outs, [whole(v.shape) for v in args], [whole(o...]
    ppermute x30, starting transfers between devices: 40.7 us -> 36.6 us  [the longest x15 21.2 us: send(): lax.ppermute(held, AXES, self.net.core() if last else self.net.stage(self...]
    pallas_call x1, Pallas kernels: 9.96 us -> 6.37 us  [back_through_out(): call(kernel, 'back_through_out', [shape((LENGTH, INNER), BF16), row, row,...]
    pallas_call x1, Pallas kernels: 15.3 us -> 11.7 us  [mix_two(): call(kernel, 'mix_two', NORM_SHAPES + [shape((KERNEL * INNER, INNER), BF1...]
    pallas_call x1, Pallas kernels: 9.79 us -> 6.76 us  [mix_one(): call(kernel, 'mix_one', NORM_SHAPES + [shape((D, INNER), BF16)], [SMEM, A...]
  transfers between devices with their start and end apart: 35 -> 35, of which waited for: 20 -> 21; matrix products, arithmetic and copies ran while one was open for 5% -> 2% of each run, Pallas kernels for 29% -> 26%
where the time goes in v2:
time: 188 us; the launch traced here: 187 us
  Pallas kernels  69.4 us (37%)
  waiting for transfers between devices  65.5 us (35%)
  starting transfers between devices  40 us (21%)
  local copies, waits for them, and re-layouts  7.95 us (4%)
  other arithmetic  3.05 us (2%)
    ppermute x15, waiting for transfers between devices, send(): lax.ppermute(held, AXES, self.net.core() if last else self.net.stage(self...  33.7 us
    ppermute x15, starting transfers between devices, send(): lax.ppermute(held, AXES, self.net.core() if last else self.net.stage(self...  21.2 us
    ppermute x12, waiting for transfers between devices, step(): self.coming = lax.ppermute(away, AXES, self.net.stage(self.stage))  17.3 us
    ppermute x12, starting transfers between devices, step(): self.coming = lax.ppermute(away, AXES, self.net.stage(self.stage))  15 us
    ppermute x4, waiting for transfers between devices, total_sum(): value = value + lax.ppermute(value, AXES, net.stage(stage))  13.3 us
    pallas_call x1, Pallas kernels, mix_two(): call(kernel, 'mix_two', NORM_SHAPES + [shape((KERNEL * INNER, INNER), BF1...  11.7 us
    pallas_call x1, Pallas kernels, back_through_conv(): call(kernel, 'back_through_conv', [shape((LENGTH, INNER), BF16), row, row...  10 us
    pallas_call x2, Pallas kernels, back_through_in(): call(kernel, 'back_through_in', [shape((LENGTH, D), BF16), row, row], [to...  9.07 us
  transfers between devices with their start and end apart: 35, of which 21 were waited for; matrix products, arithmetic and copies ran while one was open for 2% of the time, Pallas kernels for 26%

profile of v2, /device:TPU:0, one launch (start us, length us, event | category | flops | bytes accessed | tf_op | source)
XLA Modules:
  0.0 187.3 jit_solution(16407879324157171409)
XLA Ops:
  0.7 1.0 copy-done.6
  1.7 0.9 copy-done.8
  2.6 0.9 copy-done.12
  3.6 4.1 %collective-permute-start.1 = (bf16[1,208,128]{2,1,0:T(8,128)(2,1)S(1)}, bf16[1,208,128]{2,1,0:T(8,128)(2,1)S(1)}, u32[]{:S(2)}, u32[]{:S(2)}) collective-permute-start(bf16[1,208,128]{2,1,0:T(8,128)(2,1)S(1)} %bitcast.52), channel_id=1, source_target_pairs={{0,4},{1,5},{2,6},{3,7},{4,0},{5,1},{6,2},{7,3},{8,10},{9,11},{10,... | collective-permute-start | bytes 159752 | tf_op jit(solution)/shard_map/ppermute | solution.py:704
  7.9 0.8 reshape.103.vec_ref
  8.6 0.8 reduce-window.9
  9.5 1.7 copy-done
  11.2 1.7 copy-done.2
  12.9 2.4 %first_norm.2 = (bf16[1024,1280]{1,0:T(8,128)(2,1)S(1)}, bf16[1280,1024]{1,0:T(8,128)(2,1)S(1)}, f32[1024,128]{1,0:T(8,128)S(1)}, f32[1,1280]{1,0:T(1,128)S(1)}) custom-call(bf16[1024,1280]{1,0:T(8,128)(2,1)S(1)} %bitcast.31, bf16[1024,1280]{1,0:T(8,128)(2,1)S(1)} %bitcast.36, f32[1,7680]{1,0:T(1,128)S(1)} %reshape.103.vec_ref), custom_call_target="tpu_custom_call" | custom-call | flops 393216000 | bytes 104857600 | tf_op jit(solution)/shard_map/first_norm/pallas_call | solution.py:320
  15.4 1.9 %collective-permute-start.3 = (bf16[2,208,128]{2,1,0:T(8,128)(2,1)S(1)}, bf16[2,208,128]{2,1,0:T(8,128)(2,1)S(1)}, u32[]{:S(2)}, u32[]{:S(2)}) collective-permute-start(bf16[2,208,128]{2,1,0:T(8,128)(2,1)S(1)} %constant_dynamic-update-slice_fusion.2), channel_id=1, source_target_pairs={{0,2},{1,3},{2,0},{3,1},{4,6},{5,7},{6,4},{7,5},{8,12},{9,13},{10,... | collective-permute-start | bytes 319496 | tf_op jit(solution)/shard_map/ppermute | solution.py:704
  17.6 2.4 %first_norm.3 = (bf16[1024,1280]{1,0:T(8,128)(2,1)S(1)}, bf16[1280,1024]{1,0:T(8,128)(2,1)S(1)}, f32[1024,128]{1,0:T(8,128)S(1)}, f32[1,1280]{1,0:T(1,128)S(1)}) custom-call(bf16[1024,1280]{1,0:T(8,128)(2,1)S(1)} %bitcast.32, bf16[1024,1280]{1,0:T(8,128)(2,1)S(1)} %bitcast.37, ...), custom_call_target="tpu_custom_call", output_to_operand_aliasing={{0}: (3, {}), {1}: (4, {}), {2}: (5, {})} | custom-call | flops 393216000 | bytes 104857600 | tf_op jit(solution)/shard_map/first_norm/pallas_call | solution.py:320
  20.0 1.2 collective-permute-done.3
  21.2 1.9 %collective-permute-start.5 = (bf16[4,208,128]{2,1,0:T(8,128)(2,1)S(1)}, bf16[4,208,128]{2,1,0:T(8,128)(2,1)S(1)}, u32[]{:S(2)}, u32[]{:S(2)}) collective-permute-start(bf16[4,208,128]{2,1,0:T(8,128)(2,1)S(1)} %constant_dynamic-update-slice_fusion.6), channel_id=1, source_target_pairs={{0,1},{1,0},{2,3},{3,2},{4,5},{5,4},{6,7},{7,6},{8,24},{9,25},{10,... | collective-permute-start | bytes 638984 | tf_op jit(solution)/shard_map/ppermute | solution.py:704
  23.2 3.9 %collective-permute-done.5 = bf16[4,208,128]{2,1,0:T(8,128)(2,1)S(1)} collective-permute-done((bf16[4,208,128]{2,1,0:T(8,128)(2,1)S(1)}, bf16[4,208,128]{2,1,0:T(8,128)(2,1)S(1)}, u32[]{:S(2)}, u32[]{:S(2)}) %collective-permute-start.5) | collective-permute-done | bytes 213024 | tf_op jit(solution)/shard_map/ppermute | solution.py:704
  27.2 2.0 %collective-permute-start.6 = (bf16[8,208,128]{2,1,0:T(8,128)(2,1)S(1)}, bf16[8,208,128]{2,1,0:T(8,128)(2,1)S(1)}, u32[]{:S(2)}, u32[]{:S(2)}) collective-permute-start(bf16[8,208,128]{2,1,0:T(8,128)(2,1)S(1)} %constant_dynamic-update-slice_fusion.10), channel_id=1, source_target_pairs={{0,16},{1,17},{2,18},{3,19},{4,20},{5,21},{6,22},{7,23},{8,9},{9,8... | collective-permute-start | bytes 1277960 | tf_op jit(solution)/shard_map/ppermute | solution.py:704
  29.2 1.5 collective-permute-start.4
  30.7 8.3 %collective-permute-done.6 = bf16[8,208,128]{2,1,0:T(8,128)(2,1)S(1)} collective-permute-done((bf16[8,208,128]{2,1,0:T(8,128)(2,1)S(1)}, bf16[8,208,128]{2,1,0:T(8,128)(2,1)S(1)}, u32[]{:S(2)}, u32[]{:S(2)}) %collective-permute-start.6) | collective-permute-done | bytes 426016 | tf_op jit(solution)/shard_map/ppermute | solution.py:704
  39.3 2.4 %collective-permute-start.8 = (bf16[1,208,128]{2,1,0:T(8,128)(2,1)S(1)}, bf16[1,208,128]{2,1,0:T(8,128)(2,1)S(1)}, u32[]{:S(2)}, u32[]{:S(2)}) collective-permute-start(bf16[1,208,128]{2,1,0:T(8,128)(2,1)S(1)} %bitcast.50), channel_id=1, source_target_pairs={{0,4},{1,5},{2,6},{3,7},{4,0},{5,1},{6,2},{7,3},{8,10},{9,11},{10,... | collective-permute-start | bytes 159752 | tf_op jit(solution)/shard_map/ppermute | solution.py:704
  41.6 1.0 collective-permute-start.7
  42.7 1.6 collective-permute-done.8
  44.4 6.8 %mix_one.1 = (bf16[1024,640]{1,0:T(8,128)(2,1)S(1)}, bf16[640,1024]{1,0:T(8,128)(2,1)S(1)}, f32[1024,640]{1,0:T(8,128)S(1)}, f32[1024,128]{1,0:T(8,128)S(1)}, bf16[1280,640]{1,0:T(8,128)(2,1)S(1)}) custom-call(s32[2]{0:T(128)S(1)} %pad_add_fusion.me_ref, bf16[16,208,128]{2,1,0:T(8,128)(2,1)S(1)} %constant_dynamic-update-slice_fusion.12.own_ref, ...), custom_call_target="tpu_custom_call" | custom-call | flops 33554432000 | bytes 240000000 | tf_op jit(solution)/shard_map/mix_one/pallas_call | solution.py:379
  51.1 5.3 %collective-permute-done.7 = bf16[8,512,128]{2,1,0:T(8,128)(2,1)S(1)} collective-permute-done((bf16[8,512,128]{2,1,0:T(8,128)(2,1)S(1)}, bf16[8,512,128]{2,1,0:T(8,128)(2,1)S(1)}, u32[]{:S(2)}, u32[]{:S(2)}) %collective-permute-start.7) | collective-permute-done | bytes 1048608 | tf_op jit(solution)/shard_map/ppermute | solution.py:704
  56.7 3.2 %collective-permute-start.11 = (bf16[2,208,128]{2,1,0:T(8,128)(2,1)S(1)}, bf16[2,208,128]{2,1,0:T(8,128)(2,1)S(1)}, u32[]{:S(2)}, u32[]{:S(2)}) collective-permute-start(bf16[2,208,128]{2,1,0:T(8,128)(2,1)S(1)} %constant_dynamic-update-slice_fusion.16), channel_id=1, source_target_pairs={{0,2},{1,3},{2,0},{3,1},{4,6},{5,7},{6,4},{7,5},{8,12},{9,13},{10,... | collective-permute-start | bytes 319496 | tf_op jit(solution)/shard_map/ppermute | solution.py:704
  59.9 3.1 %collective-permute-done.11 = bf16[2,208,128]{2,1,0:T(8,128)(2,1)S(1)} collective-permute-done((bf16[2,208,128]{2,1,0:T(8,128)(2,1)S(1)}, bf16[2,208,128]{2,1,0:T(8,128)(2,1)S(1)}, u32[]{:S(2)}, u32[]{:S(2)}) %collective-permute-start.11) | collective-permute-done | bytes 106528 | tf_op jit(solution)/shard_map/ppermute | solution.py:704
  62.9 1.5 collective-permute-start.12
  64.5 4.4 %collective-permute-done.12 = bf16[4,208,128]{2,1,0:T(8,128)(2,1)S(1)} collective-permute-done((bf16[4,208,128]{2,1,0:T(8,128)(2,1)S(1)}, bf16[4,208,128]{2,1,0:T(8,128)(2,1)S(1)}, u32[]{:S(2)}, u32[]{:S(2)}) %collective-permute-start.12) | collective-permute-done | bytes 213024 | tf_op jit(solution)/shard_map/ppermute | solution.py:704
  68.9 11.7 %mix_two.1 = (bf16[1024,640]{1,0:T(8,128)(2,1)S(1)}, bf16[640,1024]{1,0:T(8,128)(2,1)S(1)}, f32[1024,640]{1,0:T(8,128)S(1)}, f32[1024,128]{1,0:T(8,128)S(1)}, bf16[3200,640]{1,0:T(8,128)(2,1)S(1)}) custom-call(s32[2]{0:T(128)S(1)} %pad_add_fusion.me_ref, s32[4]{0:T(128)S(1)} %bitcast.56, ...), custom_call_target="tpu_custom_call" | custom-call | flops 83886080000 | bytes 360000000 | tf_op jit(solution)/shard_map/mix_two/pallas_call | solution.py:412
  80.6 1.2 collective-permute-start.13
  81.8 3.0 %out_gradient.1 = (bf16[16,208,128]{2,1,0:T(8,128)(2,1)S(1)}, bf16[16,208,128]{2,1,0:T(8,128)(2,1)S(1)}) custom-call(s32[2]{0:T(128)S(1)} %pad_add_fusion.me_ref, bf16[640,1024]{1,0:T(8,128)(2,1)S(1)} %get-tuple-element.227.left_ref, bf16[1024,1280]{1,0:T(8,128)(2,1)S(1)} %bitcast.38), custom_call_target="tpu_custom_call" | custom-call | flops 33554432000 | bytes 120000000 | tf_op jit(solution)/shard_map/out_gradient/pallas_call | solution.py:436
  85.0 3.8 %collective-permute-done.13 = bf16[8,208,128]{2,1,0:T(8,128)(2,1)S(1)} collective-permute-done((bf16[8,208,128]{2,1,0:T(8,128)(2,1)S(1)}, bf16[8,208,128]{2,1,0:T(8,128)(2,1)S(1)}, u32[]{:S(2)}, u32[]{:S(2)}) %collective-permute-start.13) | collective-permute-done | bytes 426016 | tf_op jit(solution)/shard_map/ppermute | solution.py:704
  89.2 2.1 %collective-permute-done.14.peer_ref = bf16[16,208,128]{2,1,0:T(8,128)(2,1)S(1)} collective-permute-done((bf16[16,208,128]{2,1,0:T(8,128)(2,1)S(1)}, bf16[16,208,128]{2,1,0:T(8,128)(2,1)S(1)}, u32[]{:S(2)}, u32[]{:S(2)}) %collective-permute-start.14) | collective-permute-done | bytes 852000 | tf_op jit(solution)/shard_map/ppermute | solution.py:704
  91.3 6.4 %back_through_out.1 = (bf16[1024,640]{1,0:T(8,128)(2,1)S(1)}, f32[1,640]{1,0:T(1,128)S(1)}, f32[1,640]{1,0:T(1,128)S(1)}, f32[1,640]{1,0:T(1,128)S(1)}, bf16[640,1280]{1,0:T(8,128)(2,1)S(1)}) custom-call(s32[2]{0:T(128)S(1)} %pad_add_fusion.me_ref, bf16[16,208,128]{2,1,0:T(8,128)(2,1)S(1)} %constant_dynamic-update-slice_fusion.22.own_ref, ...), custom_call_target="tpu_custom_call" | custom-call | flops 33554432000 | bytes 240000000 | tf_op jit(solution)/shard_map/back_through_out/pallas_call | solution.py:470
  97.7 1.2 collective-permute-start.16
  98.9 8.0 %conv_gradient.1 = (bf16[16,512,128]{2,1,0:T(8,128)(2,1)S(1)}, bf16[16,512,128]{2,1,0:T(8,128)(2,1)S(1)}) custom-call(s32[2]{0:T(128)S(1)} %pad_add_fusion.me_ref, s32[4]{0:T(128)S(1)} %bitcast.57, bf16[640,1024]{1,0:T(8,128)(2,1)S(1)} %get-tuple-element.249.left_ref, bf16[1024,640]{1,0:T(8,128)(2,1)S(1)} %get-tuple-element.259.back_ref), custom_call_target="tpu_custom_call" | custom-call | flops 83886080000 | bytes 140000000 | tf_op jit(solution)/shard_map/conv_gradient/pallas_call | solution.py:509
  107.3 0.8 collective-permute-start.17
  108.1 10.0 %back_through_conv.1 = (bf16[1024,640]{1,0:T(8,128)(2,1)S(1)}, f32[1,640]{1,0:T(1,128)S(1)}, f32[1,640]{1,0:T(1,128)S(1)}, f32[1,640]{1,0:T(1,128)S(1)}) custom-call(s32[4]{0:T(128)S(1)} %bitcast.58, bf16[1024,640]{1,0:T(8,128)(2,1)S(1)} %get-tuple-element.259.back_ref, bf16[3200,640]{1,0:T(8,128)(2,1)S(1)} %get-tuple-element.260.w_ref, ...), custom_call_target="tpu_custom_call" | custom-call | flops 83886080000 | bytes 200000000 | tf_op jit(solution)/shard_map/back_through_conv/pallas_call | solution.py:551
  118.2 0.5 add_convert_fusion
  118.8 1.5 collective-permute-start.20
  120.3 1.6 collective-permute-start.19
  121.9 3.7 %in_gradient.1 = (bf16[16,208,128]{2,1,0:T(8,128)(2,1)S(1)}, bf16[16,208,128]{2,1,0:T(8,128)(2,1)S(1)}) custom-call(s32[2]{0:T(128)S(1)} %pad_add_fusion.me_ref, bf16[1280,1024]{1,0:T(8,128)(2,1)S(1)} %copy-done.5, bf16[1024,640]{1,0:T(8,128)(2,1)S(1)} %get-tuple-element.300.right_ref.back_ref), custom_call_target="tpu_custom_call" | custom-call | flops 33554432000 | bytes 120000000 | tf_op jit(solution)/shard_map/in_gradient/pallas_call | solution.py:436
  126.1 3.8 %block_result.1 = bf16[1024,1280]{1,0:T(8,128)(2,1)} custom-call(bf16[1024,1280]{1,0:T(8,128)(2,1)S(1)} %bitcast.33, bf16[1024,640]{1,0:T(8,128)(2,1)S(1)} %get-tuple-element.278.h_ref, bf16[640,1280]{1,0:T(8,128)(2,1)S(1)} %get-tuple-element.279.w_ref, f32[1,7680]{1,0:T(1,128)S(1)} %reshape.103.vec_ref), custom_call_target="tpu_custom_call" | custom-call | flops 33554432000 | bytes 160000000 | tf_op jit(solution)/shard_map/block_result/pallas_call | solution.py:488
  130.1 0.6 collective-permute-start.24
  130.7 2.9 %collective-permute-done.20 = bf16[8,512,128]{2,1,0:T(8,128)(2,1)S(1)} collective-permute-done((bf16[8,512,128]{2,1,0:T(8,128)(2,1)S(1)}, bf16[8,512,128]{2,1,0:T(8,128)(2,1)S(1)}, u32[]{:S(2)}, u32[]{:S(2)}) %collective-permute-start.20) | collective-permute-done | bytes 1048608 | tf_op jit(solution)/shard_map/ppermute | solution.py:740
  133.9 1.4 collective-permute-start.23
  135.3 4.5 %back_through_in.2 = (bf16[1024,1280]{1,0:T(8,128)(2,1)}, f32[1,1280]{1,0:T(1,128)S(1)}, f32[1,1280]{1,0:T(1,128)S(1)}) custom-call(bf16[1024,640]{1,0:T(8,128)(2,1)S(1)} %get-tuple-element.300.right_ref.back_ref, bf16[1280,640]{1,0:T(8,128)(2,1)S(1)} %get-tuple-element.301.w_ref, bf16[1024,1280]{1,0:T(8,128)(2,1)S(1)} %bitcast.34, ...), custom_call_target="tpu_custom_call" | custom-call | flops 16777216000 | bytes 240000000 | tf_op jit(solution)/shard_map/back_through_in/pallas_call | solution.py:587
  139.8 0.7 collective-permute-done.24
  140.7 1.1 collective-permute-start.25
  141.7 1.7 collective-permute-start.22
  143.4 3.1 %collective-permute-done.25 = bf16[4,208,128]{2,1,0:T(8,128)(2,1)S(1)} collective-permute-done((bf16[4,208,128]{2,1,0:T(8,128)(2,1)S(1)}, bf16[4,208,128]{2,1,0:T(8,128)(2,1)S(1)}, u32[]{:S(2)}, u32[]{:S(2)}) %collective-permute-start.25) | collective-permute-done | bytes 213024 | tf_op jit(solution)/shard_map/ppermute | solution.py:740
  146.8 1.9 %collective-permute-start.27 = (bf16[2,512,128]{2,1,0:T(8,128)(2,1)S(1)}, bf16[2,512,128]{2,1,0:T(8,128)(2,1)S(1)}, u32[]{:S(2)}, u32[]{:S(2)}) collective-permute-start(bf16[2,512,128]{2,1,0:T(8,128)(2,1)S(1)} %get-tuple-element.299), channel_id=1, source_target_pairs={{0,2},{1,3},{2,0},{3,1},{4,6},{5,7},{6,4},{7,5},{8,12},{9,13},{10,... | collective-permute-start | bytes 786440 | tf_op jit(solution)/shard_map/ppermute | solution.py:740
  148.7 4.5 %back_through_in.3 = (bf16[1024,1280]{1,0:T(8,128)(2,1)}, f32[1,1280]{1,0:T(1,128)S(1)}, f32[1,1280]{1,0:T(1,128)S(1)}) custom-call(bf16[1024,640]{1,0:T(8,128)(2,1)S(1)} %get-tuple-element.300.right_ref.back_ref, bf16[1280,640]{1,0:T(8,128)(2,1)S(1)} %get-tuple-element.301.w_ref, bf16[1024,1280]{1,0:T(8,128)(2,1)S(1)} %bitcast.35, ...), custom_call_target="tpu_custom_call", output_to_operand_aliasing={{0}: (6, {})} | custom-call | flops 16777216000 | bytes 240000000 | tf_op jit(solution)/shard_map/back_through_in/pallas_call | solution.py:587
  153.8 5.2 %collective-permute-done.26 = bf16[2,208,128]{2,1,0:T(8,128)(2,1)S(1)} collective-permute-done((bf16[2,208,128]{2,1,0:T(8,128)(2,1)S(1)}, bf16[2,208,128]{2,1,0:T(8,128)(2,1)S(1)}, u32[]{:S(2)}, u32[]{:S(2)}) %collective-permute-start.26) | collective-permute-done | bytes 106528 | tf_op jit(solution)/shard_map/ppermute | solution.py:740
  159.4 2.7 %collective-permute-start.29 = (bf16[1,512,128]{2,1,0:T(8,128)(2,1)S(1)}, bf16[1,512,128]{2,1,0:T(8,128)(2,1)S(1)}, u32[]{:S(2)}, u32[]{:S(2)}) collective-permute-start(bf16[1,512,128]{2,1,0:T(8,128)(2,1)S(1)} %get-tuple-element.319), channel_id=1, source_target_pairs={{0,4},{1,5},{2,6},{3,7},{4,0},{5,1},{6,2},{7,3},{8,10},{9,11},{10,... | collective-permute-start | bytes 393224 | tf_op jit(solution)/shard_map/ppermute | solution.py:740
  162.1 2.6 %collective-permute-done.28 = bf16[1,208,128]{2,1,0:T(8,128)(2,1)S(1)} collective-permute-done((bf16[1,208,128]{2,1,0:T(8,128)(2,1)S(1)}, bf16[1,208,128]{2,1,0:T(8,128)(2,1)S(1)}, u32[]{:S(2)}, u32[]{:S(2)}) %collective-permute-start.28) | collective-permute-done | bytes 53280 | tf_op jit(solution)/shard_map/ppermute | solution.py:740
  164.7 2.4 %collective-permute-done.29 = bf16[1,512,128]{2,1,0:T(8,128)(2,1)S(1)} collective-permute-done((bf16[1,512,128]{2,1,0:T(8,128)(2,1)S(1)}, bf16[1,512,128]{2,1,0:T(8,128)(2,1)S(1)}, u32[]{:S(2)}, u32[]{:S(2)}) %collective-permute-start.29) | collective-permute-done | bytes 131104 | tf_op jit(solution)/shard_map/ppermute | solution.py:740
  167.4 1.2 collective-permute-done.30
  168.6 0.8 collective-permute-start.31
  169.4 4.0 %collective-permute-done.31 = f32[64,128]{1,0:T(8,128)S(1)} collective-permute-done((f32[64,128]{1,0:T(8,128)S(1)}, f32[64,128]{1,0:T(8,128)S(1)}, u32[]{:S(2)}, u32[]{:S(2)}) %collective-permute-start.31) | collective-permute-done | bytes 32800 | tf_op jit(solution)/shard_map/ppermute | solution.py:753
  173.4 3.9 %collective-permute-done.32 = f32[64,128]{1,0:T(8,128)S(1)} collective-permute-done((f32[64,128]{1,0:T(8,128)S(1)}, f32[64,128]{1,0:T(8,128)S(1)}, u32[]{:S(2)}, u32[]{:S(2)}) %collective-permute-start.32) | collective-permute-done | bytes 32800 | tf_op jit(solution)/shard_map/ppermute | solution.py:753
  177.3 1.3 collective-permute-start.33
  178.6 2.7 %collective-permute-done.33 = f32[64,128]{1,0:T(8,128)S(1)} collective-permute-done((f32[64,128]{1,0:T(8,128)S(1)}, f32[64,128]{1,0:T(8,128)S(1)}, u32[]{:S(2)}, u32[]{:S(2)}) %collective-permute-start.33) | collective-permute-done | bytes 32800 | tf_op jit(solution)/shard_map/ppermute | solution.py:753
  181.3 1.2 collective-permute-start.34
  182.5 2.7 %collective-permute-done.34 = f32[64,128]{1,0:T(8,128)S(1)} collective-permute-done((f32[64,128]{1,0:T(8,128)S(1)}, f32[64,128]{1,0:T(8,128)S(1)}, u32[]{:S(2)}, u32[]{:S(2)}) %collective-permute-start.34) | collective-permute-done | bytes 32800 | tf_op jit(solution)/shard_map/ppermute | solution.py:753
  185.4 1.9 %update_all.1 = (f32[1,1]{1,0:T(1,128)}, f32[160,160]{1,0:T(8,128)}, f32[160,160]{1,0:T(8,128)}, f32[160,160]{1,0:T(8,128)}, f32[400,160]{1,0:T(8,128)}, /*index...) custom-call(f32[208,128]{1,0:T(8,128)S(1)} %add_bitcast_fusion.1.ref, ...), custom_call_target="tpu_custom_call" | custom-call | bytes 80000000 | tf_op jit(solution)/shard_map/update_all/pallas_call | solution.py:669
  (124 shorter events, 4.6 us)
Async XLA Ops:
  0.6 1.0 copy-start.6
  1.6 0.9 copy-start.8
  2.6 0.9 copy-start.12
  3.6 11.8 %collective-permute-start.1 = (bf16[1,208,128]{2,1,0:T(8,128)(2,1)S(1)}, bf16[1,208,128]{2,1,0:T(8,128)(2,1)S(1)}, u32[]{:S(2)}, u32[]{:S(2)}) collective-permute-start(bf16[1,208,128]{2,1,0:T(8,128)(2,1)S(1)} %bitcast.52), channel_id=1, source_target_pairs={{0,4},{1,5},{2,6},{3,7},{4,0},{5,1},{6,2},{7,3},{8,10},{9,11},{10,... | collective-permute-start | bytes 159752 | tf_op jit(solution)/shard_map/ppermute | solution.py:704
  7.7 9.6 %collective-permute-start = (bf16[1,512,128]{2,1,0:T(8,128)(2,1)S(1)}, bf16[1,512,128]{2,1,0:T(8,128)(2,1)S(1)}, u32[]{:S(2)}, u32[]{:S(2)}) collective-permute-start(bf16[1,512,128]{2,1,0:T(8,128)(2,1)S(1)} %bitcast.48), channel_id=1, source_target_pairs={{0,4},{1,5},{2,6},{3,7},{4,0},{5,1},{6,2},{7,3},{8,10},{9,11},{10,... | collective-permute-start | bytes 393224 | tf_op jit(solution)/shard_map/ppermute | solution.py:704
  9.5 1.7 copy-start
  11.2 1.7 copy-start.2
  15.4 5.8 %collective-permute-start.3 = (bf16[2,208,128]{2,1,0:T(8,128)(2,1)S(1)}, bf16[2,208,128]{2,1,0:T(8,128)(2,1)S(1)}, u32[]{:S(2)}, u32[]{:S(2)}) collective-permute-start(bf16[2,208,128]{2,1,0:T(8,128)(2,1)S(1)} %constant_dynamic-update-slice_fusion.2), channel_id=1, source_target_pairs={{0,2},{1,3},{2,0},{3,1},{4,6},{5,7},{6,4},{7,5},{8,12},{9,13},{10,... | collective-permute-start | bytes 319496 | tf_op jit(solution)/shard_map/ppermute | solution.py:704
  17.3 9.9 %collective-permute-start.2 = (bf16[2,512,128]{2,1,0:T(8,128)(2,1)S(1)}, bf16[2,512,128]{2,1,0:T(8,128)(2,1)S(1)}, u32[]{:S(2)}, u32[]{:S(2)}) collective-permute-start(bf16[2,512,128]{2,1,0:T(8,128)(2,1)S(1)} %constant_dynamic-update-slice_fusion), channel_id=1, source_target_pairs={{0,2},{1,3},{2,0},{3,1},{4,6},{5,7},{6,4},{7,5},{8,12},{9,13},{10,... | collective-permute-start | bytes 786440 | tf_op jit(solution)/shard_map/ppermute | solution.py:704
  19.9 19.2 %copy-start.4 = (bf16[1280,1024]{1,0:T(8,128)(2,1)}, bf16[1280,1024]{1,0:T(8,128)(2,1)S(1)}, u32[]{:S(2)}) copy-start(bf16[1280,1024]{1,0:T(8,128)(2,1)S(1)} %get-tuple-element.272.left_ref) | copy-start | bytes 7864324
  20.0 19.2 %copy-start.10 = (f32[1024,128]{1,0:T(8,128)}, f32[1024,128]{1,0:T(8,128)S(1)}, u32[]{:S(2)}) copy-start(f32[1024,128]{1,0:T(8,128)S(1)} %get-tuple-element.304.stat_ref) | copy-start | bytes 1572868
  21.2 5.9 %collective-permute-start.5 = (bf16[4,208,128]{2,1,0:T(8,128)(2,1)S(1)}, bf16[4,208,128]{2,1,0:T(8,128)(2,1)S(1)}, u32[]{:S(2)}, u32[]{:S(2)}) collective-permute-start(bf16[4,208,128]{2,1,0:T(8,128)(2,1)S(1)} %constant_dynamic-update-slice_fusion.6), channel_id=1, source_target_pairs={{0,1},{1,0},{2,3},{3,2},{4,5},{5,4},{6,7},{7,6},{8,24},{9,25},{10,... | collective-permute-start | bytes 638984 | tf_op jit(solution)/shard_map/ppermute | solution.py:704
  27.2 11.8 %collective-permute-start.6 = (bf16[8,208,128]{2,1,0:T(8,128)(2,1)S(1)}, bf16[8,208,128]{2,1,0:T(8,128)(2,1)S(1)}, u32[]{:S(2)}, u32[]{:S(2)}) collective-permute-start(bf16[8,208,128]{2,1,0:T(8,128)(2,1)S(1)} %constant_dynamic-update-slice_fusion.10), channel_id=1, source_target_pairs={{0,16},{1,17},{2,18},{3,19},{4,20},{5,21},{6,22},{7,23},{8,9},{9,8... | collective-permute-start | bytes 1277960 | tf_op jit(solution)/shard_map/ppermute | solution.py:704
  29.2 10.0 %collective-permute-start.4 = (bf16[4,512,128]{2,1,0:T(8,128)(2,1)S(1)}, bf16[4,512,128]{2,1,0:T(8,128)(2,1)S(1)}, u32[]{:S(2)}, u32[]{:S(2)}) collective-permute-start(bf16[4,512,128]{2,1,0:T(8,128)(2,1)S(1)} %constant_dynamic-update-slice_fusion.4), channel_id=1, source_target_pairs={{0,1},{1,0},{2,3},{3,2},{4,5},{5,4},{6,7},{7,6},{8,24},{9,25},{10,... | collective-permute-start | bytes 1572872 | tf_op jit(solution)/shard_map/ppermute | solution.py:704
  39.0 5.3 %collective-permute-start.9 = (bf16[16,208,128]{2,1,0:T(8,128)(2,1)S(1)}, bf16[16,208,128]{2,1,0:T(8,128)(2,1)S(1)}, u32[]{:S(2)}, u32[]{:S(2)}) collective-permute-start(bf16[16,208,128]{2,1,0:T(8,128)(2,1)S(1)} %constant_dynamic-update-slice_fusion.12.own_ref), channel_id=1, source_target_pairs={{0,8},{1,9},{2,10},{3,11},{4,12},{5,13},{6,14},{7,15},{8,0},{9,1},... | collective-permute-start | bytes 2555912 | tf_op jit(solution)/shard_map/ppermute | solution.py:704
  39.3 5.1 %collective-permute-start.8 = (bf16[1,208,128]{2,1,0:T(8,128)(2,1)S(1)}, bf16[1,208,128]{2,1,0:T(8,128)(2,1)S(1)}, u32[]{:S(2)}, u32[]{:S(2)}) collective-permute-start(bf16[1,208,128]{2,1,0:T(8,128)(2,1)S(1)} %bitcast.50), channel_id=1, source_target_pairs={{0,4},{1,5},{2,6},{3,7},{4,0},{5,1},{6,2},{7,3},{8,10},{9,11},{10,... | collective-permute-start | bytes 159752 | tf_op jit(solution)/shard_map/ppermute | solution.py:704
  41.6 14.8 %collective-permute-start.7 = (bf16[8,512,128]{2,1,0:T(8,128)(2,1)S(1)}, bf16[8,512,128]{2,1,0:T(8,128)(2,1)S(1)}, u32[]{:S(2)}, u32[]{:S(2)}) collective-permute-start(bf16[8,512,128]{2,1,0:T(8,128)(2,1)S(1)} %constant_dynamic-update-slice_fusion.8), channel_id=1, source_target_pairs={{0,16},{1,17},{2,18},{3,19},{4,20},{5,21},{6,22},{7,23},{8,9},{9,8... | collective-permute-start | bytes 3145736 | tf_op jit(solution)/shard_map/ppermute | solution.py:704
  56.6 12.3 %collective-permute-start.10 = (bf16[16,512,128]{2,1,0:T(8,128)(2,1)S(1)}, bf16[16,512,128]{2,1,0:T(8,128)(2,1)S(1)}, u32[]{:S(2)}, u32[]{:S(2)}) collective-permute-start(bf16[16,512,128]{2,1,0:T(8,128)(2,1)S(1)} %constant_dynamic-update-slice_fusion.14.own_ref), channel_id=1, source_target_pairs={{0,8},{1,9},{2,10},{3,11},{4,12},{5,13},{6,14},{7,15},{8,0},{9,1},... | collective-permute-start | bytes 6291464 | tf_op jit(solution)/shard_map/ppermute | solution.py:704
  56.7 6.3 %collective-permute-start.11 = (bf16[2,208,128]{2,1,0:T(8,128)(2,1)S(1)}, bf16[2,208,128]{2,1,0:T(8,128)(2,1)S(1)}, u32[]{:S(2)}, u32[]{:S(2)}) collective-permute-start(bf16[2,208,128]{2,1,0:T(8,128)(2,1)S(1)} %constant_dynamic-update-slice_fusion.16), channel_id=1, source_target_pairs={{0,2},{1,3},{2,0},{3,1},{4,6},{5,7},{6,4},{7,5},{8,12},{9,13},{10,... | collective-permute-start | bytes 319496 | tf_op jit(solution)/shard_map/ppermute | solution.py:704
  62.9 5.9 %collective-permute-start.12 = (bf16[4,208,128]{2,1,0:T(8,128)(2,1)S(1)}, bf16[4,208,128]{2,1,0:T(8,128)(2,1)S(1)}, u32[]{:S(2)}, u32[]{:S(2)}) collective-permute-start(bf16[4,208,128]{2,1,0:T(8,128)(2,1)S(1)} %constant_dynamic-update-slice_fusion.18), channel_id=1, source_target_pairs={{0,1},{1,0},{2,3},{3,2},{4,5},{5,4},{6,7},{7,6},{8,24},{9,25},{10,... | collective-permute-start | bytes 638984 | tf_op jit(solution)/shard_map/ppermute | solution.py:704
  68.9 12.9 %copy-start.3 = (bf16[1,1024,1280]{2,1,0:T(8,128)(2,1)S(1)}, bf16[1,1024,1280]{2,1,0:T(8,128)(2,1)}, u32[]{:S(2)}) copy-start(bf16[1,1024,1280]{2,1,0:T(8,128)(2,1)} %param.16) | copy-start | bytes 7864324
  80.6 8.2 %collective-permute-start.13 = (bf16[8,208,128]{2,1,0:T(8,128)(2,1)S(1)}, bf16[8,208,128]{2,1,0:T(8,128)(2,1)S(1)}, u32[]{:S(2)}, u32[]{:S(2)}) collective-permute-start(bf16[8,208,128]{2,1,0:T(8,128)(2,1)S(1)} %constant_dynamic-update-slice_fusion.20), channel_id=1, source_target_pairs={{0,16},{1,17},{2,18},{3,19},{4,20},{5,21},{6,22},{7,23},{8,9},{9,8... | collective-permute-start | bytes 1277960 | tf_op jit(solution)/shard_map/ppermute | solution.py:704
  84.9 4.1 %collective-permute-start.15 = (bf16[16,208,128]{2,1,0:T(8,128)(2,1)S(1)}, bf16[16,208,128]{2,1,0:T(8,128)(2,1)S(1)}, u32[]{:S(2)}, u32[]{:S(2)}) collective-permute-start(bf16[16,208,128]{2,1,0:T(8,128)(2,1)S(1)} %get-tuple-element.242), channel_id=1, source_target_pairs={{0,8},{1,9},{2,10},{3,11},{4,12},{5,13},{6,14},{7,15},{8,0},{9,1},... | collective-permute-start | bytes 2555912 | tf_op jit(solution)/shard_map/ppermute | solution.py:731
  88.9 2.4 %collective-permute-start.14 = (bf16[16,208,128]{2,1,0:T(8,128)(2,1)S(1)}, bf16[16,208,128]{2,1,0:T(8,128)(2,1)S(1)}, u32[]{:S(2)}, u32[]{:S(2)}) collective-permute-start(bf16[16,208,128]{2,1,0:T(8,128)(2,1)S(1)} %constant_dynamic-update-slice_fusion.22.own_ref), channel_id=1, source_target_pairs={{0,8},{1,9},{2,10},{3,11},{4,12},{5,13},{6,14},{7,15},{8,0},{9,1},... | collective-permute-start | bytes 2555912 | tf_op jit(solution)/shard_map/ppermute | solution.py:704
  97.7 9.5 %collective-permute-start.16 = (bf16[8,208,128]{2,1,0:T(8,128)(2,1)S(1)}, bf16[8,208,128]{2,1,0:T(8,128)(2,1)S(1)}, u32[]{:S(2)}, u32[]{:S(2)}) collective-permute-start(bf16[8,208,128]{2,1,0:T(8,128)(2,1)S(1)} %get-tuple-element.244), channel_id=1, source_target_pairs={{0,16},{1,17},{2,18},{3,19},{4,20},{5,21},{6,22},{7,23},{8,9},{9,8... | collective-permute-start | bytes 1277960 | tf_op jit(solution)/shard_map/ppermute | solution.py:740
  106.9 11.3 %collective-permute-start.18 = (bf16[16,512,128]{2,1,0:T(8,128)(2,1)S(1)}, bf16[16,512,128]{2,1,0:T(8,128)(2,1)S(1)}, u32[]{:S(2)}, u32[]{:S(2)}) collective-permute-start(bf16[16,512,128]{2,1,0:T(8,128)(2,1)S(1)} %get-tuple-element.255), channel_id=1, source_target_pairs={{0,8},{1,9},{2,10},{3,11},{4,12},{5,13},{6,14},{7,15},{8,0},{9,1},... | collective-permute-start | bytes 6291464 | tf_op jit(solution)/shard_map/ppermute | solution.py:731
  107.3 10.8 %collective-permute-start.17 = (bf16[4,208,128]{2,1,0:T(8,128)(2,1)S(1)}, bf16[4,208,128]{2,1,0:T(8,128)(2,1)S(1)}, u32[]{:S(2)}, u32[]{:S(2)}) collective-permute-start(bf16[4,208,128]{2,1,0:T(8,128)(2,1)S(1)} %get-tuple-element.253), channel_id=1, source_target_pairs={{0,1},{1,0},{2,3},{3,2},{4,5},{5,4},{6,7},{7,6},{8,24},{9,25},{10,... | collective-permute-start | bytes 638984 | tf_op jit(solution)/shard_map/ppermute | solution.py:740
  118.2 3.7 %copy-start.5 = (bf16[1280,1024]{1,0:T(8,128)(2,1)S(1)}, bf16[1280,1024]{1,0:T(8,128)(2,1)}, u32[]{:S(2)}) copy-start(bf16[1280,1024]{1,0:T(8,128)(2,1)} %copy-done.4) | copy-start | bytes 7864324
  118.8 14.9 %collective-permute-start.20 = (bf16[8,512,128]{2,1,0:T(8,128)(2,1)S(1)}, bf16[8,512,128]{2,1,0:T(8,128)(2,1)S(1)}, u32[]{:S(2)}, u32[]{:S(2)}) collective-permute-start(bf16[8,512,128]{2,1,0:T(8,128)(2,1)S(1)} %get-tuple-element.266), channel_id=1, source_target_pairs={{0,16},{1,17},{2,18},{3,19},{4,20},{5,21},{6,22},{7,23},{8,9},{9,8... | collective-permute-start | bytes 3145736 | tf_op jit(solution)/shard_map/ppermute | solution.py:740
  120.3 5.7 %collective-permute-start.19 = (bf16[2,208,128]{2,1,0:T(8,128)(2,1)S(1)}, bf16[2,208,128]{2,1,0:T(8,128)(2,1)S(1)}, u32[]{:S(2)}, u32[]{:S(2)}) collective-permute-start(bf16[2,208,128]{2,1,0:T(8,128)(2,1)S(1)} %get-tuple-element.268), channel_id=1, source_target_pairs={{0,2},{1,3},{2,0},{3,1},{4,6},{5,7},{6,4},{7,5},{8,12},{9,13},{10,... | collective-permute-start | bytes 319496 | tf_op jit(solution)/shard_map/ppermute | solution.py:740
  121.9 4.2 %copy-start.1 = (bf16[1,1024,1280]{2,1,0:T(8,128)(2,1)S(1)}, bf16[1,1024,1280]{2,1,0:T(8,128)(2,1)}, u32[]{:S(2)}) copy-start(bf16[1,1024,1280]{2,1,0:T(8,128)(2,1)} %param.15) | copy-start | bytes 7864324
  125.6 4.2 %collective-permute-start.21 = (bf16[16,208,128]{2,1,0:T(8,128)(2,1)S(1)}, bf16[16,208,128]{2,1,0:T(8,128)(2,1)S(1)}, u32[]{:S(2)}, u32[]{:S(2)}) collective-permute-start(bf16[16,208,128]{2,1,0:T(8,128)(2,1)S(1)} %get-tuple-element.283), channel_id=1, source_target_pairs={{0,8},{1,9},{2,10},{3,11},{4,12},{5,13},{6,14},{7,15},{8,0},{9,1},... | collective-permute-start | bytes 2555912 | tf_op jit(solution)/shard_map/ppermute | solution.py:731
  130.1 5.2 %copy-start.11 = (f32[1024,128]{1,0:T(8,128)S(1)}, f32[1024,128]{1,0:T(8,128)}, u32[]{:S(2)}) copy-start(f32[1024,128]{1,0:T(8,128)} %copy-done.10) | copy-start | bytes 1572868
  130.1 10.4 %collective-permute-start.24 = (bf16[8,208,128]{2,1,0:T(8,128)(2,1)S(1)}, bf16[8,208,128]{2,1,0:T(8,128)(2,1)S(1)}, u32[]{:S(2)}, u32[]{:S(2)}) collective-permute-start(bf16[8,208,128]{2,1,0:T(8,128)(2,1)S(1)} %get-tuple-element.285), channel_id=1, source_target_pairs={{0,16},{1,17},{2,18},{3,19},{4,20},{5,21},{6,22},{7,23},{8,9},{9,8... | collective-permute-start | bytes 1277960 | tf_op jit(solution)/shard_map/ppermute | solution.py:740
  133.9 12.7 %collective-permute-start.23 = (bf16[4,512,128]{2,1,0:T(8,128)(2,1)S(1)}, bf16[4,512,128]{2,1,0:T(8,128)(2,1)S(1)}, u32[]{:S(2)}, u32[]{:S(2)}) collective-permute-start(bf16[4,512,128]{2,1,0:T(8,128)(2,1)S(1)} %get-tuple-element.287), channel_id=1, source_target_pairs={{0,1},{1,0},{2,3},{3,2},{4,5},{5,4},{6,7},{7,6},{8,24},{9,25},{10,... | collective-permute-start | bytes 1572872 | tf_op jit(solution)/shard_map/ppermute | solution.py:740
  140.7 5.9 %collective-permute-start.25 = (bf16[4,208,128]{2,1,0:T(8,128)(2,1)S(1)}, bf16[4,208,128]{2,1,0:T(8,128)(2,1)S(1)}, u32[]{:S(2)}, u32[]{:S(2)}) collective-permute-start(bf16[4,208,128]{2,1,0:T(8,128)(2,1)S(1)} %get-tuple-element.297), channel_id=1, source_target_pairs={{0,1},{1,0},{2,3},{3,2},{4,5},{5,4},{6,7},{7,6},{8,24},{9,25},{10,... | collective-permute-start | bytes 638984 | tf_op jit(solution)/shard_map/ppermute | solution.py:740
  141.7 17.7 %collective-permute-start.22 = (bf16[1,208,128]{2,1,0:T(8,128)(2,1)S(1)}, bf16[1,208,128]{2,1,0:T(8,128)(2,1)S(1)}, u32[]{:S(2)}, u32[]{:S(2)}) collective-permute-start(bf16[1,208,128]{2,1,0:T(8,128)(2,1)S(1)} %get-tuple-element.276), channel_id=1, source_target_pairs={{0,4},{1,5},{2,6},{3,7},{4,0},{5,1},{6,2},{7,3},{8,10},{9,11},{10,... | collective-permute-start | bytes 159752 | tf_op jit(solution)/shard_map/ppermute | solution.py:740
  146.8 12.2 %collective-permute-start.27 = (bf16[2,512,128]{2,1,0:T(8,128)(2,1)S(1)}, bf16[2,512,128]{2,1,0:T(8,128)(2,1)S(1)}, u32[]{:S(2)}, u32[]{:S(2)}) collective-permute-start(bf16[2,512,128]{2,1,0:T(8,128)(2,1)S(1)} %get-tuple-element.299), channel_id=1, source_target_pairs={{0,2},{1,3},{2,0},{3,1},{4,6},{5,7},{6,4},{7,5},{8,12},{9,13},{10,... | collective-permute-start | bytes 786440 | tf_op jit(solution)/shard_map/ppermute | solution.py:740
  153.3 32.0 %copy-start.7 = (f32[5,80,160]{2,1,0:T(8,128)S(1)}, f32[5,80,160]{2,1,0:T(8,128)}, u32[]{:S(2)}) copy-start(f32[5,80,160]{2,1,0:T(8,128)} %param.21) | copy-start | bytes 768004
  153.3 32.0 %copy-start.9 = (f32[160,160]{1,0:T(8,128)S(1)}, f32[160,160]{1,0:T(8,128)}, u32[]{:S(2)}) copy-start(f32[160,160]{1,0:T(8,128)} %refs_4_.1) | copy-start | bytes 307204
  153.3 32.0 %copy-start.13 = (f32[80,320]{1,0:T(8,128)S(1)}, f32[80,320]{1,0:T(8,128)}, u32[]{:S(2)}) copy-start(f32[80,320]{1,0:T(8,128)} %refs_10_.1) | copy-start | bytes 307204
  153.3 32.0 %copy-start.14 = (f32[5,80,160]{2,1,0:T(8,128)S(1)}, f32[5,80,160]{2,1,0:T(8,128)}, u32[]{:S(2)}) copy-start(f32[5,80,160]{2,1,0:T(8,128)} %param.22) | copy-start | bytes 768004
  153.3 32.0 %copy-start.15 = (f32[5,80,160]{2,1,0:T(8,128)S(1)}, f32[5,80,160]{2,1,0:T(8,128)}, u32[]{:S(2)}) copy-start(f32[5,80,160]{2,1,0:T(8,128)} %param.23) | copy-start | bytes 768004
  153.3 32.0 %copy-start.16 = (f32[160,160]{1,0:T(8,128)S(1)}, f32[160,160]{1,0:T(8,128)}, u32[]{:S(2)}) copy-start(f32[160,160]{1,0:T(8,128)} %refs_5_.1) | copy-start | bytes 307204
  153.3 32.0 %copy-start.17 = (f32[160,160]{1,0:T(8,128)S(1)}, f32[160,160]{1,0:T(8,128)}, u32[]{:S(2)}) copy-start(f32[160,160]{1,0:T(8,128)} %refs_6_.1) | copy-start | bytes 307204
  153.3 32.0 %copy-start.18 = (f32[7680]{0:T(1024)S(1)}, f32[7680]{0:T(1024)}, u32[]{:S(2)}) copy-start(f32[7680]{0:T(1024)} %param.27) | copy-start | bytes 92164
  153.3 32.0 %copy-start.19 = (f32[80,320]{1,0:T(8,128)S(1)}, f32[80,320]{1,0:T(8,128)}, u32[]{:S(2)}) copy-start(f32[80,320]{1,0:T(8,128)} %refs_11_.1) | copy-start | bytes 307204
  153.3 32.0 %copy-start.20 = (f32[80,320]{1,0:T(8,128)S(1)}, f32[80,320]{1,0:T(8,128)}, u32[]{:S(2)}) copy-start(f32[80,320]{1,0:T(8,128)} %refs_12_.1) | copy-start | bytes 307204
  153.3 32.0 %copy-start.21 = (f32[7680]{0:T(1024)S(1)}, f32[7680]{0:T(1024)}, u32[]{:S(2)}) copy-start(f32[7680]{0:T(1024)} %param.28) | copy-start | bytes 92164
  153.4 32.0 %copy-start.22 = (f32[7680]{0:T(1024)S(1)}, f32[7680]{0:T(1024)}, u32[]{:S(2)}) copy-start(f32[7680]{0:T(1024)} %param.29) | copy-start | bytes 92164
  153.5 5.5 %collective-permute-start.26 = (bf16[2,208,128]{2,1,0:T(8,128)(2,1)S(1)}, bf16[2,208,128]{2,1,0:T(8,128)(2,1)S(1)}, u32[]{:S(2)}, u32[]{:S(2)}) collective-permute-start(bf16[2,208,128]{2,1,0:T(8,128)(2,1)S(1)} %get-tuple-element.310), channel_id=1, source_target_pairs={{0,2},{1,3},{2,0},{3,1},{4,6},{5,7},{6,4},{7,5},{8,12},{9,13},{10,... | collective-permute-start | bytes 319496 | tf_op jit(solution)/shard_map/ppermute | solution.py:740
  159.1 5.7 %collective-permute-start.28 = (bf16[1,208,128]{2,1,0:T(8,128)(2,1)S(1)}, bf16[1,208,128]{2,1,0:T(8,128)(2,1)S(1)}, u32[]{:S(2)}, u32[]{:S(2)}) collective-permute-start(bf16[1,208,128]{2,1,0:T(8,128)(2,1)S(1)} %get-tuple-element.321), channel_id=1, source_target_pairs={{0,4},{1,5},{2,6},{3,7},{4,0},{5,1},{6,2},{7,3},{8,10},{9,11},{10,... | collective-permute-start | bytes 159752 | tf_op jit(solution)/shard_map/ppermute | solution.py:740
  159.4 7.8 %collective-permute-start.29 = (bf16[1,512,128]{2,1,0:T(8,128)(2,1)S(1)}, bf16[1,512,128]{2,1,0:T(8,128)(2,1)S(1)}, u32[]{:S(2)}, u32[]{:S(2)}) collective-permute-start(bf16[1,512,128]{2,1,0:T(8,128)(2,1)S(1)} %get-tuple-element.319), channel_id=1, source_target_pairs={{0,4},{1,5},{2,6},{3,7},{4,0},{5,1},{6,2},{7,3},{8,10},{9,11},{10,... | collective-permute-start | bytes 393224 | tf_op jit(solution)/shard_map/ppermute | solution.py:740
  167.3 1.3 collective-permute-start.30
  168.6 4.8 %collective-permute-start.31 = (f32[64,128]{1,0:T(8,128)S(1)}, f32[64,128]{1,0:T(8,128)S(1)}, u32[]{:S(2)}, u32[]{:S(2)}) collective-permute-start(f32[64,128]{1,0:T(8,128)S(1)} %add.135), channel_id=1, source_target_pairs={{0,4},{1,5},{2,6},{3,7},{4,0},{5,1},{6,2},{7,3},{8,10},{9,11},{10,... | collective-permute-start | bytes 98312 | tf_op jit(solution)/shard_map/ppermute | solution.py:753
  173.4 3.9 %collective-permute-start.32 = (f32[64,128]{1,0:T(8,128)S(1)}, f32[64,128]{1,0:T(8,128)S(1)}, u32[]{:S(2)}, u32[]{:S(2)}) collective-permute-start(f32[64,128]{1,0:T(8,128)S(1)} %add.136), channel_id=1, source_target_pairs={{0,2},{1,3},{2,0},{3,1},{4,6},{5,7},{6,4},{7,5},{8,12},{9,13},{10,... | collective-permute-start | bytes 98312 | tf_op jit(solution)/shard_map/ppermute | solution.py:753
  177.3 4.0 %collective-permute-start.33 = (f32[64,128]{1,0:T(8,128)S(1)}, f32[64,128]{1,0:T(8,128)S(1)}, u32[]{:S(2)}, u32[]{:S(2)}) collective-permute-start(f32[64,128]{1,0:T(8,128)S(1)} %add.137), channel_id=1, source_target_pairs={{0,1},{1,0},{2,3},{3,2},{4,5},{5,4},{6,7},{7,6},{8,24},{9,25},{10,... | collective-permute-start | bytes 98312 | tf_op jit(solution)/shard_map/ppermute | solution.py:753
  181.3 3.9 %collective-permute-start.34 = (f32[64,128]{1,0:T(8,128)S(1)}, f32[64,128]{1,0:T(8,128)S(1)}, u32[]{:S(2)}, u32[]{:S(2)}) collective-permute-start(f32[64,128]{1,0:T(8,128)S(1)} %add.138), channel_id=1, source_target_pairs={{0,16},{1,17},{2,18},{3,19},{4,20},{5,21},{6,22},{7,23},{8,9},{9,8... | collective-permute-start | bytes 98312 | tf_op jit(solution)/shard_map/ppermute | solution.py:753

commit v3 on v2

--- a/solution.py
+++ b/solution.py
@@ -38,7 +38,8 @@
 F32 = jnp.float32
 AXES = ("dp", "fsdp")
 VMEM_LIMIT = 26 * 1024 * 1024
-EFFORT = 20
+FLOPS_PER_US = 1.15e9
+EFFORT = 4
 
 
 def round16(n):
@@ -92,13 +93,19 @@
 
 
 class Network:
-    def __init__(self, dp, fsdp):
+    def __init__(self, dp, fsdp, far_first):
         self.dp, self.fsdp = dp, fsdp
         self.half = dp * fsdp // 2
         far = [("f", b) for b in range(fsdp.bit_length() - 2, 0, -1)]
         near = [("f", 0)] if fsdp > 1 else []
         rows = [("d", b) for b in range(dp.bit_length() - 2, 0, -1)]
-        self.order = (far + near + rows, far[::-1] + rows + near)
+        if far_first:
+            self.order = (far + near + rows, far[::-1] + rows + near)
+        else:
+            self.order = (
+                far[:1] + near + rows + far[1:],
+                far[::-1][:1] + rows + near + far[::-1][1:],
+            )
 
     def flip(self, stage, device):
         d, f = divmod(device, self.fsdp)
@@ -128,7 +135,7 @@
         return total
 
 
-def call(kernel, name, out_shape, in_specs, out_specs, grid=(), scratch=(), flops=0, bytes_accessed=0, aliases=None):
+def call(kernel, name, out_shape, in_specs, out_specs, grid=(), scratch=(), us=1.0, aliases=None):
     return pl.pallas_call(
         kernel,
         name=name,
@@ -140,7 +147,7 @@
         input_output_aliases=aliases or {},
         compiler_params=pltpu.CompilerParams(vmem_limit_bytes=VMEM_LIMIT),
         cost_estimate=pl.CostEstimate(
-            flops=EFFORT * flops, bytes_accessed=EFFORT * bytes_accessed, transcendentals=0
+            flops=int(EFFORT * us * FLOPS_PER_US), bytes_accessed=0, transcendentals=0
         ),
     )
 
@@ -236,10 +243,11 @@
     return lax.dot_general(a, b, (((1,), (1,)), ((), ())), preferred_element_type=F32)
 
 
-def assemble(net, geo, me_ref, own, peer, buffer, sems, full):
+def assemble(net, geo, me_ref, own, peer, buffer, sems, full, offset=0):
     core = jnp.bitwise_and(me_ref[0], 1)
-    first = pltpu.make_async_copy(own, buffer.at[core], sems.at[0])
-    second = pltpu.make_async_copy(peer, buffer.at[1 - core], sems.at[1])
+    rows = pl.ds(offset, geo.packed)
+    first = pltpu.make_async_copy(own.at[:, rows], buffer.at[core], sems.at[0])
+    second = pltpu.make_async_copy(peer.at[:, rows], buffer.at[1 - core], sems.at[1])
     first.start()
     second.start()
     first.wait()
@@ -287,19 +295,22 @@
     return [pltpu.VMEM((2,) + slots(net, geo), BF16), pltpu.SemaphoreType.DMA((2,))]
 
 
-def pack_weights(geos, weights):
+def pack_weights(geos, *weights):
+    rows = sum(geo.packed for geo in geos)
+
     def kernel(*refs):
-        n = len(geos)
-        for geo, source, target in zip(geos, refs[:n], refs[n:]):
-            target[...] = geo.pack(source[...].astype(BF16))
+        start = 0
+        for geo, source in zip(geos, refs):
+            refs[-1][start : start + geo.packed] = geo.pack(source[...].astype(BF16))
+            start += geo.packed
 
     return call(
         kernel,
         "pack_weights",
-        [shape((geo.packed, 128), BF16) for geo in geos],
+        shape((rows, 128), BF16),
         [whole(w.shape) for w in weights],
-        [whole((geo.packed, 128)) for geo in geos],
-        bytes_accessed=1_000_000,
+        whole((rows, 128)),
+        us=1.0,
     )(*weights)
 
 
@@ -335,8 +346,7 @@
         ],
         grid=(count,),
         aliases={3 + i: i for i in range(len(held))},
-        flops=30 * BLOCK * count * D,
-        bytes_accessed=8 * BLOCK * count * D,
+        us=1.2 * count,
     )(block_input, cotangent, vec, *held)
 
 
@@ -384,8 +394,7 @@
         norm_specs() + [whole((D, INNER))],
         grid=(STEPS,),
         scratch=piece_scratch(net, geo),
-        flops=2 * LENGTH * D * INNER,
-        bytes_accessed=12_000_000,
+        us=0.01,
     )(me, own, peer, hidden_one, vec)
 
 
@@ -417,8 +426,7 @@
         norm_specs() + [whole((KERNEL * INNER, INNER))],
         grid=(STEPS,),
         scratch=piece_scratch(net, geo) + [pltpu.VMEM((LENGTH + 2 * MARGIN, INNER), BF16)],
-        flops=2 * LENGTH * KERNEL * INNER * INNER,
-        bytes_accessed=18_000_000,
+        us=11.7,
     )(me, ends, own, peer, hidden_two, vec)
 
 
@@ -441,12 +449,11 @@
         [ANY, ANY],
         grid=(1,),
         scratch=[pltpu.VMEM(dims, BF16)] + piece_scratch(net, geo),
-        flops=2 * LENGTH * dims[0] * dims[1],
-        bytes_accessed=6_000_000,
+        us=3.0 if dims[0] < dims[1] else 3.7,
     )(me, left, right)
 
 
-def back_through_out(net, geo, me, own, peer, cotangent, normed, root, vec):
+def back_through_out(net, geo, offset, me, own, peer, cotangent, normed, root, vec):
     def kernel(
         me_ref, own_ref, peer_ref, cot_ref, n_ref, r_ref, vec_ref, back_ref, gg_ref, gs_ref, gb_ref, full, buf, sems
     ):
@@ -454,7 +461,7 @@
 
         @pl.when(first)
         def _():
-            assemble(net, geo, me_ref, own_ref, peer_ref, buf, sems, full)
+            assemble(net, geo, me_ref, own_ref, peer_ref, buf, sems, full, offset)
 
         grad = dot_nt(cot_ref[...], full[...])
         back, to_gain, to_shift = norm_backward(
@@ -475,8 +482,7 @@
         [tokens(INNER)] + [whole((1, INNER))] * 3 + [whole((INNER, D))],
         grid=(STEPS,),
         scratch=piece_scratch(net, geo),
-        flops=2 * LENGTH * D * INNER,
-        bytes_accessed=12_000_000,
+        us=6.4,
     )(me, own, peer, cotangent, normed, root, vec)
 
 
@@ -492,8 +498,7 @@
         [tokens(D), tokens(INNER), whole((INNER, D)), whole(vec.shape)],
         tokens(D),
         grid=(STEPS,),
-        flops=2 * LENGTH * D * INNER,
-        bytes_accessed=8_000_000,
+        us=3.8,
     )(block_input, hidden_three, full_out, vec)
 
 
@@ -518,8 +523,7 @@
             pltpu.VMEM((LENGTH + 2 * MARGIN, INNER), BF16),
         ]
         + piece_scratch(net, geo),
-        flops=2 * LENGTH * KERNEL * INNER * INNER,
-        bytes_accessed=7_000_000,
+        us=8.0,
     )(me, ends, hidden_two_t, back_two)
 
 
@@ -563,8 +567,7 @@
         [tokens(INNER)] + [whole((1, INNER))] * 3,
         grid=(STEPS,),
         scratch=[pltpu.VMEM((LENGTH + 2 * MARGIN, INNER), BF16)],
-        flops=2 * LENGTH * KERNEL * INNER * INNER,
-        bytes_accessed=10_000_000,
+        us=10.0,
     )(ends, back_two, full_conv, normed, root, vec)
 
 
@@ -600,8 +603,7 @@
         [tokens(D, first)] + [whole((1, D))] * 2,
         grid=(count,),
         aliases={6 + i: i for i in range(len(held))},
-        flops=2 * BLOCK * count * D * INNER,
-        bytes_accessed=12_000_000,
+        us=1.1 * count,
     )(back_one, full_in, block_input, cotangent, stat, vec, *held)
 
 
@@ -625,7 +627,7 @@
         shape((total_rows, 128), F32),
         [whole(v.shape) for v in owned] + [whole(partial.shape)],
         whole((total_rows, 128)),
-        bytes_accessed=1_000_000,
+        us=0.3,
     )(*owned, partial)
 
 
@@ -672,7 +674,7 @@
         outs,
         [whole(v.shape) for v in args],
         [whole(o.shape) for o in outs],
-        bytes_accessed=4_000_000,
+        us=2.0,
     )(*args)
 
 
@@ -705,6 +707,7 @@
         self.stage += 1
 
     def take(self):
+        self.held, self.coming = self.seq.after(self.held, self.coming)
         if self.stage <= self.net.stages():
             self.held = jnp.concatenate([self.held, self.coming], axis=0)
         self.seq.wait(self.held, self.coming)
@@ -732,6 +735,7 @@
 
     def step(self):
         self.stage -= 1
+        self.keep, self.coming = self.seq.after(self.keep, self.coming)
         half = self.keep.shape[0] // 2
         away = add(self.keep[half:], self.coming[half:])
         keep = add(self.keep[:half], self.coming[:half])
@@ -742,6 +746,7 @@
     def end(self):
         while self.stage:
             self.step()
+        self.keep, self.coming = self.seq.after(self.keep, self.coming)
         held = self.keep.astype(F32) + self.coming.astype(F32)
         self.seq.wait(held)
         return held[0]
@@ -773,7 +778,8 @@
     moment_vectors,
     square_vectors,
 ):
-    net = Network(dp, fsdp)
+    net = Network(dp, fsdp, True)
+    net_ends = Network(dp, fsdp, False)
     geo_in = Geometry(1, weight_in.shape[0], weight_in.shape[1])
     geo_conv = Geometry(KERNEL, weight_conv.shape[1], weight_conv.shape[2])
     geo_out = Geometry(1, weight_out.shape[0], weight_out.shape[1])
@@ -789,50 +795,50 @@
     cot = cotangent[0]
 
     seq = Sequence()
-    shard_in, shard_conv, shard_out = seq.run(
-        lambda *weights: pack_weights(geos, weights), weight_in, flat(weight_conv), weight_out
-    )
-    get_in = Gather(net, seq, shard_in)
+    shard_in = seq.run(functools.partial(pack_weights, (geo_in,)), weight_in)
+    get_in = Gather(net_ends, seq, shard_in)
+    get_in.send()
+    shard_conv = seq.run(functools.partial(pack_weights, (geo_conv,)), flat(weight_conv))
     get_conv = Gather(net, seq, shard_conv)
+    get_conv.send()
+    shard_out = seq.run(functools.partial(pack_weights, (geo_out,)), weight_out)
     get_out = Gather(net, seq, shard_out)
-    get_in.send()
-    get_conv.send()
     seq.wait(me, ends, vec)
-    norms = seq.run(first_norm, x, cot, vec, first=0, count=STEPS // 2)
-    get_in.step()
-    get_conv.step()
-    h1, h1_t, stat, half_b3 = seq.run(
-        lambda x, cot, vec, *held: first_norm(x, cot, vec, STEPS // 2, STEPS // 2, held),
-        x, cot, vec, *norms[:3],
-    )
-    grad_b3 = norms[3] + half_b3
-    get_in.step()
-    get_conv.step()
-    get_in.step()
-    get_in.step()
-    get_conv.step()
-    get_out.send()
+    norms = seq.run(first_norm, x, cot, vec, first=0, count=1)
+    biases = [norms[3]]
+    for step in range(1, STEPS):
+        get_in.step()
+        get_conv.step()
+        if step == 1:
+            get_out.send()
+        elif step == 2:
+            get_out.step()
+        norms = seq.run(
+            lambda x, cot, vec, *held: first_norm(x, cot, vec, step, 1, held), x, cot, vec, *norms[:3]
+        )
+        biases.append(norms[3])
+    h1, h1_t, stat = norms[:3]
+    grad_b3 = sum(biases)
     get_in.finish()
     h2, h2_t, n2, r2, full_in = seq.run(
-        functools.partial(mix_one, net, geo_in), me, get_in.held, get_in.coming, h1, vec
+        functools.partial(mix_one, net_ends, geo_in), me, get_in.held, get_in.coming, h1, vec
     )
     get_out.step()
     get_conv.step()
+    get_conv.finish()
     get_out.step()
-    get_conv.finish()
     h3, h3_t, n3, r3, full_conv = seq.run(
         functools.partial(mix_two, net, geo_conv),
         me, ends, get_conv.held, get_conv.coming, h2, vec,
     )
     get_out.step()
     pieces = seq.run(
-        functools.partial(weight_gradient, net, geo_out, name="out_gradient"), me, h3_t, cot
-    )
-    sum_out = Reduce(net, seq, *pieces)
-    get_out.step()
+        functools.partial(weight_gradient, net_ends, geo_out, name="out_gradient"), me, h3_t, cot
+    )
+    sum_out = Reduce(net_ends, seq, *pieces)
     get_out.finish()
     back_two, grad_g3, grad_s3, grad_b2, full_out = seq.run(
-        functools.partial(back_through_out, net, geo_out),
+        functools.partial(back_through_out, net, geo_out, 0),
         me, get_out.held, get_out.coming, cot, n3, r3, vec,
     )
     sum_out.step()
@@ -847,12 +853,13 @@
     sum_conv.step()
     sum_out.step()
     pieces = seq.run(
-        functools.partial(weight_gradient, net, geo_in, name="in_gradient"), me, h1_t, back_one
-    )
-    sum_in = Reduce(net, seq, *pieces)
-    sum_out.step()
+        functools.partial(weight_gradient, net_ends, geo_in, name="in_gradient"),
+        me, h1_t, back_one,
+    )
+    sum_in = Reduce(net_ends, seq, *pieces)
     block_output = seq.run(block_result, x, h3, full_out, vec)
     sum_in.step()
+    sum_out.step()
     sum_conv.step()
     ends_in = seq.run(back_through_in, back_one, full_in, x, cot, stat, vec, first=0, count=STEPS // 2)
     sum_in.step()
@@ -862,12 +869,12 @@
         lambda *args: back_through_in(*args[:6], STEPS // 2, STEPS // 2, args[6:]),
         back_one, full_in, x, cot, stat, vec, ends_in[0],
     )
+    sum_in.step()
+    sum_conv.step()
     grad_g1, grad_s1 = ends_in[1] + more_g1, ends_in[2] + more_s1
     partial = jnp.concatenate(
         [grad_g1, grad_s1, grad_g2, grad_s2, grad_g3, grad_s3, grad_b1, grad_b2, grad_b3], axis=1
     ).reshape(-1, 128)
-    sum_in.step()
-    sum_conv.step()
     seq.wait(partial)
     sum_in.step()
     grad_conv = sum_conv.end()

time: 188 us -> 174 us (0.926)
  waiting for transfers between devices: 65.5 us -> 57 us
  starting transfers between devices: 40 us -> 34 us
    ppermute x15, waiting for transfers between devices: 33.7 us -> 24.5 us  [send(): lax.ppermute(held, AXES, self.net.core() if last else self.net.stage(self...]
    ppermute x15, starting transfers between devices: 21.2 us -> 17 us  [send(): lax.ppermute(held, AXES, self.net.core() if last else self.net.stage(self...]
    pallas_call x2 -> x4, Pallas kernels: 4.75 us -> 4.36 us  [first_norm(): call(kernel, 'first_norm', [shape((LENGTH, D), BF16), shape((D, LENGTH),...]
    unnamed x64 -> x66, local copies, waits for them, and re-layouts: 6.69 us -> 6.71 us
  transfers between devices with their start and end apart: 35 -> 35, of which waited for: 21 -> 20; matrix products, arithmetic and copies ran while one was open for 2% -> 3% of each run, Pallas kernels for 26% -> 39%
where the time goes in v3:
time: 174 us
  Pallas kernels  69.4 us (40%)
  waiting for transfers between devices  57 us (33%)
  starting transfers between devices  34 us (20%)
  local copies, waits for them, and re-layouts  7.23 us (4%)
  other arithmetic  4.55 us (3%)
    ppermute x15, waiting for transfers between devices, send(): lax.ppermute(held, AXES, self.net.core() if last else self.net.stage(self...  24.5 us
    ppermute x15, starting transfers between devices, send(): lax.ppermute(held, AXES, self.net.core() if last else self.net.stage(self...  17 us
    ppermute x12, waiting for transfers between devices, step(): self.coming = lax.ppermute(away, AXES, self.net.stage(self.stage))  16.8 us
    ppermute x4, waiting for transfers between devices, total_sum(): value = value + lax.ppermute(value, AXES, net.stage(stage))  14.4 us
    ppermute x12, starting transfers between devices, step(): self.coming = lax.ppermute(away, AXES, self.net.stage(self.stage))  13.7 us
    pallas_call x1, Pallas kernels, mix_two(): call(kernel, 'mix_two', NORM_SHAPES + [shape((KERNEL * INNER, INNER), BF1...  11.7 us
    pallas_call x1, Pallas kernels, back_through_conv(): call(kernel, 'back_through_conv', [shape((LENGTH, INNER), BF16), row, row...  10.1 us
    pallas_call x2, Pallas kernels, back_through_in(): call(kernel, 'back_through_in', [shape((LENGTH, D), BF16), row, row], [to...  9.12 us
  transfers between devices with their start and end apart: 35, of which 20 were waited for; matrix products, arithmetic and copies ran while one was open for 3% of the time, Pallas kernels for 39%

profile of v3, /device:TPU:0, one launch (start us, length us, event | category | flops | bytes accessed | tf_op | source)
XLA Modules:
  0.0 173.6 jit_solution(6558183954659780599)
XLA Ops:
  0.7 1.0 copy-done.9
  1.7 4.1 %collective-permute-start.1 = (bf16[1,208,128]{2,1,0:T(8,128)(2,1)S(1)}, bf16[1,208,128]{2,1,0:T(8,128)(2,1)S(1)}, u32[]{:S(2)}, u32[]{:S(2)}) collective-permute-start(bf16[1,208,128]{2,1,0:T(8,128)(2,1)S(1)} %bitcast.35), channel_id=1, source_target_pairs={{0,4},{1,5},{2,6},{3,7},{4,0},{5,1},{6,2},{7,3},{8,10},{9,11},{10,... | collective-permute-start | bytes 159752 | tf_op jit(solution)/shard_map/ppermute | solution.py:706
  6.0 0.6 copy-done
  6.9 0.5 copy-done.23
  7.5 0.9 copy-done.2
  8.5 1.7 %copy-done.3 = bf16[1,1024,1280]{2,1,0:T(8,128)(2,1)S(1)} copy-done((bf16[1,1024,1280]{2,1,0:T(8,128)(2,1)S(1)}, bf16[1,1024,1280]{2,1,0:T(8,128)(2,1)}, u32[]{:S(2)}) %copy-start.3) | copy-done | bytes 2621464
  10.2 1.1 first_norm.4
  11.3 1.6 collective-permute-start.3
  13.3 1.9 %collective-permute-start.6 = (bf16[1,208,128]{2,1,0:T(8,128)(2,1)S(1)}, bf16[1,208,128]{2,1,0:T(8,128)(2,1)S(1)}, u32[]{:S(2)}, u32[]{:S(2)}) collective-permute-start(bf16[1,208,128]{2,1,0:T(8,128)(2,1)S(1)} %bitcast.33), channel_id=1, source_target_pairs={{0,4},{1,5},{2,6},{3,7},{4,0},{5,1},{6,2},{7,3},{8,10},{9,11},{10,... | collective-permute-start | bytes 159752 | tf_op jit(solution)/shard_map/ppermute | solution.py:706
  15.2 1.6 collective-permute-start.2
  16.8 1.1 first_norm.5
  17.9 1.6 collective-permute-start.5
  19.5 4.4 %collective-permute-done.2 = bf16[2,512,128]{2,1,0:T(8,128)(2,1)S(1)} collective-permute-done((bf16[2,512,128]{2,1,0:T(8,128)(2,1)S(1)}, bf16[2,512,128]{2,1,0:T(8,128)(2,1)S(1)}, u32[]{:S(2)}, u32[]{:S(2)}) %collective-permute-start.2) | collective-permute-done | bytes 262176 | tf_op jit(solution)/shard_map/ppermute | solution.py:706
  24.0 0.6 collective-permute-start.4
  24.6 1.1 first_norm.6
  25.8 0.6 collective-permute-start.9
  26.3 6.9 %collective-permute-done.4 = bf16[4,512,128]{2,1,0:T(8,128)(2,1)S(1)} collective-permute-done((bf16[4,512,128]{2,1,0:T(8,128)(2,1)S(1)}, bf16[4,512,128]{2,1,0:T(8,128)(2,1)S(1)}, u32[]{:S(2)}, u32[]{:S(2)}) %collective-permute-start.4) | collective-permute-done | bytes 524320 | tf_op jit(solution)/shard_map/ppermute | solution.py:706
  33.4 1.1 first_norm.7
  34.5 1.5 copy-done.18
  36.0 2.1 %collective-permute-done.9 = bf16[8,208,128]{2,1,0:T(8,128)(2,1)S(1)} collective-permute-done((bf16[8,208,128]{2,1,0:T(8,128)(2,1)S(1)}, bf16[8,208,128]{2,1,0:T(8,128)(2,1)S(1)}, u32[]{:S(2)}, u32[]{:S(2)}) %collective-permute-start.9) | collective-permute-done | bytes 426016 | tf_op jit(solution)/shard_map/ppermute | solution.py:706
  38.2 1.6 collective-permute-start.7
  39.8 0.7 collective-permute-done.10.peer_ref
  40.6 6.7 %mix_one.1 = (bf16[1024,640]{1,0:T(8,128)(2,1)S(1)}, bf16[640,1024]{1,0:T(8,128)(2,1)S(1)}, f32[1024,640]{1,0:T(8,128)S(1)}, f32[1024,128]{1,0:T(8,128)S(1)}, bf16[1280,640]{1,0:T(8,128)(2,1)S(1)}) custom-call(s32[2]{0:T(128)S(1)} %pad_add_fusion.me_ref, bf16[16,208,128]{2,1,0:T(8,128)(2,1)S(1)} %constant_dynamic-update-slice_fusion.14.own_ref, ...), custom_call_target="tpu_custom_call" | custom-call | flops 46000000 | tf_op jit(solution)/shard_map/mix_one/pallas_call | solution.py:389
  47.4 5.7 %collective-permute-done.7 = bf16[8,512,128]{2,1,0:T(8,128)(2,1)S(1)} collective-permute-done((bf16[8,512,128]{2,1,0:T(8,128)(2,1)S(1)}, bf16[8,512,128]{2,1,0:T(8,128)(2,1)S(1)}, u32[]{:S(2)}, u32[]{:S(2)}) %collective-permute-start.7) | collective-permute-done | bytes 1048608 | tf_op jit(solution)/shard_map/ppermute | solution.py:706
  53.4 1.6 collective-permute-start.12
  55.0 2.6 %collective-permute-done.11.peer_ref = bf16[16,512,128]{2,1,0:T(8,128)(2,1)S(1)} collective-permute-done((bf16[16,512,128]{2,1,0:T(8,128)(2,1)S(1)}, bf16[16,512,128]{2,1,0:T(8,128)(2,1)S(1)}, u32[]{:S(2)}, u32[]{:S(2)}) %collective-permute-start.11) | collective-permute-done | bytes 2097184 | tf_op jit(solution)/shard_map/ppermute | solution.py:706
  57.5 1.8 %collective-permute-done.12 = bf16[4,208,128]{2,1,0:T(8,128)(2,1)S(1)} collective-permute-done((bf16[4,208,128]{2,1,0:T(8,128)(2,1)S(1)}, bf16[4,208,128]{2,1,0:T(8,128)(2,1)S(1)}, u32[]{:S(2)}, u32[]{:S(2)}) %collective-permute-start.12) | collective-permute-done | bytes 213024 | tf_op jit(solution)/shard_map/ppermute | solution.py:706
  59.3 1.6 collective-permute-start.13
  61.0 11.7 %mix_two.1 = (bf16[1024,640]{1,0:T(8,128)(2,1)S(1)}, bf16[640,1024]{1,0:T(8,128)(2,1)S(1)}, f32[1024,640]{1,0:T(8,128)S(1)}, f32[1024,128]{1,0:T(8,128)S(1)}, bf16[3200,640]{1,0:T(8,128)(2,1)S(1)}) custom-call(s32[2]{0:T(128)S(1)} %pad_add_fusion.me_ref, s32[4]{0:T(128)S(1)} %bitcast.60, ...), custom_call_target="tpu_custom_call" | custom-call | flops 53819998208 | tf_op jit(solution)/shard_map/mix_two/pallas_call | solution.py:421
  72.8 3.0 %out_gradient.1 = (bf16[16,208,128]{2,1,0:T(8,128)(2,1)S(1)}, bf16[16,208,128]{2,1,0:T(8,128)(2,1)S(1)}) custom-call(s32[2]{0:T(128)S(1)} %pad_add_fusion.me_ref, bf16[640,1024]{1,0:T(8,128)(2,1)S(1)} %get-tuple-element.348.left_ref, bf16[1024,1280]{1,0:T(8,128)(2,1)S(1)} %bitcast.50), custom_call_target="tpu_custom_call" | custom-call | flops 13799999488 | tf_op jit(solution)/shard_map/out_gradient/pallas_call | solution.py:444
  75.9 0.6 collective-permute-start.15
  76.4 6.6 %back_through_out.1 = (bf16[1024,640]{1,0:T(8,128)(2,1)S(1)}, f32[1,640]{1,0:T(1,128)S(1)}, f32[1,640]{1,0:T(1,128)S(1)}, f32[1,640]{1,0:T(1,128)S(1)}, bf16[640,1280]{1,0:T(8,128)(2,1)S(1)}) custom-call(s32[2]{0:T(128)S(1)} %pad_add_fusion.me_ref, bf16[16,208,128]{2,1,0:T(8,128)(2,1)S(1)} %constant_dynamic-update-slice_fusion.22.own_ref, ...), custom_call_target="tpu_custom_call" | custom-call | flops 29440000000 | tf_op jit(solution)/shard_map/back_through_out/pallas_call | solution.py:477
  83.4 8.0 %conv_gradient.1 = (bf16[16,512,128]{2,1,0:T(8,128)(2,1)S(1)}, bf16[16,512,128]{2,1,0:T(8,128)(2,1)S(1)}) custom-call(s32[2]{0:T(128)S(1)} %pad_add_fusion.me_ref, s32[4]{0:T(128)S(1)} %bitcast.61, bf16[640,1024]{1,0:T(8,128)(2,1)S(1)} %get-tuple-element.376.left_ref, bf16[1024,640]{1,0:T(8,128)(2,1)S(1)} %get-tuple-element.384.back_ref), custom_call_target="tpu_custom_call" | custom-call | flops 36800000000 | tf_op jit(solution)/shard_map/conv_gradient/pallas_call | solution.py:514
  91.5 0.4 collective-permute-start.18
  91.9 4.2 %collective-permute-done.16 = bf16[8,208,128]{2,1,0:T(8,128)(2,1)S(1)} collective-permute-done((bf16[8,208,128]{2,1,0:T(8,128)(2,1)S(1)}, bf16[8,208,128]{2,1,0:T(8,128)(2,1)S(1)}, u32[]{:S(2)}, u32[]{:S(2)}) %collective-permute-start.16) | collective-permute-done | bytes 426016 | tf_op jit(solution)/shard_map/ppermute | solution.py:744
  96.5 10.1 %back_through_conv.1 = (bf16[1024,640]{1,0:T(8,128)(2,1)S(1)}, f32[1,640]{1,0:T(1,128)S(1)}, f32[1,640]{1,0:T(1,128)S(1)}, f32[1,640]{1,0:T(1,128)S(1)}) custom-call(s32[4]{0:T(128)S(1)} %bitcast.62, bf16[1024,640]{1,0:T(8,128)(2,1)S(1)} %get-tuple-element.384.back_ref, bf16[3200,640]{1,0:T(8,128)(2,1)S(1)} %get-tuple-element.385.w_ref, ...), custom_call_target="tpu_custom_call" | custom-call | flops 46000001024 | tf_op jit(solution)/shard_map/back_through_conv/pallas_call | solution.py:555
  106.6 0.5 add_convert_fusion
  107.1 1.9 %collective-permute-start.19 = (bf16[8,512,128]{2,1,0:T(8,128)(2,1)S(1)}, bf16[8,512,128]{2,1,0:T(8,128)(2,1)S(1)}, u32[]{:S(2)}, u32[]{:S(2)}) collective-permute-start(bf16[8,512,128]{2,1,0:T(8,128)(2,1)S(1)} %get-tuple-element.396), channel_id=1, source_target_pairs={{0,16},{1,17},{2,18},{3,19},{4,20},{5,21},{6,22},{7,23},{8,9},{9,8... | collective-permute-start | bytes 3145736 | tf_op jit(solution)/shard_map/ppermute | solution.py:744
  109.1 1.6 collective-permute-start.20
  110.7 3.7 %in_gradient.1 = (bf16[16,208,128]{2,1,0:T(8,128)(2,1)S(1)}, bf16[16,208,128]{2,1,0:T(8,128)(2,1)S(1)}) custom-call(s32[2]{0:T(128)S(1)} %pad_add_fusion.me_ref, bf16[1280,1024]{1,0:T(8,128)(2,1)S(1)} %copy-done.19, bf16[1024,640]{1,0:T(8,128)(2,1)S(1)} %get-tuple-element.442.right_ref.back_ref), custom_call_target="tpu_custom_call" | custom-call | flops 17020000256 | tf_op jit(solution)/shard_map/in_gradient/pallas_call | solution.py:444
  114.5 3.8 %block_result.1 = bf16[1024,1280]{1,0:T(8,128)(2,1)} custom-call(bf16[1024,1280]{1,0:T(8,128)(2,1)S(1)} %bitcast.43, bf16[1024,640]{1,0:T(8,128)(2,1)S(1)} %get-tuple-element.406.h_ref, bf16[640,1280]{1,0:T(8,128)(2,1)S(1)} %get-tuple-element.407.w_ref, f32[1,7680]{1,0:T(1,128)S(1)} %reshape.103.vec_ref), custom_call_target="tpu_custom_call" | custom-call | flops 17479999488 | tf_op jit(solution)/shard_map/block_result/pallas_call | solution.py:494
  118.6 0.7 add_convert_fusion.22
  119.3 3.0 %collective-permute-start.22 = (bf16[1,208,128]{2,1,0:T(8,128)(2,1)}, bf16[1,208,128]{2,1,0:T(8,128)(2,1)}, u32[]{:S(2)}, u32[]{:S(2)}) collective-permute-start(bf16[1,208,128]{2,1,0:T(8,128)(2,1)} %get-tuple-element.419), channel_id=1, source_target_pairs={{0,4},{1,5},{2,6},{3,7},{4,0},{5,1},{6,2},{7,3},{8,10},{9,11},{10,... | collective-permute-start | bytes 159752 | tf_op jit(solution)/shard_map/ppermute | solution.py:744
  122.3 0.8 collective-permute-done.19
  123.4 1.7 collective-permute-start.23
  125.2 4.6 %back_through_in.2 = (bf16[1024,1280]{1,0:T(8,128)(2,1)}, f32[1,1280]{1,0:T(1,128)S(1)}, f32[1,1280]{1,0:T(1,128)S(1)}) custom-call(bf16[1024,640]{1,0:T(8,128)(2,1)S(1)} %get-tuple-element.442.right_ref.back_ref, bf16[1280,640]{1,0:T(8,128)(2,1)S(1)} %get-tuple-element.443.w_ref, bf16[1024,1280]{1,0:T(8,128)(2,1)S(1)} %bitcast.44, ...), custom_call_target="tpu_custom_call" | custom-call | flops 10119999488 | tf_op jit(solution)/shard_map/back_through_in/pallas_call | solution.py:590
  129.7 2.7 %collective-permute-done.24 = bf16[8,208,128]{2,1,0:T(8,128)(2,1)S(1)} collective-permute-done((bf16[8,208,128]{2,1,0:T(8,128)(2,1)S(1)}, bf16[8,208,128]{2,1,0:T(8,128)(2,1)S(1)}, u32[]{:S(2)}, u32[]{:S(2)}) %collective-permute-start.24) | collective-permute-done | bytes 426016 | tf_op jit(solution)/shard_map/ppermute | solution.py:744
  132.6 0.5 collective-permute-start.25
  133.1 0.8 add_convert_fusion.8
  133.9 4.6 %back_through_in.3 = (bf16[1024,1280]{1,0:T(8,128)(2,1)}, f32[1,1280]{1,0:T(1,128)S(1)}, f32[1,1280]{1,0:T(1,128)S(1)}) custom-call(bf16[1024,640]{1,0:T(8,128)(2,1)S(1)} %get-tuple-element.442.right_ref.back_ref, bf16[1280,640]{1,0:T(8,128)(2,1)S(1)} %get-tuple-element.443.w_ref, bf16[1024,1280]{1,0:T(8,128)(2,1)S(1)} %bitcast.45, ...), custom_call_target="tpu_custom_call", output_to_operand_aliasing={{0}: (6, {})} | custom-call | flops 10119999488 | tf_op jit(solution)/shard_map/back_through_in/pallas_call | solution.py:590
  138.7 1.3 collective-permute-start.26
  140.1 3.2 %collective-permute-done.27 = bf16[2,512,128]{2,1,0:T(8,128)(2,1)S(1)} collective-permute-done((bf16[2,512,128]{2,1,0:T(8,128)(2,1)}, bf16[2,512,128]{2,1,0:T(8,128)(2,1)S(1)}, u32[]{:S(2)}, u32[]{:S(2)}) %collective-permute-start.27) | collective-permute-done | bytes 262176 | tf_op jit(solution)/shard_map/ppermute | solution.py:744
  143.5 3.2 %collective-permute-start.28 = (bf16[1,208,128]{2,1,0:T(8,128)(2,1)S(1)}, bf16[1,208,128]{2,1,0:T(8,128)(2,1)S(1)}, u32[]{:S(2)}, u32[]{:S(2)}) collective-permute-start(bf16[1,208,128]{2,1,0:T(8,128)(2,1)S(1)} %get-tuple-element.469), channel_id=1, source_target_pairs={{0,4},{1,5},{2,6},{3,7},{4,0},{5,1},{6,2},{7,3},{8,10},{9,11},{10,... | collective-permute-start | bytes 159752 | tf_op jit(solution)/shard_map/ppermute | solution.py:744
  146.7 2.1 %collective-permute-done.28 = bf16[1,208,128]{2,1,0:T(8,128)(2,1)S(1)} collective-permute-done((bf16[1,208,128]{2,1,0:T(8,128)(2,1)S(1)}, bf16[1,208,128]{2,1,0:T(8,128)(2,1)S(1)}, u32[]{:S(2)}, u32[]{:S(2)}) %collective-permute-start.28) | collective-permute-done | bytes 53280 | tf_op jit(solution)/shard_map/ppermute | solution.py:744
  148.9 0.8 add_bitcast_fusion
  149.7 3.7 %collective-permute-done.29 = bf16[1,512,128]{2,1,0:T(8,128)(2,1)S(1)} collective-permute-done((bf16[1,512,128]{2,1,0:T(8,128)(2,1)S(1)}, bf16[1,512,128]{2,1,0:T(8,128)(2,1)S(1)}, u32[]{:S(2)}, u32[]{:S(2)}) %collective-permute-start.29) | collective-permute-done | bytes 131104 | tf_op jit(solution)/shard_map/ppermute | solution.py:744
  153.7 1.2 collective-permute-done.30
  154.9 4.8 %collective-permute-done.31 = f32[64,128]{1,0:T(8,128)S(1)} collective-permute-done((f32[64,128]{1,0:T(8,128)S(1)}, f32[64,128]{1,0:T(8,128)S(1)}, u32[]{:S(2)}, u32[]{:S(2)}) %collective-permute-start.31) | collective-permute-done | bytes 32800 | tf_op jit(solution)/shard_map/ppermute | solution.py:758
  159.7 3.9 %collective-permute-done.32 = f32[64,128]{1,0:T(8,128)S(1)} collective-permute-done((f32[64,128]{1,0:T(8,128)S(1)}, f32[64,128]{1,0:T(8,128)S(1)}, u32[]{:S(2)}, u32[]{:S(2)}) %collective-permute-start.32) | collective-permute-done | bytes 32800 | tf_op jit(solution)/shard_map/ppermute | solution.py:758
  163.6 0.7 collective-permute-start.33
  164.3 3.3 %collective-permute-done.33 = f32[64,128]{1,0:T(8,128)S(1)} collective-permute-done((f32[64,128]{1,0:T(8,128)S(1)}, f32[64,128]{1,0:T(8,128)S(1)}, u32[]{:S(2)}, u32[]{:S(2)}) %collective-permute-start.33) | collective-permute-done | bytes 32800 | tf_op jit(solution)/shard_map/ppermute | solution.py:758
  167.6 1.5 collective-permute-start.34
  169.1 2.4 %collective-permute-done.34 = f32[64,128]{1,0:T(8,128)S(1)} collective-permute-done((f32[64,128]{1,0:T(8,128)S(1)}, f32[64,128]{1,0:T(8,128)S(1)}, u32[]{:S(2)}, u32[]{:S(2)}) %collective-permute-start.34) | collective-permute-done | bytes 32800 | tf_op jit(solution)/shard_map/ppermute | solution.py:758
  171.7 1.9 %update_all.1 = (f32[1,1]{1,0:T(1,128)}, f32[160,160]{1,0:T(8,128)}, f32[160,160]{1,0:T(8,128)}, f32[160,160]{1,0:T(8,128)}, f32[400,160]{1,0:T(8,128)}, /*index...) custom-call(f32[208,128]{1,0:T(8,128)S(1)} %get-tuple-element.511.re, ...), custom_call_target="tpu_custom_call" | custom-call | flops 9200000000 | tf_op jit(solution)/shard_map/update_all/pallas_call | solution.py:671
  (129 shorter events, 4.4 us)
Async XLA Ops:
  0.6 5.1 %copy-start.5 = (f32[5,80,160]{2,1,0:T(8,128)S(1)}, f32[5,80,160]{2,1,0:T(8,128)}, u32[]{:S(2)}) copy-start(f32[5,80,160]{2,1,0:T(8,128)} %param.21) | copy-start | bytes 768004
  0.7 1.0 copy-start.9
  1.7 9.6 %collective-permute-start.1 = (bf16[1,208,128]{2,1,0:T(8,128)(2,1)S(1)}, bf16[1,208,128]{2,1,0:T(8,128)(2,1)S(1)}, u32[]{:S(2)}, u32[]{:S(2)}) collective-permute-start(bf16[1,208,128]{2,1,0:T(8,128)(2,1)S(1)} %bitcast.35), channel_id=1, source_target_pairs={{0,4},{1,5},{2,6},{3,7},{4,0},{5,1},{6,2},{7,3},{8,10},{9,11},{10,... | collective-permute-start | bytes 159752 | tf_op jit(solution)/shard_map/ppermute | solution.py:706
  5.8 0.8 copy-start
  5.8 0.9 copy-start.13
  5.9 7.3 %collective-permute-start = (bf16[1,512,128]{2,1,0:T(8,128)(2,1)S(1)}, bf16[1,512,128]{2,1,0:T(8,128)(2,1)S(1)}, u32[]{:S(2)}, u32[]{:S(2)}) collective-permute-start(bf16[1,512,128]{2,1,0:T(8,128)(2,1)S(1)} %bitcast.31), channel_id=1, source_target_pairs={{0,4},{1,5},{2,6},{3,7},{4,0},{5,1},{6,2},{7,3},{8,10},{9,11},{10,... | collective-permute-start | bytes 393224 | tf_op jit(solution)/shard_map/ppermute | solution.py:706
  6.7 0.7 copy-start.23
  6.7 1.8 %copy-start.2 = (bf16[1,1024,1280]{2,1,0:T(8,128)(2,1)S(1)}, bf16[1,1024,1280]{2,1,0:T(8,128)(2,1)}, u32[]{:S(2)}) copy-start(bf16[1,1024,1280]{2,1,0:T(8,128)(2,1)} %param.15) | copy-start | bytes 7864324
  8.5 1.7 %copy-start.3 = (bf16[1,1024,1280]{2,1,0:T(8,128)(2,1)S(1)}, bf16[1,1024,1280]{2,1,0:T(8,128)(2,1)}, u32[]{:S(2)}) copy-start(bf16[1,1024,1280]{2,1,0:T(8,128)(2,1)} %param.16) | copy-start | bytes 7864324
  11.3 6.5 %collective-permute-start.3 = (bf16[2,208,128]{2,1,0:T(8,128)(2,1)S(1)}, bf16[2,208,128]{2,1,0:T(8,128)(2,1)S(1)}, u32[]{:S(2)}, u32[]{:S(2)}) collective-permute-start(bf16[2,208,128]{2,1,0:T(8,128)(2,1)S(1)} %constant_dynamic-update-slice_fusion), channel_id=1, source_target_pairs={{0,1},{1,0},{2,3},{3,2},{4,5},{5,4},{6,7},{7,6},{8,24},{9,25},{10,... | collective-permute-start | bytes 319496 | tf_op jit(solution)/shard_map/ppermute | solution.py:706
  13.3 10.7 %collective-permute-start.6 = (bf16[1,208,128]{2,1,0:T(8,128)(2,1)S(1)}, bf16[1,208,128]{2,1,0:T(8,128)(2,1)S(1)}, u32[]{:S(2)}, u32[]{:S(2)}) collective-permute-start(bf16[1,208,128]{2,1,0:T(8,128)(2,1)S(1)} %bitcast.33), channel_id=1, source_target_pairs={{0,4},{1,5},{2,6},{3,7},{4,0},{5,1},{6,2},{7,3},{8,10},{9,11},{10,... | collective-permute-start | bytes 159752 | tf_op jit(solution)/shard_map/ppermute | solution.py:706
  15.2 8.7 %collective-permute-start.2 = (bf16[2,512,128]{2,1,0:T(8,128)(2,1)S(1)}, bf16[2,512,128]{2,1,0:T(8,128)(2,1)S(1)}, u32[]{:S(2)}, u32[]{:S(2)}) collective-permute-start(bf16[2,512,128]{2,1,0:T(8,128)(2,1)S(1)} %constant_dynamic-update-slice_fusion.2), channel_id=1, source_target_pairs={{0,2},{1,3},{2,0},{3,1},{4,6},{5,7},{6,4},{7,5},{8,12},{9,13},{10,... | collective-permute-start | bytes 786440 | tf_op jit(solution)/shard_map/ppermute | solution.py:706
  17.9 7.8 %collective-permute-start.5 = (bf16[4,208,128]{2,1,0:T(8,128)(2,1)S(1)}, bf16[4,208,128]{2,1,0:T(8,128)(2,1)S(1)}, u32[]{:S(2)}, u32[]{:S(2)}) collective-permute-start(bf16[4,208,128]{2,1,0:T(8,128)(2,1)S(1)} %constant_dynamic-update-slice_fusion.4), channel_id=1, source_target_pairs={{0,16},{1,17},{2,18},{3,19},{4,20},{5,21},{6,22},{7,23},{8,9},{9,8... | collective-permute-start | bytes 638984 | tf_op jit(solution)/shard_map/ppermute | solution.py:706
  24.0 9.2 %collective-permute-start.4 = (bf16[4,512,128]{2,1,0:T(8,128)(2,1)S(1)}, bf16[4,512,128]{2,1,0:T(8,128)(2,1)S(1)}, u32[]{:S(2)}, u32[]{:S(2)}) collective-permute-start(bf16[4,512,128]{2,1,0:T(8,128)(2,1)S(1)} %constant_dynamic-update-slice_fusion.6), channel_id=1, source_target_pairs={{0,1},{1,0},{2,3},{3,2},{4,5},{5,4},{6,7},{7,6},{8,24},{9,25},{10,... | collective-permute-start | bytes 1572872 | tf_op jit(solution)/shard_map/ppermute | solution.py:706
  25.8 12.2 %collective-permute-start.9 = (bf16[8,208,128]{2,1,0:T(8,128)(2,1)S(1)}, bf16[8,208,128]{2,1,0:T(8,128)(2,1)S(1)}, u32[]{:S(2)}, u32[]{:S(2)}) collective-permute-start(bf16[8,208,128]{2,1,0:T(8,128)(2,1)S(1)} %constant_dynamic-update-slice_fusion.10), channel_id=1, source_target_pairs={{0,2},{1,3},{2,0},{3,1},{4,6},{5,7},{6,4},{7,5},{8,12},{9,13},{10,... | collective-permute-start | bytes 1277960 | tf_op jit(solution)/shard_map/ppermute | solution.py:706
  34.5 1.5 copy-start.18
  36.0 11.3 %copy-start.20 = (f32[1024,128]{1,0:T(8,128)}, f32[1024,128]{1,0:T(8,128)S(1)}, u32[]{:S(2)}) copy-start(f32[1024,128]{1,0:T(8,128)S(1)} %get-tuple-element.446.stat_ref) | copy-start | bytes 1572868
  38.1 2.4 %collective-permute-start.10 = (bf16[16,208,128]{2,1,0:T(8,128)(2,1)S(1)}, bf16[16,208,128]{2,1,0:T(8,128)(2,1)S(1)}, u32[]{:S(2)}, u32[]{:S(2)}) collective-permute-start(bf16[16,208,128]{2,1,0:T(8,128)(2,1)S(1)} %constant_dynamic-update-slice_fusion.14.own_ref), channel_id=1, source_target_pairs={{0,8},{1,9},{2,10},{3,11},{4,12},{5,13},{6,14},{7,15},{8,0},{9,1},... | collective-permute-start | bytes 2555912 | tf_op jit(solution)/shard_map/ppermute | solution.py:706
  38.2 14.9 %collective-permute-start.7 = (bf16[8,512,128]{2,1,0:T(8,128)(2,1)S(1)}, bf16[8,512,128]{2,1,0:T(8,128)(2,1)S(1)}, u32[]{:S(2)}, u32[]{:S(2)}) collective-permute-start(bf16[8,512,128]{2,1,0:T(8,128)(2,1)S(1)} %constant_dynamic-update-slice_fusion.12), channel_id=1, source_target_pairs={{0,16},{1,17},{2,18},{3,19},{4,20},{5,21},{6,22},{7,23},{8,9},{9,8... | collective-permute-start | bytes 3145736 | tf_op jit(solution)/shard_map/ppermute | solution.py:706
  39.8 7.5 %collective-permute-start.8 = (bf16[2,208,128]{2,1,0:T(8,128)(2,1)S(1)}, bf16[2,208,128]{2,1,0:T(8,128)(2,1)S(1)}, u32[]{:S(2)}, u32[]{:S(2)}) collective-permute-start(bf16[2,208,128]{2,1,0:T(8,128)(2,1)S(1)} %constant_dynamic-update-slice_fusion.8), channel_id=1, source_target_pairs={{0,2},{1,3},{2,0},{3,1},{4,6},{5,7},{6,4},{7,5},{8,12},{9,13},{10,... | collective-permute-start | bytes 319496 | tf_op jit(solution)/shard_map/ppermute | solution.py:706
  53.3 4.2 %collective-permute-start.11 = (bf16[16,512,128]{2,1,0:T(8,128)(2,1)S(1)}, bf16[16,512,128]{2,1,0:T(8,128)(2,1)S(1)}, u32[]{:S(2)}, u32[]{:S(2)}) collective-permute-start(bf16[16,512,128]{2,1,0:T(8,128)(2,1)S(1)} %constant_dynamic-update-slice_fusion.18.own_ref), channel_id=1, source_target_pairs={{0,8},{1,9},{2,10},{3,11},{4,12},{5,13},{6,14},{7,15},{8,0},{9,1},... | collective-permute-start | bytes 6291464 | tf_op jit(solution)/shard_map/ppermute | solution.py:706
  53.4 5.9 %collective-permute-start.12 = (bf16[4,208,128]{2,1,0:T(8,128)(2,1)S(1)}, bf16[4,208,128]{2,1,0:T(8,128)(2,1)S(1)}, u32[]{:S(2)}, u32[]{:S(2)}) collective-permute-start(bf16[4,208,128]{2,1,0:T(8,128)(2,1)S(1)} %constant_dynamic-update-slice_fusion.16), channel_id=1, source_target_pairs={{0,1},{1,0},{2,3},{3,2},{4,5},{5,4},{6,7},{7,6},{8,24},{9,25},{10,... | collective-permute-start | bytes 638984 | tf_op jit(solution)/shard_map/ppermute | solution.py:706
  59.3 13.5 %copy-start.4 = (bf16[1,1024,1280]{2,1,0:T(8,128)(2,1)S(1)}, bf16[1,1024,1280]{2,1,0:T(8,128)(2,1)}, u32[]{:S(2)}) copy-start(bf16[1,1024,1280]{2,1,0:T(8,128)(2,1)} %param.16) | copy-start | bytes 7864324
  59.3 13.3 %collective-permute-start.13 = (bf16[8,208,128]{2,1,0:T(8,128)(2,1)S(1)}, bf16[8,208,128]{2,1,0:T(8,128)(2,1)S(1)}, u32[]{:S(2)}, u32[]{:S(2)}) collective-permute-start(bf16[8,208,128]{2,1,0:T(8,128)(2,1)S(1)} %constant_dynamic-update-slice_fusion.20), channel_id=1, source_target_pairs={{0,16},{1,17},{2,18},{3,19},{4,20},{5,21},{6,22},{7,23},{8,9},{9,8... | collective-permute-start | bytes 1277960 | tf_op jit(solution)/shard_map/ppermute | solution.py:706
  72.8 3.7 %collective-permute-start.14 = (bf16[16,208,128]{2,1,0:T(8,128)(2,1)S(1)}, bf16[16,208,128]{2,1,0:T(8,128)(2,1)S(1)}, u32[]{:S(2)}, u32[]{:S(2)}) collective-permute-start(bf16[16,208,128]{2,1,0:T(8,128)(2,1)S(1)} %constant_dynamic-update-slice_fusion.22.own_ref), channel_id=1, source_target_pairs={{0,8},{1,9},{2,10},{3,11},{4,12},{5,13},{6,14},{7,15},{8,0},{9,1},... | collective-permute-start | bytes 2555912 | tf_op jit(solution)/shard_map/ppermute | solution.py:706
  75.9 7.2 %collective-permute-start.15 = (bf16[16,208,128]{2,1,0:T(8,128)(2,1)S(1)}, bf16[16,208,128]{2,1,0:T(8,128)(2,1)S(1)}, u32[]{:S(2)}, u32[]{:S(2)}) collective-permute-start(bf16[16,208,128]{2,1,0:T(8,128)(2,1)S(1)} %get-tuple-element.368), channel_id=1, source_target_pairs={{0,8},{1,9},{2,10},{3,11},{4,12},{5,13},{6,14},{7,15},{8,0},{9,1},... | collective-permute-start | bytes 2555912 | tf_op jit(solution)/shard_map/ppermute | solution.py:734
  83.3 12.8 %collective-permute-start.16 = (bf16[8,208,128]{2,1,0:T(8,128)(2,1)S(1)}, bf16[8,208,128]{2,1,0:T(8,128)(2,1)S(1)}, u32[]{:S(2)}, u32[]{:S(2)}) collective-permute-start(bf16[8,208,128]{2,1,0:T(8,128)(2,1)S(1)} %get-tuple-element.372), channel_id=1, source_target_pairs={{0,2},{1,3},{2,0},{3,1},{4,6},{5,7},{6,4},{7,5},{8,12},{9,13},{10,... | collective-permute-start | bytes 1277960 | tf_op jit(solution)/shard_map/ppermute | solution.py:744
  91.5 15.1 %collective-permute-start.18 = (bf16[16,512,128]{2,1,0:T(8,128)(2,1)S(1)}, bf16[16,512,128]{2,1,0:T(8,128)(2,1)S(1)}, u32[]{:S(2)}, u32[]{:S(2)}) collective-permute-start(bf16[16,512,128]{2,1,0:T(8,128)(2,1)S(1)} %get-tuple-element.391), channel_id=1, source_target_pairs={{0,8},{1,9},{2,10},{3,11},{4,12},{5,13},{6,14},{7,15},{8,0},{9,1},... | collective-permute-start | bytes 6291464 | tf_op jit(solution)/shard_map/ppermute | solution.py:734
  96.2 12.8 %collective-permute-start.17 = (bf16[4,208,128]{2,1,0:T(8,128)(2,1)S(1)}, bf16[4,208,128]{2,1,0:T(8,128)(2,1)S(1)}, u32[]{:S(2)}, u32[]{:S(2)}) collective-permute-start(bf16[4,208,128]{2,1,0:T(8,128)(2,1)S(1)} %get-tuple-element.382), channel_id=1, source_target_pairs={{0,16},{1,17},{2,18},{3,19},{4,20},{5,21},{6,22},{7,23},{8,9},{9,8... | collective-permute-start | bytes 638984 | tf_op jit(solution)/shard_map/ppermute | solution.py:744
  106.6 4.1 %copy-start.19 = (bf16[1280,1024]{1,0:T(8,128)(2,1)S(1)}, bf16[1280,1024]{1,0:T(8,128)(2,1)}, u32[]{:S(2)}) copy-start(bf16[1280,1024]{1,0:T(8,128)(2,1)} %copy-done.18) | copy-start | bytes 7864324
  107.1 16.0 %collective-permute-start.19 = (bf16[8,512,128]{2,1,0:T(8,128)(2,1)S(1)}, bf16[8,512,128]{2,1,0:T(8,128)(2,1)S(1)}, u32[]{:S(2)}, u32[]{:S(2)}) collective-permute-start(bf16[8,512,128]{2,1,0:T(8,128)(2,1)S(1)} %get-tuple-element.396), channel_id=1, source_target_pairs={{0,16},{1,17},{2,18},{3,19},{4,20},{5,21},{6,22},{7,23},{8,9},{9,8... | collective-permute-start | bytes 3145736 | tf_op jit(solution)/shard_map/ppermute | solution.py:744
  109.1 9.5 %collective-permute-start.20 = (bf16[2,208,128]{2,1,0:T(8,128)(2,1)S(1)}, bf16[2,208,128]{2,1,0:T(8,128)(2,1)S(1)}, u32[]{:S(2)}, u32[]{:S(2)}) collective-permute-start(bf16[2,208,128]{2,1,0:T(8,128)(2,1)S(1)} %get-tuple-element.400), channel_id=1, source_target_pairs={{0,1},{1,0},{2,3},{3,2},{4,5},{5,4},{6,7},{7,6},{8,24},{9,25},{10,... | collective-permute-start | bytes 319496 | tf_op jit(solution)/shard_map/ppermute | solution.py:744
  114.4 3.9 %collective-permute-start.21 = (bf16[16,208,128]{2,1,0:T(8,128)(2,1)S(1)}, bf16[16,208,128]{2,1,0:T(8,128)(2,1)S(1)}, u32[]{:S(2)}, u32[]{:S(2)}) collective-permute-start(bf16[16,208,128]{2,1,0:T(8,128)(2,1)S(1)} %get-tuple-element.411), channel_id=1, source_target_pairs={{0,8},{1,9},{2,10},{3,11},{4,12},{5,13},{6,14},{7,15},{8,0},{9,1},... | collective-permute-start | bytes 2555912 | tf_op jit(solution)/shard_map/ppermute | solution.py:734
  118.5 6.6 %copy-start.21 = (f32[1024,128]{1,0:T(8,128)S(1)}, f32[1024,128]{1,0:T(8,128)}, u32[]{:S(2)}) copy-start(f32[1024,128]{1,0:T(8,128)} %copy-done.20) | copy-start | bytes 1572868
  118.5 13.9 %collective-permute-start.24 = (bf16[8,208,128]{2,1,0:T(8,128)(2,1)S(1)}, bf16[8,208,128]{2,1,0:T(8,128)(2,1)S(1)}, u32[]{:S(2)}, u32[]{:S(2)}) collective-permute-start(bf16[8,208,128]{2,1,0:T(8,128)(2,1)S(1)} %get-tuple-element.415), channel_id=1, source_target_pairs={{0,2},{1,3},{2,0},{3,1},{4,6},{5,7},{6,4},{7,5},{8,12},{9,13},{10,... | collective-permute-start | bytes 1277960 | tf_op jit(solution)/shard_map/ppermute | solution.py:744
  119.3 27.3 %collective-permute-start.22 = (bf16[1,208,128]{2,1,0:T(8,128)(2,1)}, bf16[1,208,128]{2,1,0:T(8,128)(2,1)}, u32[]{:S(2)}, u32[]{:S(2)}) collective-permute-start(bf16[1,208,128]{2,1,0:T(8,128)(2,1)} %get-tuple-element.419), channel_id=1, source_target_pairs={{0,4},{1,5},{2,6},{3,7},{4,0},{5,1},{6,2},{7,3},{8,10},{9,11},{10,... | collective-permute-start | bytes 159752 | tf_op jit(solution)/shard_map/ppermute | solution.py:744
  123.4 9.7 %collective-permute-start.23 = (bf16[4,512,128]{2,1,0:T(8,128)(2,1)S(1)}, bf16[4,512,128]{2,1,0:T(8,128)(2,1)S(1)}, u32[]{:S(2)}, u32[]{:S(2)}) collective-permute-start(bf16[4,512,128]{2,1,0:T(8,128)(2,1)S(1)} %get-tuple-element.423), channel_id=1, source_target_pairs={{0,1},{1,0},{2,3},{3,2},{4,5},{5,4},{6,7},{7,6},{8,24},{9,25},{10,... | collective-permute-start | bytes 1572872 | tf_op jit(solution)/shard_map/ppermute | solution.py:744
  132.6 6.0 %collective-permute-start.25 = (bf16[4,208,128]{2,1,0:T(8,128)(2,1)S(1)}, bf16[4,208,128]{2,1,0:T(8,128)(2,1)S(1)}, u32[]{:S(2)}, u32[]{:S(2)}) collective-permute-start(bf16[4,208,128]{2,1,0:T(8,128)(2,1)S(1)} %get-tuple-element.435), channel_id=1, source_target_pairs={{0,16},{1,17},{2,18},{3,19},{4,20},{5,21},{6,22},{7,23},{8,9},{9,8... | collective-permute-start | bytes 638984 | tf_op jit(solution)/shard_map/ppermute | solution.py:744
  133.9 9.4 %collective-permute-start.27 = (bf16[2,512,128]{2,1,0:T(8,128)(2,1)}, bf16[2,512,128]{2,1,0:T(8,128)(2,1)S(1)}, u32[]{:S(2)}, u32[]{:S(2)}) collective-permute-start(bf16[2,512,128]{2,1,0:T(8,128)(2,1)} %get-tuple-element.439), channel_id=1, source_target_pairs={{0,2},{1,3},{2,0},{3,1},{4,6},{5,7},{6,4},{7,5},{8,12},{9,13},{10,... | collective-permute-start | bytes 786440 | tf_op jit(solution)/shard_map/ppermute | solution.py:744
  133.9 14.9 %copy-start.22 = (bf16[1,208,128]{2,1,0:T(8,128)(2,1)S(1)}, bf16[1,208,128]{2,1,0:T(8,128)(2,1)}, u32[]{:S(2)}) copy-start(bf16[1,208,128]{2,1,0:T(8,128)(2,1)} %get-tuple-element.440) | copy-start | bytes 159748
  138.7 4.8 %collective-permute-start.26 = (bf16[2,208,128]{2,1,0:T(8,128)(2,1)S(1)}, bf16[2,208,128]{2,1,0:T(8,128)(2,1)S(1)}, u32[]{:S(2)}, u32[]{:S(2)}) collective-permute-start(bf16[2,208,128]{2,1,0:T(8,128)(2,1)S(1)} %get-tuple-element.454), channel_id=1, source_target_pairs={{0,1},{1,0},{2,3},{3,2},{4,5},{5,4},{6,7},{7,6},{8,24},{9,25},{10,... | collective-permute-start | bytes 319496 | tf_op jit(solution)/shard_map/ppermute | solution.py:744
  143.5 5.4 %collective-permute-start.28 = (bf16[1,208,128]{2,1,0:T(8,128)(2,1)S(1)}, bf16[1,208,128]{2,1,0:T(8,128)(2,1)S(1)}, u32[]{:S(2)}, u32[]{:S(2)}) collective-permute-start(bf16[1,208,128]{2,1,0:T(8,128)(2,1)S(1)} %get-tuple-element.469), channel_id=1, source_target_pairs={{0,4},{1,5},{2,6},{3,7},{4,0},{5,1},{6,2},{7,3},{8,10},{9,11},{10,... | collective-permute-start | bytes 159752 | tf_op jit(solution)/shard_map/ppermute | solution.py:744
  146.7 6.7 %collective-permute-start.29 = (bf16[1,512,128]{2,1,0:T(8,128)(2,1)S(1)}, bf16[1,512,128]{2,1,0:T(8,128)(2,1)S(1)}, u32[]{:S(2)}, u32[]{:S(2)}) collective-permute-start(bf16[1,512,128]{2,1,0:T(8,128)(2,1)S(1)} %get-tuple-element.465), channel_id=1, source_target_pairs={{0,4},{1,5},{2,6},{3,7},{4,0},{5,1},{6,2},{7,3},{8,10},{9,11},{10,... | collective-permute-start | bytes 393224 | tf_op jit(solution)/shard_map/ppermute | solution.py:744
  153.4 18.2 %copy-start.1 = (f32[7680]{0:T(1024)S(1)}, f32[7680]{0:T(1024)}, u32[]{:S(2)}) copy-start(f32[7680]{0:T(1024)} %param.27) | copy-start | bytes 92164
  153.4 18.2 %copy-start.6 = (f32[5,80,160]{2,1,0:T(8,128)S(1)}, f32[5,80,160]{2,1,0:T(8,128)}, u32[]{:S(2)}) copy-start(f32[5,80,160]{2,1,0:T(8,128)} %param.21) | copy-start | bytes 768004
  153.4 18.2 %copy-start.7 = (f32[5,80,160]{2,1,0:T(8,128)S(1)}, f32[5,80,160]{2,1,0:T(8,128)}, u32[]{:S(2)}) copy-start(f32[5,80,160]{2,1,0:T(8,128)} %param.22) | copy-start | bytes 768004
  153.4 18.2 %copy-start.8 = (f32[5,80,160]{2,1,0:T(8,128)S(1)}, f32[5,80,160]{2,1,0:T(8,128)}, u32[]{:S(2)}) copy-start(f32[5,80,160]{2,1,0:T(8,128)} %param.23) | copy-start | bytes 768004
  153.4 18.2 %copy-start.10 = (f32[160,160]{1,0:T(8,128)S(1)}, f32[160,160]{1,0:T(8,128)}, u32[]{:S(2)}) copy-start(f32[160,160]{1,0:T(8,128)} %refs_4_.1) | copy-start | bytes 307204
  153.5 18.2 %copy-start.11 = (f32[160,160]{1,0:T(8,128)S(1)}, f32[160,160]{1,0:T(8,128)}, u32[]{:S(2)}) copy-start(f32[160,160]{1,0:T(8,128)} %refs_5_.1) | copy-start | bytes 307204
  153.5 18.1 %copy-start.12 = (f32[160,160]{1,0:T(8,128)S(1)}, f32[160,160]{1,0:T(8,128)}, u32[]{:S(2)}) copy-start(f32[160,160]{1,0:T(8,128)} %refs_6_.1) | copy-start | bytes 307204
  153.5 18.1 %copy-start.14 = (f32[80,320]{1,0:T(8,128)S(1)}, f32[80,320]{1,0:T(8,128)}, u32[]{:S(2)}) copy-start(f32[80,320]{1,0:T(8,128)} %refs_11_.1) | copy-start | bytes 307204
  153.5 18.1 %copy-start.15 = (f32[80,320]{1,0:T(8,128)S(1)}, f32[80,320]{1,0:T(8,128)}, u32[]{:S(2)}) copy-start(f32[80,320]{1,0:T(8,128)} %refs_12_.1) | copy-start | bytes 307204
  153.5 18.1 %copy-start.16 = (f32[7680]{0:T(1024)S(1)}, f32[7680]{0:T(1024)}, u32[]{:S(2)}) copy-start(f32[7680]{0:T(1024)} %param.28) | copy-start | bytes 92164
  153.5 18.1 %copy-start.17 = (f32[7680]{0:T(1024)S(1)}, f32[7680]{0:T(1024)}, u32[]{:S(2)}) copy-start(f32[7680]{0:T(1024)} %param.29) | copy-start | bytes 92164
  153.6 1.3 collective-permute-start.30
  154.9 4.8 %collective-permute-start.31 = (f32[64,128]{1,0:T(8,128)S(1)}, f32[64,128]{1,0:T(8,128)S(1)}, u32[]{:S(2)}, u32[]{:S(2)}) collective-permute-start(f32[64,128]{1,0:T(8,128)S(1)} %add.143), channel_id=1, source_target_pairs={{0,4},{1,5},{2,6},{3,7},{4,0},{5,1},{6,2},{7,3},{8,10},{9,11},{10,... | collective-permute-start | bytes 98312 | tf_op jit(solution)/shard_map/ppermute | solution.py:758
  159.7 3.9 %collective-permute-start.32 = (f32[64,128]{1,0:T(8,128)S(1)}, f32[64,128]{1,0:T(8,128)S(1)}, u32[]{:S(2)}, u32[]{:S(2)}) collective-permute-start(f32[64,128]{1,0:T(8,128)S(1)} %add.144), channel_id=1, source_target_pairs={{0,2},{1,3},{2,0},{3,1},{4,6},{5,7},{6,4},{7,5},{8,12},{9,13},{10,... | collective-permute-start | bytes 98312 | tf_op jit(solution)/shard_map/ppermute | solution.py:758
  163.6 4.0 %collective-permute-start.33 = (f32[64,128]{1,0:T(8,128)S(1)}, f32[64,128]{1,0:T(8,128)S(1)}, u32[]{:S(2)}, u32[]{:S(2)}) collective-permute-start(f32[64,128]{1,0:T(8,128)S(1)} %add.145), channel_id=1, source_target_pairs={{0,1},{1,0},{2,3},{3,2},{4,5},{5,4},{6,7},{7,6},{8,24},{9,25},{10,... | collective-permute-start | bytes 98312 | tf_op jit(solution)/shard_map/ppermute | solution.py:758
  167.6 3.9 %collective-permute-start.34 = (f32[64,128]{1,0:T(8,128)S(1)}, f32[64,128]{1,0:T(8,128)S(1)}, u32[]{:S(2)}, u32[]{:S(2)}) collective-permute-start(f32[64,128]{1,0:T(8,128)S(1)} %add.146), channel_id=1, source_target_pairs={{0,16},{1,17},{2,18},{3,19},{4,20},{5,21},{6,22},{7,23},{8,9},{9,8... | collective-permute-start | bytes 98312 | tf_op jit(solution)/shard_map/ppermute | solution.py:758
